TPU v7x, 512 devices: a whole 4x8x8 slice. The times are simulated.
512 devices in a mesh: section: 16 (over x, y_hi, core), tp: 32 (over y_lo, z).
Axes of the slice: x: 4, y: 8 (y_hi: 2, y_lo: 4; y = y_hi * 4 + y_lo), z: 8, core: 2. Of those that a mesh axis runs over, the one named last changes fastest.
Arguments:
- inputs: bfloat16 [2, 2, 64, 4096], P(None, None, None, 'tp'), may hold values from -6 to 6
- weights: bfloat16 [8, 4096, 4096], P(None, 'section', 'tp'), may hold values from -0.09375 to 0.09375
- targets: bfloat16 [2, 2, 64, 4096], P(None, None, None, 'tp'), may hold values from -6 to 6
Outputs:
- grads: bfloat16 [8, 4096, 4096], P(None, 'section', 'tp')
All inputs are finite; a program needn't handle non-finite values.
Results may differ from a plain program's by a relative error of at most 0.015.
Values may be sent and summed in bfloat16 or wider, within the bound.
No kernel may reach another device: no remote copies, remote signals or barrier semaphores. Data moves between devices by JAX's collectives and lax.ppermute only.
A program may use at most 64 MiB of HBM per device.

v0:
```python
import jax
import jax.numpy as jnp
from jax import lax
from jax.sharding import PartitionSpec as P

EPSILON = 1e-05


def passed_along(shard, axis, by):
    devices = lax.axis_size(axis)
    pairs = [(i, i + by) for i in range(devices) if 0 <= i + by < devices]
    return lax.ppermute(shard, axis, pairs)


def silu_slope(activation):
    sigmoid = jax.nn.sigmoid(activation)
    return sigmoid * (1.0 + activation * (1.0 - sigmoid))


def forward_product(direction, segment, first_matrix, second_matrix):

    def forward_with_first():
        return jnp.dot(segment, first_matrix, preferred_element_type=jnp.float32)

    def forward_with_second():
        return jnp.dot(segment, second_matrix, preferred_element_type=jnp.float32)

    return lax.cond(direction == 0, forward_with_first, forward_with_second)


def backward_product(direction, segment, first_rows, second_rows):
    numbers = (((1,), (1,)), ((), ()))

    def backward_with_first():
        return lax.dot_general(segment, first_rows, numbers, preferred_element_type=jnp.float32)

    def backward_with_second():
        return lax.dot_general(segment, second_rows, numbers, preferred_element_type=jnp.float32)

    return lax.cond(direction == 0, backward_with_first, backward_with_second)


def on_device(inputs, weights, targets):
    sections = lax.axis_size("section")
    position = lax.axis_index("section")
    groups = sections // 2
    group = position // 2
    member = position % 2
    tp_index = lax.axis_index("tp")
    columns = weights.shape[2]
    features = columns * lax.axis_size("tp")
    tokens = inputs.shape[2]
    own_send = jnp.repeat(weights, 2, axis=0)
    other_send = jnp.repeat(weights[::-1], 2, axis=0)
    own_fetched, other_fetched = (
        lax.all_to_all(own_send, "section", split_axis=0, concat_axis=1, tiled=True),
        lax.all_to_all(other_send, "section", split_axis=0, concat_axis=1, tiled=True),
    )
    own_matrix = own_fetched[0]
    other_matrix = other_fetched[0]
    own_rows, other_rows = (
        lax.all_to_all(own_matrix, "tp", split_axis=0, concat_axis=1, tiled=True),
        lax.all_to_all(other_matrix, "tp", split_axis=0, concat_axis=1, tiled=True),
    )

    def forward_plan(moment):
        lower_on = moment == group
        upper_on = moment == groups - 1 - group
        return (lower_on | upper_on, jnp.where(lower_on, 0, 1), lower_on)

    def backward_plan(moment):
        first_on = moment == groups - 1 - group
        second_on = moment == group
        return (first_on | second_on, jnp.where(first_on, 0, 1), second_on)

    def forward_fetch(outgoing):
        lower_side = passed_along(outgoing, "section", 2)
        upper_side = passed_along(outgoing, "section", -2)
        return (lower_side, upper_side)

    def backward_fetch(outgoing):
        lower_side = passed_along(outgoing, "section", 2)
        upper_side = passed_along(outgoing, "section", -2)
        return (lower_side, upper_side)

    slots = 3

    def forward_tick(moment, running):
        outgoing, stored_inputs, stored_products, stored_scales = running
        lower_side, upper_side = forward_fetch(outgoing)
        active, direction, from_lower = forward_plan(moment)
        at_boundary = jnp.where(from_lower, group == 0, group == groups - 1)
        arrival = jnp.where(
            at_boundary, inputs[direction, member], jnp.where(from_lower, lower_side, upper_side)
        )
        segment = lax.all_gather(arrival, "tp", axis=1, tiled=True)
        product_sum = forward_product(direction, segment, own_matrix, other_matrix)
        squares = jnp.sum(jnp.square(segment.astype(jnp.float32)), axis=1)
        gathered = segment
        product, squares, gathered = (product_sum, squares, gathered)
        inverse_rms = lax.rsqrt(squares / features + EPSILON)
        activation = inverse_rms[:, None] * product
        result = (arrival.astype(jnp.float32) + jax.nn.silu(activation)).astype(jnp.bfloat16)
        storage_slot = jnp.where(active, direction, 2)
        stored_inputs = lax.dynamic_update_index_in_dim(stored_inputs, gathered, storage_slot, 0)
        stored_products = lax.dynamic_update_index_in_dim(stored_products, product, storage_slot, 0)
        stored_scales = lax.dynamic_update_index_in_dim(stored_scales, inverse_rms, storage_slot, 0)
        return (result, stored_inputs, stored_products, stored_scales)

    forward_start = (
        jnp.zeros((tokens, columns), jnp.bfloat16),
        jnp.zeros((slots, tokens, features), jnp.bfloat16),
        jnp.zeros((slots, tokens, columns), jnp.float32),
        jnp.zeros((slots, tokens), jnp.float32),
    )
    forward_final = lax.fori_loop(0, groups, forward_tick, forward_start)
    stored_inputs, stored_products, stored_scales = (
        forward_final[1],
        forward_final[2],
        forward_final[3],
    )

    def backward_tick(moment, running):
        outgoing, stored_slopes = running
        lower_side, upper_side = backward_fetch(outgoing)
        active, direction, from_lower = backward_plan(moment)
        storage_slot = jnp.where(active, direction, 2)
        gathered = lax.dynamic_index_in_dim(stored_inputs, storage_slot, 0, False)
        product = lax.dynamic_index_in_dim(stored_products, storage_slot, 0, False)
        inverse_rms = lax.dynamic_index_in_dim(stored_scales, storage_slot, 0, False)
        activation = inverse_rms[:, None] * product
        own_columns = lax.dynamic_slice_in_dim(gathered, tp_index * columns, columns, 1)
        at_boundary = jnp.where(from_lower, group == 0, group == groups - 1)
        finished = (own_columns.astype(jnp.float32) + jax.nn.silu(activation)).astype(jnp.bfloat16)
        target = targets[direction, member]
        first_grad = (finished.astype(jnp.float32) - target.astype(jnp.float32)) / tokens
        incoming = jnp.where(from_lower, lower_side, upper_side).astype(jnp.float32)
        cotangent = jnp.where(at_boundary, first_grad, incoming)
        scaled_grad = (inverse_rms[:, None] * cotangent * silu_slope(activation)).astype(
            jnp.bfloat16
        )
        partial_value = jnp.sum(scaled_grad.astype(jnp.float32) * product, axis=1)
        returned = backward_product(
            direction, lax.all_gather(scaled_grad, "tp", axis=1, tiled=True), own_rows, other_rows
        )
        row_total = lax.psum(partial_value, "tp")
        result = (
            cotangent
            + returned
            - (inverse_rms * inverse_rms / features * row_total)[:, None]
            * own_columns.astype(jnp.float32)
        )
        stored_slopes = lax.dynamic_update_index_in_dim(stored_slopes, scaled_grad, storage_slot, 0)
        return (result.astype(jnp.bfloat16), stored_slopes)

    backward_start = (
        jnp.zeros((tokens, columns), jnp.bfloat16),
        jnp.zeros((slots, tokens, columns), jnp.bfloat16),
    )
    backward_final = lax.fori_loop(0, groups, backward_tick, backward_start)
    stored_slopes = backward_final[1]

    def set_total(which):
        total = lax.dot_general(
            stored_inputs[which],
            stored_slopes[which],
            (((0,), (0,)), ((), ())),
            preferred_element_type=jnp.float32,
        )
        return total.astype(jnp.bfloat16).reshape(sections, features // sections, columns)

    first_part = set_total(0)
    second_part = set_total(1)
    row_count = features // sections
    got_first, got_second = (
        lax.all_to_all(first_part, "section", split_axis=0, concat_axis=0, tiled=True),
        lax.all_to_all(second_part, "section", split_axis=0, concat_axis=0, tiled=True),
    )
    first_sum = jnp.sum(
        got_first.astype(jnp.float32).reshape(groups, 2, row_count, columns), axis=1
    )
    second_sum = jnp.sum(
        got_second.astype(jnp.float32).reshape(groups, 2, row_count, columns), axis=1
    )[::-1]
    return (first_sum + second_sum).astype(jnp.bfloat16)


def solution(mesh):
    placed = (P(None, None, None, "tp"), P(None, "section", "tp"), P(None, None, None, "tp"))
    return jax.shard_map(
        on_device, mesh=mesh, in_specs=placed, out_specs=P(None, "section", "tp"), check_vma=False
    )
```

profile of v0, /device:TPU:1, one launch (start us, length us, event | category | flops | bytes accessed | tf_op | source)
XLA Modules:
  0.0 2316.4 jit_solution(1577689993734183672)
XLA Ops:
  1.3 35.9 %all_to_all.66 = bf16[16,256,128]{2,1,0:T(8,128)(2,1)S(1)} all-to-all(bf16[16,256,128]{2,1,0:T(8,128)(2,1)S(1)} %bitcast.104), channel_id=1, replica_groups=mesh['section'=16,'tp'=32] {'section'}, dimensions={0} | all-to-all | bytes 2097152 | tf_op jit(solution)/shard_map/all_to_all | solution.py:57
  37.4 25.2 %all_to_all.67 = bf16[16,256,128]{2,1,0:T(8,128)(2,1)} all-to-all(bf16[16,256,128]{2,1,0:T(8,128)(2,1)S(1)} %bitcast.107), channel_id=1, replica_groups=mesh['section'=16,'tp'=32] {'section'}, dimensions={0} | all-to-all | bytes 2097152 | tf_op jit(solution)/shard_map/all_to_all | solution.py:56
  62.6 49.2 %all_to_all.68 = bf16[32,128,128]{2,1,0:T(8,128)(2,1)S(1)} all-to-all(bf16[32,128,128]{2,1,0:T(8,128)(2,1)S(1)} %bitcast.100), channel_id=1, replica_groups=mesh['section'=16,'tp'=32] {'tp'}, dimensions={0} | all-to-all | bytes 2097152 | tf_op jit(solution)/shard_map/all_to_all | solution.py:63
  111.8 8.1 all-to-all-start.3
  122.7 23.0 all-to-all-done.3
  149.8 647.7 %while.41 = (s32[]{:T(128)}, bf16[64,128]{1,0:T(8,128)(2,1)S(1)}, bf16[3,64,4096]{2,1,0:T(8,128)(2,1)}, f32[3,64,128]{2,1,0:T(8,128)S(1)}, f32[3,64]{1,0:T(4,128...) while((s32[]{:T(128)}, bf16[64,128]{1,0:T(8,128)(2,1)S(1)}, ...), condition=%wide.region_4.5_spmd.clone, body=%wide.region_0.4_spmd.clone.sunk | while | flops 67985480 | bytes 4147326 | solution.py:116
  152.5 7.1 collective-permute-done.1
  160.3 67.3 %all_gather.24 = bf16[64,4096]{1,0:T(8,128)(2,1)S(1)} all-gather(bf16[64,128]{1,0:T(8,128)(2,1)S(1)} %bitcast_select_fusion.2), channel_id=1, replica_groups=mesh['section'=16,'tp'=32] {'tp'}, dimensions={1}, use_global_device_ids=true | all-gather | bytes 540672 | tf_op jit(solution)/shard_map/while/body/eval_jaxpr/all_gather | solution.py:96
  232.5 6.8 collective-permute-start
  240.6 7.1 collective-permute-done.1
  248.4 61.8 %all_gather.24 = bf16[64,4096]{1,0:T(8,128)(2,1)S(1)} all-gather(bf16[64,128]{1,0:T(8,128)(2,1)S(1)} %bitcast_select_fusion.2), channel_id=1, replica_groups=mesh['section'=16,'tp'=32] {'tp'}, dimensions={1}, use_global_device_ids=true | all-gather | bytes 540672 | tf_op jit(solution)/shard_map/while/body/eval_jaxpr/all_gather | solution.py:96
  313.9 4.7 collective-permute-start
  319.9 7.1 collective-permute-done.1
  327.7 62.4 %all_gather.24 = bf16[64,4096]{1,0:T(8,128)(2,1)S(1)} all-gather(bf16[64,128]{1,0:T(8,128)(2,1)S(1)} %bitcast_select_fusion.2), channel_id=1, replica_groups=mesh['section'=16,'tp'=32] {'tp'}, dimensions={1}, use_global_device_ids=true | all-gather | bytes 540672 | tf_op jit(solution)/shard_map/while/body/eval_jaxpr/all_gather | solution.py:96
  393.9 7.2 collective-permute-start
  402.4 7.1 collective-permute-done.1
  410.2 63.9 %all_gather.24 = bf16[64,4096]{1,0:T(8,128)(2,1)S(1)} all-gather(bf16[64,128]{1,0:T(8,128)(2,1)S(1)} %bitcast_select_fusion.2), channel_id=1, replica_groups=mesh['section'=16,'tp'=32] {'tp'}, dimensions={1}, use_global_device_ids=true | all-gather | bytes 540672 | tf_op jit(solution)/shard_map/while/body/eval_jaxpr/all_gather | solution.py:96
  477.7 3.6 collective-permute-start
  482.7 7.1 collective-permute-done.1
  490.4 62.0 %all_gather.24 = bf16[64,4096]{1,0:T(8,128)(2,1)S(1)} all-gather(bf16[64,128]{1,0:T(8,128)(2,1)S(1)} %bitcast_select_fusion.2), channel_id=1, replica_groups=mesh['section'=16,'tp'=32] {'tp'}, dimensions={1}, use_global_device_ids=true | all-gather | bytes 540672 | tf_op jit(solution)/shard_map/while/body/eval_jaxpr/all_gather | solution.py:96
  556.1 7.3 collective-permute-start
  564.8 7.1 collective-permute-done.1
  572.5 62.6 %all_gather.24 = bf16[64,4096]{1,0:T(8,128)(2,1)S(1)} all-gather(bf16[64,128]{1,0:T(8,128)(2,1)S(1)} %bitcast_select_fusion.2), channel_id=1, replica_groups=mesh['section'=16,'tp'=32] {'tp'}, dimensions={1}, use_global_device_ids=true | all-gather | bytes 540672 | tf_op jit(solution)/shard_map/while/body/eval_jaxpr/all_gather | solution.py:96
  638.8 4.8 collective-permute-start
  645.0 7.1 collective-permute-done.1
  652.7 62.8 %all_gather.24 = bf16[64,4096]{1,0:T(8,128)(2,1)S(1)} all-gather(bf16[64,128]{1,0:T(8,128)(2,1)S(1)} %bitcast_select_fusion.2), channel_id=1, replica_groups=mesh['section'=16,'tp'=32] {'tp'}, dimensions={1}, use_global_device_ids=true | all-gather | bytes 540672 | tf_op jit(solution)/shard_map/while/body/eval_jaxpr/all_gather | solution.py:96
  719.2 3.1 collective-permute-start
  723.7 7.1 collective-permute-done.1
  731.5 62.5 %all_gather.24 = bf16[64,4096]{1,0:T(8,128)(2,1)S(1)} all-gather(bf16[64,128]{1,0:T(8,128)(2,1)S(1)} %bitcast_select_fusion.2), channel_id=1, replica_groups=mesh['section'=16,'tp'=32] {'tp'}, dimensions={1}, use_global_device_ids=true | all-gather | bytes 540672 | tf_op jit(solution)/shard_map/while/body/eval_jaxpr/all_gather | solution.py:96
  797.6 1108.8 %while.42 = (s32[]{:T(128)}, bf16[64,128]{1,0:T(8,128)(2,1)S(1)}, bf16[3,64,128]{2,1,0:T(8,128)(2,1)S(1)}, s32[]{:T(128)}, pred[]{:T(512)}, /*index=5*/pred[]{:T...) while((s32[]{:T(128)}, bf16[64,128]{1,0:T(8,128)(2,1)S(1)}, ...), condition=%wide.region_10.11_spmd.clone, body=%wide.region_5.10_spmd.clone.sunk | while | flops 67477704 | bytes 2641328 | solution.py:160
  797.6 4.4 collective-permute-start.2
  803.4 7.0 collective-permute-done.3
  811.3 63.6 %all_gather.25 = bf16[64,4096]{1,0:T(8,128)(2,1)S(1)} all-gather(bf16[64,128]{1,0:T(8,128)(2,1)S(1)} %get-tuple-element.1022), channel_id=1, replica_groups=mesh['section'=16,'tp'=32] {'tp'}, dimensions={1}, use_global_device_ids=true | all-gather | bytes 540672 | tf_op jit(solution)/shard_map/while/body/eval_jaxpr/all_gather | solution.py:144
  875.0 60.6 %psum.17 = f32[64]{0:T(128)S(1)} all-reduce(f32[64]{0:T(128)S(1)} %fusion.34), channel_id=1, replica_groups=mesh['section'=16,'tp'=32] {'tp'}, use_global_device_ids=true, to_apply=%region_9.9 | all-reduce | flops 64 | bytes 512 | tf_op jit(solution)/shard_map/while/body/eval_jaxpr/psum | solution.py:146
  937.0 3.2 collective-permute-start.2
  941.6 7.0 collective-permute-done.3
  949.5 63.1 %all_gather.25 = bf16[64,4096]{1,0:T(8,128)(2,1)S(1)} all-gather(bf16[64,128]{1,0:T(8,128)(2,1)S(1)} %get-tuple-element.1022), channel_id=1, replica_groups=mesh['section'=16,'tp'=32] {'tp'}, dimensions={1}, use_global_device_ids=true | all-gather | bytes 540672 | tf_op jit(solution)/shard_map/while/body/eval_jaxpr/all_gather | solution.py:144
  1012.6 60.5 %psum.17 = f32[64]{0:T(128)S(1)} all-reduce(f32[64]{0:T(128)S(1)} %fusion.34), channel_id=1, replica_groups=mesh['section'=16,'tp'=32] {'tp'}, use_global_device_ids=true, to_apply=%region_9.9 | all-reduce | flops 64 | bytes 512 | tf_op jit(solution)/shard_map/while/body/eval_jaxpr/psum | solution.py:146
  1074.5 4.7 collective-permute-start.2
  1080.6 7.0 collective-permute-done.3
  1088.5 62.2 %all_gather.25 = bf16[64,4096]{1,0:T(8,128)(2,1)S(1)} all-gather(bf16[64,128]{1,0:T(8,128)(2,1)S(1)} %get-tuple-element.1022), channel_id=1, replica_groups=mesh['section'=16,'tp'=32] {'tp'}, dimensions={1}, use_global_device_ids=true | all-gather | bytes 540672 | tf_op jit(solution)/shard_map/while/body/eval_jaxpr/all_gather | solution.py:144
  1150.8 62.3 %psum.17 = f32[64]{0:T(128)S(1)} all-reduce(f32[64]{0:T(128)S(1)} %fusion.34), channel_id=1, replica_groups=mesh['section'=16,'tp'=32] {'tp'}, use_global_device_ids=true, to_apply=%region_9.9 | all-reduce | flops 64 | bytes 512 | tf_op jit(solution)/shard_map/while/body/eval_jaxpr/psum | solution.py:146
  1214.6 3.1 collective-permute-start.2
  1219.0 7.0 collective-permute-done.3
  1226.9 61.9 %all_gather.25 = bf16[64,4096]{1,0:T(8,128)(2,1)S(1)} all-gather(bf16[64,128]{1,0:T(8,128)(2,1)S(1)} %get-tuple-element.1022), channel_id=1, replica_groups=mesh['section'=16,'tp'=32] {'tp'}, dimensions={1}, use_global_device_ids=true | all-gather | bytes 540672 | tf_op jit(solution)/shard_map/while/body/eval_jaxpr/all_gather | solution.py:144
  1289.0 62.7 %psum.17 = f32[64]{0:T(128)S(1)} all-reduce(f32[64]{0:T(128)S(1)} %fusion.34), channel_id=1, replica_groups=mesh['section'=16,'tp'=32] {'tp'}, use_global_device_ids=true, to_apply=%region_9.9 | all-reduce | flops 64 | bytes 512 | tf_op jit(solution)/shard_map/while/body/eval_jaxpr/psum | solution.py:146
  1357.0 7.2 collective-permute-done.3
  1365.1 61.8 %all_gather.25 = bf16[64,4096]{1,0:T(8,128)(2,1)S(1)} all-gather(bf16[64,128]{1,0:T(8,128)(2,1)S(1)} %get-tuple-element.1022), channel_id=1, replica_groups=mesh['section'=16,'tp'=32] {'tp'}, dimensions={1}, use_global_device_ids=true | all-gather | bytes 540672 | tf_op jit(solution)/shard_map/while/body/eval_jaxpr/all_gather | solution.py:144
  1427.0 62.1 %psum.17 = f32[64]{0:T(128)S(1)} all-reduce(f32[64]{0:T(128)S(1)} %fusion.34), channel_id=1, replica_groups=mesh['section'=16,'tp'=32] {'tp'}, use_global_device_ids=true, to_apply=%region_9.9 | all-reduce | flops 64 | bytes 512 | tf_op jit(solution)/shard_map/while/body/eval_jaxpr/psum | solution.py:146
  1494.9 7.0 collective-permute-done.3
  1502.8 62.0 %all_gather.25 = bf16[64,4096]{1,0:T(8,128)(2,1)S(1)} all-gather(bf16[64,128]{1,0:T(8,128)(2,1)S(1)} %get-tuple-element.1022), channel_id=1, replica_groups=mesh['section'=16,'tp'=32] {'tp'}, dimensions={1}, use_global_device_ids=true | all-gather | bytes 540672 | tf_op jit(solution)/shard_map/while/body/eval_jaxpr/all_gather | solution.py:144
  1564.8 62.3 %psum.17 = f32[64]{0:T(128)S(1)} all-reduce(f32[64]{0:T(128)S(1)} %fusion.34), channel_id=1, replica_groups=mesh['section'=16,'tp'=32] {'tp'}, use_global_device_ids=true, to_apply=%region_9.9 | all-reduce | flops 64 | bytes 512 | tf_op jit(solution)/shard_map/while/body/eval_jaxpr/psum | solution.py:146
  1628.6 3.8 collective-permute-start.2
  1633.8 7.0 collective-permute-done.3
  1641.7 62.4 %all_gather.25 = bf16[64,4096]{1,0:T(8,128)(2,1)S(1)} all-gather(bf16[64,128]{1,0:T(8,128)(2,1)S(1)} %get-tuple-element.1022), channel_id=1, replica_groups=mesh['section'=16,'tp'=32] {'tp'}, dimensions={1}, use_global_device_ids=true | all-gather | bytes 540672 | tf_op jit(solution)/shard_map/while/body/eval_jaxpr/all_gather | solution.py:144
  1704.2 61.4 %psum.17 = f32[64]{0:T(128)S(1)} all-reduce(f32[64]{0:T(128)S(1)} %fusion.34), channel_id=1, replica_groups=mesh['section'=16,'tp'=32] {'tp'}, use_global_device_ids=true, to_apply=%region_9.9 | all-reduce | flops 64 | bytes 512 | tf_op jit(solution)/shard_map/while/body/eval_jaxpr/psum | solution.py:146
  1767.0 3.9 collective-permute-start.2
  1772.3 7.0 collective-permute-done.3
  1780.2 63.1 %all_gather.25 = bf16[64,4096]{1,0:T(8,128)(2,1)S(1)} all-gather(bf16[64,128]{1,0:T(8,128)(2,1)S(1)} %get-tuple-element.1022), channel_id=1, replica_groups=mesh['section'=16,'tp'=32] {'tp'}, dimensions={1}, use_global_device_ids=true | all-gather | bytes 540672 | tf_op jit(solution)/shard_map/while/body/eval_jaxpr/all_gather | solution.py:144
  1843.4 61.6 %psum.17 = f32[64]{0:T(128)S(1)} all-reduce(f32[64]{0:T(128)S(1)} %fusion.34), channel_id=1, replica_groups=mesh['section'=16,'tp'=32] {'tp'}, use_global_device_ids=true, to_apply=%region_9.9 | all-reduce | flops 64 | bytes 512 | tf_op jit(solution)/shard_map/while/body/eval_jaxpr/psum | solution.py:146
  1908.9 352.9 %all-to-all-start.5 = ((bf16[16,256,128]{2,1,0:T(8,128)(2,1)}), bf16[16,256,128]{2,1,0:T(8,128)(2,1)S(1)}, u32[]{:S(2)}, u32[]{:S(2)}) async-start(bf16[16,256,128]{2,1,0:T(8,128)(2,1)} %bitcast.18), calls=%async_computation.5 | async-start | bytes 2097152 | tf_op jit(solution)/shard_map/all_to_all | solution.py:177
  2264.3 24.6 %all-to-all-done.5 = bf16[16,256,128]{2,1,0:T(8,128)(2,1)S(1)} async-done(((bf16[16,256,128]{2,1,0:T(8,128)(2,1)}), bf16[16,256,128]{2,1,0:T(8,128)(2,1)S(1)}, u32[]{:S(2)}, u32[]{:S(2)}) %all-to-all-start.5) | async-done | bytes 1048608 | tf_op jit(solution)/shard_map/all_to_all | solution.py:177
  2288.8 6.9 all-to-all-start.4
  2295.9 19.4 all-to-all-done.4
  (209 shorter events, 116.2 us)
Async XLA Ops:
  1.1 36.1 %copy-start = (bf16[8,256,128]{2,1,0:T(8,128)(2,1)S(1)}, bf16[8,256,128]{2,1,0:T(8,128)(2,1)}, u32[]{:S(2)}) copy-start(bf16[8,256,128]{2,1,0:T(8,128)(2,1)} %param.12) | copy-start | bytes 1572868
  111.8 33.9 %all-to-all-start.3 = ((bf16[32,128,128]{2,1,0:T(8,128)(2,1)}), bf16[32,128,128]{2,1,0:T(8,128)(2,1)S(1)}, u32[]{:S(2)}, u32[]{:S(2)}) async-start(bf16[32,128,128]{2,1,0:T(8,128)(2,1)} %bitcast.10), calls=%async_computation.3 | async-start | bytes 2097152 | tf_op jit(solution)/shard_map/all_to_all | solution.py:62
  149.8 647.8 %copy-start.1 = (bf16[2,2,64,128]{3,2,1,0:T(8,128)(2,1)S(1)}, bf16[2,2,64,128]{3,2,1,0:T(8,128)(2,1)}, u32[]{:S(2)}) copy-start(bf16[2,2,64,128]{3,2,1,0:T(8,128)(2,1)} %param.13) | copy-start | bytes 196612
  149.9 2.6 collective-permute-start
  151.2 8.4 collective-permute-start.1
  232.5 8.1 collective-permute-start
  239.3 8.4 collective-permute-start.1
  313.9 6.0 collective-permute-start
  318.6 8.4 collective-permute-start.1
  393.9 8.5 collective-permute-start
  401.1 8.4 collective-permute-start.1
  477.7 4.9 collective-permute-start
  481.3 8.4 collective-permute-start.1
  556.1 8.6 collective-permute-start
  563.4 8.4 collective-permute-start.1
  638.8 6.2 collective-permute-start
  643.6 8.4 collective-permute-start.1
  719.2 4.4 collective-permute-start
  722.3 8.4 collective-permute-start.1
  797.6 5.8 collective-permute-start.2
  802.0 8.4 collective-permute-start.3
  937.0 4.5 collective-permute-start.2
  940.2 8.4 collective-permute-start.3
  1074.5 6.0 collective-permute-start.2
  1079.2 8.4 collective-permute-start.3
  1214.6 4.5 collective-permute-start.2
  1217.7 8.4 collective-permute-start.3
  1353.1 3.9 collective-permute-start.2
  1355.7 8.6 collective-permute-start.3
  1490.5 4.4 collective-permute-start.2
  1493.5 8.4 collective-permute-start.3
  1628.6 5.2 collective-permute-start.2
  1632.4 8.4 collective-permute-start.3
  1767.0 5.2 collective-permute-start.2
  1770.9 8.4 collective-permute-start.3
  1908.9 379.9 %all-to-all-start.5 = ((bf16[16,256,128]{2,1,0:T(8,128)(2,1)}), bf16[16,256,128]{2,1,0:T(8,128)(2,1)S(1)}, u32[]{:S(2)}, u32[]{:S(2)}) async-start(bf16[16,256,128]{2,1,0:T(8,128)(2,1)} %bitcast.18), calls=%async_computation.5 | async-start | bytes 2097152 | tf_op jit(solution)/shard_map/all_to_all | solution.py:177
  2288.8 26.5 %all-to-all-start.4 = ((bf16[16,256,128]{2,1,0:T(8,128)(2,1)}), bf16[16,256,128]{2,1,0:T(8,128)(2,1)S(1)}, u32[]{:S(2)}, u32[]{:S(2)}) async-start(bf16[16,256,128]{2,1,0:T(8,128)(2,1)} %bitcast.14), calls=%async_computation.4 | async-start | bytes 2097152 | tf_op jit(solution)/shard_map/all_to_all | solution.py:176
where the time goes:
time: 2320 us
  blocking collectives  1610 us (69%)
  starting transfers between devices  456 us (20%)
  waiting for transfers between devices  180 us (8%)
  other arithmetic  30.5 us (1%)
    all_gather x8, blocking collectives, forward_tick(): segment = lax.all_gather(arrival, 'tp', axis=1, tiled=True)  505 us
    all_gather x8, blocking collectives, backward_tick(): lax.all_gather(scaled_grad, 'tp', axis=1, tiled=True)  500 us
    psum x8, blocking collectives, backward_tick(): row_total = lax.psum(partial_value, 'tp')  493 us
    all_to_all x1, starting transfers between devices, on_device(): lax.all_to_all(second_part, 'section', split_axis=0, concat_axis=0, tiled...  353 us
    ppermute x32, waiting for transfers between devices, passed_along(): return lax.ppermute(shard, axis, pairs)  113 us
    ppermute x32, starting transfers between devices, passed_along(): return lax.ppermute(shard, axis, pairs)  88.1 us
    all_to_all x1, blocking collectives, on_device(): lax.all_to_all(other_matrix, 'tp', split_axis=0, concat_axis=1, tiled=True)  49.2 us
  transfers between devices with their start and end apart: 35, of which 19 were waited for; matrix products, arithmetic and copies ran while one was open for 0% of the time, Pallas kernels for 0%

commit v1 on v0

v1 whole, which is shorter than its diff:
```python
import jax
import jax.numpy as jnp
from jax import lax
from jax.sharding import PartitionSpec as P

EPSILON = 1e-05
F32 = jnp.float32
BF16 = jnp.bfloat16


def silu_slope(activation):
    sigmoid = jax.nn.sigmoid(activation)
    return sigmoid * (1.0 + activation * (1.0 - sigmoid))


def spread(block, copies):
    return lax.optimization_barrier(jnp.broadcast_to(block[None], (copies,) + block.shape))


def exchanged(blocks, axis):
    return lax.all_to_all(blocks, axis, split_axis=0, concat_axis=0, tiled=True)


def on_device(inputs, weights, targets):
    groups = lax.axis_size("section")
    members = lax.axis_size("tp")
    group = lax.axis_index("section")
    sections, row_count, columns = weights.shape
    features = columns * members
    micro_tokens = inputs.shape[2]
    all_tokens = inputs.shape[0] * inputs.shape[1] * micro_tokens
    tokens = all_tokens // groups
    own_x = lax.dynamic_slice_in_dim(inputs.reshape(all_tokens, columns), group * tokens, tokens, 0)
    own_target = lax.dynamic_slice_in_dim(
        targets.reshape(all_tokens, columns), group * tokens, tokens, 0
    )
    matrices = lax.all_gather(weights, "section", axis=1, tiled=True)

    kept = []
    x = own_x
    for s in range(sections):
        blocks = exchanged(spread(x, members), "tp")
        full = blocks.transpose(1, 0, 2).reshape(tokens, features)
        product = jnp.dot(full, matrices[s], preferred_element_type=F32)
        squares = jnp.sum(jnp.square(full.astype(F32)), axis=1)
        inverse_rms = lax.rsqrt(squares / features + EPSILON)
        activation = inverse_rms[:, None] * product
        kept.append((blocks, full, product, inverse_rms, activation))
        x = (x.astype(F32) + jax.nn.silu(activation)).astype(BF16)

    cotangent = (x.astype(F32) - own_target.astype(F32)) / micro_tokens
    grads_h = [None] * sections
    for s in reversed(range(sections)):
        blocks, full, product, inverse_rms, activation = kept[s]
        h = (inverse_rms[:, None] * cotangent * silu_slope(activation)).astype(BF16)
        grads_h[s] = h
        if s == 0:
            break
        share = jnp.sum(h.astype(F32) * product, axis=1)
        back = lax.dot_general(h, matrices[s], (((1,), (1,)), ((), ())), preferred_element_type=F32)
        back = back - (inverse_rms * inverse_rms / features * share)[:, None] * full.astype(F32)
        parts = back.astype(BF16).reshape(tokens, members, columns).transpose(1, 0, 2)
        got = exchanged(parts, "tp")
        cotangent = (cotangent + jnp.sum(got.astype(F32), axis=0)).astype(BF16).astype(F32)

    outgoing = []
    for s in range(sections):
        rows = kept[s][0].reshape(groups, members // groups, tokens, columns)
        outgoing.append(rows)
        outgoing.append(jnp.broadcast_to(grads_h[s][None, None], (groups, 1, tokens, columns)))
    per = members // groups + 1
    arrived = exchanged(jnp.concatenate(outgoing, axis=1), "section")
    arrived = arrived.reshape(groups, sections, per, tokens, columns).transpose(1, 2, 0, 3, 4)
    arrived = arrived.reshape(sections, per, all_tokens, columns)
    result = []
    for s in range(sections):
        left = arrived[s, : per - 1]
        right = arrived[s, per - 1]
        result.append(
            lax.dot_general(left, right, (((1,), (0,)), ((), ())), preferred_element_type=F32)
            .astype(BF16)
            .reshape(row_count, columns)
        )
    return jnp.stack(result)


def solution(mesh):
    placed = (P(None, None, None, "tp"), P(None, "section", "tp"), P(None, None, None, "tp"))
    return jax.shard_map(
        on_device, mesh=mesh, in_specs=placed, out_specs=P(None, "section", "tp"), check_vma=False
    )
```

time: 2320 us -> 411 us (0.18)
  the two profiles are of different devices: /device:TPU:1 before, /device:TPU:8 now
where the time goes in v1:
time: 411 us; the launch traced here: 410 us
  blocking collectives  252 us (61%)
  waiting for transfers between devices  107 us (26%)
  matrix products  16.2 us (4%)
  between operations  13.9 us (3%)
  local copies, waits for them, and re-layouts  12.5 us (3%)
  starting transfers between devices  4.94 us (1%)
    all_to_all x15, blocking collectives, exchanged(): return lax.all_to_all(blocks, axis, split_axis=0, concat_axis=0, tiled=True)  252 us
    all_gather x1, waiting for transfers between devices, on_device(): matrices = lax.all_gather(weights, 'section', axis=1, tiled=True)  97.3 us
    dot_general x8, matrix products, on_device(): product = jnp.dot(full, matrices[s], preferred_element_type=F32)  11.6 us
    all_to_all x1, waiting for transfers between devices, exchanged(): return lax.all_to_all(blocks, axis, split_axis=0, concat_axis=0, tiled=True)  8.53 us
  transfers between devices with their start and end apart: 2, of which 2 were waited for; matrix products, arithmetic and copies ran while one was open for 0% of the time, Pallas kernels for 0%

profile of v1, /device:TPU:8, one launch (start us, length us, event | category | flops | bytes accessed | tf_op | source)
XLA Modules:
  0.0 409.8 jit_solution(11301479345079587975)
XLA Ops:
  6.5 0.7 all-gather.2.cloned.1.call-update
  7.3 0.1 copy-done
  7.4 23.1 %all_to_all.80 = bf16[32,16,128]{2,1,0:T(8,128)(2,1)S(1)} all-to-all(bf16[32,16,128]{2,1,0:T(8,128)(2,1)S(1)} %broadcast_in_dim.32), channel_id=1, replica_groups=mesh['section'=16,'tp'=32] {'tp'}, dimensions={0} | all-to-all | bytes 262144 | tf_op jit(solution)/shard_map/all_to_all | solution.py:21
  30.5 0.1 multiply_reduce_fusion.7
  30.7 97.3 %all-gather.2.cloned.1.call-done = bf16[8,4096,128]{2,1,0:T(8,128)(2,1)} async-done(((bf16[8,256,128]{2,1,0:T(8,128)(2,1)}), bf16[8,4096,128]{2,1,0:T(8,128)(2,1)}) %all-gather.2.cloned.1.call-update) | async-done | bytes 8388624 | tf_op jit(solution)/shard_map/all_gather | solution.py:37
  128.0 1.6 add_convert_fusion.8
  129.7 18.5 %all_to_all.81 = bf16[32,16,128]{2,1,0:T(8,128)(2,1)S(1)} all-to-all(bf16[32,16,128]{2,1,0:T(8,128)(2,1)S(1)} %broadcast_in_dim.33), channel_id=1, replica_groups=mesh['section'=16,'tp'=32] {'tp'}, dimensions={0} | all-to-all | bytes 262144 | tf_op jit(solution)/shard_map/all_to_all | solution.py:21
  148.2 0.1 multiply_reduce_fusion.6
  148.3 1.5 add_convert_fusion.7
  149.8 13.9 %all_to_all.82 = bf16[32,16,128]{2,1,0:T(8,128)(2,1)S(1)} all-to-all(bf16[32,16,128]{2,1,0:T(8,128)(2,1)S(1)} %broadcast_in_dim.34), channel_id=1, replica_groups=mesh['section'=16,'tp'=32] {'tp'}, dimensions={0} | all-to-all | bytes 262144 | tf_op jit(solution)/shard_map/all_to_all | solution.py:21
  163.7 0.1 multiply_reduce_fusion.5
  163.9 1.5 add_convert_fusion.6
  165.4 13.6 %all_to_all.83 = bf16[32,16,128]{2,1,0:T(8,128)(2,1)S(1)} all-to-all(bf16[32,16,128]{2,1,0:T(8,128)(2,1)S(1)} %broadcast_in_dim.35), channel_id=1, replica_groups=mesh['section'=16,'tp'=32] {'tp'}, dimensions={0} | all-to-all | bytes 262144 | tf_op jit(solution)/shard_map/all_to_all | solution.py:21
  179.0 0.1 multiply_reduce_fusion.4
  179.2 1.5 add_convert_fusion.5
  180.7 13.6 %all_to_all.84 = bf16[32,16,128]{2,1,0:T(8,128)(2,1)S(1)} all-to-all(bf16[32,16,128]{2,1,0:T(8,128)(2,1)S(1)} %broadcast_in_dim.36), channel_id=1, replica_groups=mesh['section'=16,'tp'=32] {'tp'}, dimensions={0} | all-to-all | bytes 262144 | tf_op jit(solution)/shard_map/all_to_all | solution.py:21
  194.3 0.1 multiply_reduce_fusion.3
  194.4 1.5 add_convert_fusion.4
  196.0 13.6 %all_to_all.85 = bf16[32,16,128]{2,1,0:T(8,128)(2,1)S(1)} all-to-all(bf16[32,16,128]{2,1,0:T(8,128)(2,1)S(1)} %broadcast_in_dim.37), channel_id=1, replica_groups=mesh['section'=16,'tp'=32] {'tp'}, dimensions={0} | all-to-all | bytes 262144 | tf_op jit(solution)/shard_map/all_to_all | solution.py:21
  209.6 0.1 multiply_reduce_fusion.2
  209.7 1.5 add_convert_fusion.3
  211.3 13.6 %all_to_all.86 = bf16[32,16,128]{2,1,0:T(8,128)(2,1)S(1)} all-to-all(bf16[32,16,128]{2,1,0:T(8,128)(2,1)S(1)} %broadcast_in_dim.38), channel_id=1, replica_groups=mesh['section'=16,'tp'=32] {'tp'}, dimensions={0} | all-to-all | bytes 262144 | tf_op jit(solution)/shard_map/all_to_all | solution.py:21
  224.9 0.1 multiply_reduce_fusion.1
  225.0 1.5 add_convert_fusion.2
  226.6 13.6 %all_to_all.87 = bf16[32,16,128]{2,1,0:T(8,128)(2,1)S(1)} all-to-all(bf16[32,16,128]{2,1,0:T(8,128)(2,1)S(1)} %broadcast_in_dim.39), channel_id=1, replica_groups=mesh['section'=16,'tp'=32] {'tp'}, dimensions={0} | all-to-all | bytes 262144 | tf_op jit(solution)/shard_map/all_to_all | solution.py:21
  240.2 0.1 multiply_reduce_fusion
  240.3 1.1 multiply_reduce_fusion.14
  241.4 0.4 fusion.13
  241.8 13.6 %all_to_all.88 = bf16[32,16,128]{2,1,0:T(8,128)(2,1)S(1)} all-to-all(bf16[32,16,128]{2,1,0:T(8,128)(2,1)S(1)} %bitcast.339), channel_id=1, replica_groups=mesh['section'=16,'tp'=32] {'tp'}, dimensions={0} | all-to-all | bytes 262144 | tf_op jit(solution)/shard_map/all_to_all | solution.py:21
  255.5 0.9 multiply_reduce_fusion.13
  256.4 0.4 fusion.12
  256.8 13.6 %all_to_all.89 = bf16[32,16,128]{2,1,0:T(8,128)(2,1)S(1)} all-to-all(bf16[32,16,128]{2,1,0:T(8,128)(2,1)S(1)} %bitcast.340), channel_id=1, replica_groups=mesh['section'=16,'tp'=32] {'tp'}, dimensions={0} | all-to-all | bytes 262144 | tf_op jit(solution)/shard_map/all_to_all | solution.py:21
  270.5 0.2 multiply_reduce_fusion.12
  270.7 0.4 fusion.11
  271.1 13.6 %all_to_all.90 = bf16[32,16,128]{2,1,0:T(8,128)(2,1)S(1)} all-to-all(bf16[32,16,128]{2,1,0:T(8,128)(2,1)S(1)} %bitcast.341), channel_id=1, replica_groups=mesh['section'=16,'tp'=32] {'tp'}, dimensions={0} | all-to-all | bytes 262144 | tf_op jit(solution)/shard_map/all_to_all | solution.py:21
  284.8 0.2 multiply_reduce_fusion.11
  285.0 0.4 fusion.10
  285.4 13.6 %all_to_all.91 = bf16[32,16,128]{2,1,0:T(8,128)(2,1)S(1)} all-to-all(bf16[32,16,128]{2,1,0:T(8,128)(2,1)S(1)} %bitcast.342), channel_id=1, replica_groups=mesh['section'=16,'tp'=32] {'tp'}, dimensions={0} | all-to-all | bytes 262144 | tf_op jit(solution)/shard_map/all_to_all | solution.py:21
  299.0 0.2 multiply_reduce_fusion.10
  299.2 0.4 fusion.9
  299.7 13.6 %all_to_all.92 = bf16[32,16,128]{2,1,0:T(8,128)(2,1)S(1)} all-to-all(bf16[32,16,128]{2,1,0:T(8,128)(2,1)S(1)} %bitcast.343), channel_id=1, replica_groups=mesh['section'=16,'tp'=32] {'tp'}, dimensions={0} | all-to-all | bytes 262144 | tf_op jit(solution)/shard_map/all_to_all | solution.py:21
  313.3 0.2 multiply_reduce_fusion.9
  313.5 0.4 fusion.8
  314.0 13.6 %all_to_all.93 = bf16[32,16,128]{2,1,0:T(8,128)(2,1)S(1)} all-to-all(bf16[32,16,128]{2,1,0:T(8,128)(2,1)S(1)} %bitcast.344), channel_id=1, replica_groups=mesh['section'=16,'tp'=32] {'tp'}, dimensions={0} | all-to-all | bytes 262144 | tf_op jit(solution)/shard_map/all_to_all | solution.py:21
  327.6 0.2 multiply_reduce_fusion.8
  327.8 0.4 fusion.7
  328.2 0.7 copy.163
  328.9 4.9 %all-to-all-start.14 = ((bf16[32,16,128]{2,1,0:T(8,128)(2,1)}), bf16[32,16,128]{2,1,0:T(8,128)(2,1)S(1)}, u32[]{:S(2)}, u32[]{:S(2)}) async-start(bf16[32,16,128]{2,1,0:T(8,128)(2,1)} %bitcast.301), calls=%async_computation.14 | async-start | bytes 262144 | tf_op jit(solution)/shard_map/all_to_all | solution.py:21
  334.7 8.5 %all-to-all-done.14 = bf16[32,16,128]{2,1,0:T(8,128)(2,1)S(1)} async-done(((bf16[32,16,128]{2,1,0:T(8,128)(2,1)}), bf16[32,16,128]{2,1,0:T(8,128)(2,1)S(1)}, u32[]{:S(2)}, u32[]{:S(2)}) %all-to-all-start.14) | async-done | bytes 131104 | tf_op jit(solution)/shard_map/all_to_all | solution.py:21
  343.8 0.7 broadcast_in_dim.46
  344.6 0.7 broadcast_in_dim.47
  345.3 6.7 %concatenate.3 = bf16[16,24,16,128]{3,1,2,0:T(8,128)(2,1)S(1)} concatenate(bf16[16,2,16,128]{3,1,2,0:T(2,128)(2,1)S(1)} %copy.59, bf16[16,1,16,128]{3,1,2,0:T(2,128)(2,1)S(1)} %broadcast_in_dim.40, bf16[16,2,16,128]{3,1,2,0:T(2,128)(2,1)S(1)} %copy.60, bf16[16,1,16,128]{3,1,2,0:T(2,128)(2,1)S(1)} %broadcast_in_dim.41, bf16[16,2,16,128]{3,1,2,0:T(2,128)(2,1)S(1)} %copy.61, ...), dimensions={1} | concatenate | bytes 3145728 | tf_op jit(solution)/shard_map/concatenate | solution.py:72
  352.0 47.2 %all_to_all.94 = bf16[16,24,16,128]{3,1,2,0:T(8,128)(2,1)S(1)} all-to-all(bf16[16,24,16,128]{3,1,2,0:T(8,128)(2,1)S(1)} %concatenate.3), channel_id=1, replica_groups=mesh['section'=16,'tp'=32] {'section'}, dimensions={0} | all-to-all | bytes 3145728 | tf_op jit(solution)/shard_map/all_to_all | solution.py:21
  399.2 0.3 copy.85
  399.6 0.2 convolution_convert_fusion.7
  399.8 0.2 convolution_convert_fusion.6
  400.0 0.2 convolution_convert_fusion.5
  400.3 0.2 convolution_convert_fusion.4
  400.5 0.2 convolution_convert_fusion.3
  400.7 0.2 convolution_convert_fusion.2
  401.0 0.2 convolution_convert_fusion.1
  401.2 0.2 convolution_convert_fusion
  401.6 0.8 copy-done.2
  402.4 0.6 bitcast_dynamic-update-slice_fusion
  (64 shorter events, 2.2 us)
Async XLA Ops:
  6.5 0.8 copy-start
  6.5 121.5 %all-gather.2.cloned.1.call-start = ((), (), s32[]{:S(2)}) async-start(), calls=%async_computation.16 | async-start | bytes 8912896 | tf_op jit(solution)/shard_map/all_gather | solution.py:37
  128.0 112.3 %copy-start.1 = (bf16[8,4096,128]{2,1,0:T(8,128)(2,1)S(1)}, bf16[8,4096,128]{2,1,0:T(8,128)(2,1)}, u32[]{:S(2)}) copy-start(bf16[8,4096,128]{2,1,0:T(8,128)(2,1)} %all-gather.2.cloned.1.call-done) | copy-start | bytes 25165828
  328.9 14.4 %all-to-all-start.14 = ((bf16[32,16,128]{2,1,0:T(8,128)(2,1)}), bf16[32,16,128]{2,1,0:T(8,128)(2,1)S(1)}, u32[]{:S(2)}, u32[]{:S(2)}) async-start(bf16[32,16,128]{2,1,0:T(8,128)(2,1)} %bitcast.301), calls=%async_computation.14 | async-start | bytes 262144 | tf_op jit(solution)/shard_map/all_to_all | solution.py:21
  401.6 0.8 copy-start.2
Sparse Core Ops, SparseCore 0:
  10.7 117.2 all-gather.1

commit v2 on v1

v2 whole, which is shorter than its diff:
```python
import functools

import jax
import jax.numpy as jnp
from jax import lax
from jax.experimental import pallas as pl
from jax.experimental.pallas import tpu as pltpu
from jax.sharding import Mesh, PartitionSpec as P

EPSILON = 1e-05
F32 = jnp.float32
BF16 = jnp.bfloat16
TP = "tp"
SECTION = ("x", "far", "core")
EARLY = 3
CHUNKS = 4
RIDERS = (0, 2, 2, 2, 2, 0, 0)


def spread(block, copies):
    return lax.optimization_barrier(jnp.broadcast_to(block[None], (copies,) + block.shape))


def exchanged(blocks, axis):
    return lax.all_to_all(blocks, axis, split_axis=0, concat_axis=0, tiled=True)


def swapped(block, axis):
    return lax.ppermute(block, axis, [(0, 1), (1, 0)])


def in_order(own, other, axis, at):
    first = lax.axis_index(axis) == 0
    return jnp.stack([jnp.where(first, own, other), jnp.where(first, other, own)], axis=at)


def fetched_matrices(weights, own_x, members):
    sections, row_count, columns = weights.shape
    first = weights[:EARLY]
    crossed = swapped(first, "far")
    blocks = exchanged(spread(own_x, members), TP)
    crossed, blocks, last = lax.optimization_barrier((crossed, blocks, weights[EARLY:]))
    crossed_last = swapped(last, "far")
    pair = in_order(first, crossed, "far", 1).reshape(EARLY, 2 * row_count, columns)
    mine = exchanged(spread(pair, lax.axis_size("x")), "x")
    crossed_last, mine = lax.optimization_barrier((crossed_last, mine))
    pair = in_order(last, crossed_last, "far", 1).reshape(-1, 2 * row_count, columns)
    late = lax.all_gather(pair, ("x", "core"), axis=1, tiled=True)
    both = in_order(mine, swapped(mine, "core"), "core", 1)
    early = both.transpose(2, 0, 1, 3, 4).reshape(EARLY, -1, columns)
    late = pltpu.with_memory_space_constraint(late, pltpu.HBM)
    early = pltpu.with_memory_space_constraint(early, pltpu.HBM)
    matrices = [(early, s) for s in range(EARLY)]
    matrices += [(late, s) for s in range(sections - EARLY)]
    return matrices, blocks


def block_order(far, cores, across, per):
    return [
        ((x * far + f) * cores + c) * per + b
        for x in range(across)
        for c in range(cores)
        for f in range(far)
        for b in range(per)
    ]


def fetches(layer, matrices, held, arrived):
    rows = held.shape[0] // CHUNKS
    copies = []
    for n in range(CHUNKS):
        part = pl.ds(n * rows, rows)
        copy = pltpu.make_async_copy(matrices.at[layer, part], held.at[part], arrived.at[n])
        copy.start()
        copies.append(copy)
    return copies


def forward_kernel(order, layer, got, x, matrices, *rest):
    *sent, x_new, slope, scaled, held, arrived = rest
    copies = fetches(layer, matrices, held, arrived)
    features, columns = held.shape
    squares = jnp.zeros(x.shape, F32)
    for m in range(len(order)):
        squares += jnp.square(got[m].astype(F32))
    mean = jnp.sum(squares, axis=1, keepdims=True) / features
    inverse_rms = lax.rsqrt(mean + EPSILON)
    product = jnp.zeros(x.shape, F32)
    rows, count = features // CHUNKS, len(order) // CHUNKS
    for n in range(CHUNKS):
        segment = jnp.concatenate([got[m] for m in order[n * count : (n + 1) * count]], axis=1)
        copies[n].wait()
        product += jnp.dot(segment, held[pl.ds(n * rows, rows), :], preferred_element_type=F32)
    activation = inverse_rms * product
    sigmoid = jax.nn.sigmoid(activation)
    result = (x[...].astype(F32) + activation * sigmoid).astype(BF16)
    x_new[...] = result
    for target in sent:
        target[...] = jnp.broadcast_to(result[None], target.shape)
    slope[...] = inverse_rms * sigmoid * (1.0 + activation * (1.0 - sigmoid))
    scaled[...] = product * (inverse_rms * inverse_rms / features)


def backward_kernel(order, layer, riding, *refs):
    if riding:
        riders, *refs = refs
    received, cotangent, slope, scaled, blocks, matrices, *rest = refs
    parts, h_out, cot_out, held, arrived = rest
    copies = fetches(layer, matrices, held, arrived)
    if riding:
        for n in range(riding):
            parts[:, 1 + n] = jnp.broadcast_to(riders[n][None], (len(order),) + riders.shape[1:])
    cot = cotangent[...]
    if len(received.shape) == 3:
        total = cot
        for m in range(len(order)):
            total += received[m].astype(F32)
        cot = total.astype(BF16).astype(F32)
    cot_out[...] = cot
    h = (slope[...] * cot).astype(BF16)
    h_out[...] = h
    share = jnp.sum(h.astype(F32) * scaled[...], axis=1, keepdims=True)
    features, columns = held.shape
    rows, count = features // CHUNKS, len(order) // CHUNKS
    for n in range(CHUNKS):
        copies[n].wait()
        back = lax.dot_general(
            h,
            held[pl.ds(n * rows, rows), :],
            (((1,), (1,)), ((), ())),
            preferred_element_type=F32,
        )
        for k in range(count):
            m = order[n * count + k]
            mine = back[:, k * columns : (k + 1) * columns] - share * blocks[m].astype(F32)
            if riding:
                parts[m, 0] = mine.astype(BF16)
            else:
                parts[m] = mine.astype(BF16)


def local_call(kernel, outs, features, columns, specs):
    vmem = pl.BlockSpec(memory_space=pltpu.VMEM)
    hbm = pl.BlockSpec(memory_space=pltpu.HBM)
    return pl.pallas_call(
        kernel,
        out_shape=[pltpu.VMEM(shape, dtype) for shape, dtype in outs],
        in_specs=[vmem if spec else hbm for spec in specs],
        out_specs=[vmem] * len(outs),
        scratch_shapes=[
            pltpu.VMEM((features, columns), BF16),
            pltpu.SemaphoreType.DMA((CHUNKS,)),
        ],
        compiler_params=pltpu.CompilerParams(vmem_limit_bytes=16 * 2**20),
    )


def forward_layer(order, layer, got, x, matrices, sending):
    members, tokens, columns = got.shape
    outs = [(got.shape, BF16)] if sending else []
    outs += [(x.shape, BF16), (x.shape, F32), (x.shape, F32)]
    kernel = functools.partial(forward_kernel, order, layer)
    call = local_call(kernel, outs, members * columns, columns, (True, True, False))
    return call(got, x, matrices)


def backward_layer(order, layer, received, cotangent, slope, scaled, blocks, matrices, riders):
    members, tokens, columns = blocks.shape
    riding = 0 if riders is None else riders.shape[0]
    shape = (members, 1 + riding, tokens, columns) if riding else blocks.shape
    outs = [(shape, BF16), (cotangent.shape, BF16), (cotangent.shape, F32)]
    kernel = functools.partial(backward_kernel, order, layer, riding)
    blocks = pltpu.with_memory_space_constraint(blocks, pltpu.VMEM)
    given = ([riders] if riding else []) + [received, cotangent, slope, scaled, blocks, matrices]
    specs = [True] * (len(given) - 1) + [False]
    return local_call(kernel, outs, members * columns, columns, specs)(*given)


def moved_rows(x_stack, groups, members):
    per = members // groups
    pairs = [
        (g * members + per * r + b, r * members + per * g + b)
        for g in range(groups)
        for r in range(groups)
        for b in range(per)
    ]
    return lax.ppermute(x_stack, SECTION + (TP,), pairs)


def on_device(inputs, weights, targets):
    groups = lax.axis_size(SECTION)
    members = lax.axis_size(TP)
    group = lax.axis_index(SECTION)
    across, cores = lax.axis_size("x"), lax.axis_size("core")
    sections, row_count, columns = weights.shape
    micro_tokens = inputs.shape[2]
    all_tokens = inputs.shape[0] * inputs.shape[1] * micro_tokens
    tokens = all_tokens // groups
    per = members // groups
    own_x = lax.dynamic_slice_in_dim(inputs.reshape(all_tokens, columns), group * tokens, tokens, 0)
    own_target = lax.dynamic_slice_in_dim(
        targets.reshape(all_tokens, columns), group * tokens, tokens, 0
    )
    matrices, blocks = fetched_matrices(weights, own_x, members)

    order = block_order(2, cores, across, per)
    kept = []
    xs = [own_x]
    for s in range(sections):
        held, at = matrices[s]
        *sent, x, slope, scaled = forward_layer(order, at, blocks, xs[-1], held, s < sections - 1)
        kept.append((blocks, slope, scaled))
        if sent:
            xs.append(x)
            blocks = exchanged(sent[0], TP)

    riders = moved_rows(jnp.stack(xs), groups, members)
    all_rows = []
    cotangent = (x.astype(F32) - own_target.astype(F32)) / micro_tokens
    grads_h = [None] * sections
    received = x
    for s in range(sections - 1, 0, -1):
        blocks, slope, scaled = kept[s]
        held, at = matrices[s]
        count = RIDERS[sections - 1 - s]
        taken = riders[len(all_rows) : len(all_rows) + count] if count else None
        parts, grads_h[s], cotangent = backward_layer(
            order, at, received, cotangent, slope, scaled, blocks, held, taken
        )
        received = exchanged(parts, TP)
        if count:
            all_rows.extend(received[:, 1 + n] for n in range(count))
            received = received[:, 0]
    cotangent = (cotangent + jnp.sum(received.astype(F32), axis=0)).astype(BF16).astype(F32)
    grads_h[0] = (kept[0][1] * cotangent).astype(BF16)

    h_all = exchanged(spread(jnp.stack(grads_h), groups), SECTION)
    result = []
    for s in range(sections):
        left = all_rows[s].reshape(groups, per, tokens, columns)
        result.append(
            lax.dot_general(
                left, h_all[:, s], (((0, 2), (0, 1)), ((), ())), preferred_element_type=F32
            )
            .astype(BF16)
            .reshape(row_count, columns)
        )
    return jnp.stack(result)


def solution(mesh):
    devices = mesh.devices.reshape(4, 2, 2, mesh.shape[TP])
    finer = Mesh(devices, SECTION + (TP,))
    matrix = P(None, SECTION, TP)
    placed = (P(None, None, None, TP), matrix, P(None, None, None, TP))
    return jax.shard_map(
        on_device, mesh=finer, in_specs=placed, out_specs=matrix, check_vma=False
    )
```

time: 411 us -> 364 us (0.89)
  blocking collectives: 252 us -> 180 us
  starting transfers between devices: 4.94 us -> 57.5 us
  waiting for transfers between devices: 107 us -> 68.8 us
  Pallas kernels: 0 us -> 29 us
  matrix products: 16.2 us -> 1.89 us
    all_gather x1, waiting for transfers between devices: 97.3 us -> 0.01 us  [fetched_matrices(): late = lax.all_gather(pair, ('x', 'core'), axis=1, tiled=True)]
    all_to_all x15 -> x10, blocking collectives: 252 us -> 180 us  [exchanged(): return lax.all_to_all(blocks, axis, split_axis=0, concat_axis=0, tiled=True)]
    all_to_all x1 -> x7, waiting for transfers between devices: 8.53 us -> 50.5 us  [exchanged(): return lax.all_to_all(blocks, axis, split_axis=0, concat_axis=0, tiled=True)]
    all_to_all x1 -> x7, starting transfers between devices: 4.94 us -> 43.1 us  [exchanged(): return lax.all_to_all(blocks, axis, split_axis=0, concat_axis=0, tiled=True)]
    pallas_call x0 -> x15, Pallas kernels: none -> 29 us  [the longest x8 15.9 us: forward_layer(): return call(got, x, matrices)]
    ppermute x0 -> x4, waiting for transfers between devices: none -> 18.4 us  [the longest x3 18.4 us: swapped(): return lax.ppermute(block, axis, [(0, 1), (1, 0)])]
    ppermute x0 -> x4, starting transfers between devices: none -> 14.4 us  [the longest x3 12.2 us: swapped(): return lax.ppermute(block, axis, [(0, 1), (1, 0)])]
    dot_general x23 -> x8, matrix products: 16.2 us -> 1.89 us  [on_device(): lax.dot_general(left, h_all[:, s], (((0, 2), (0, 1)), ((), ())), preferre...]
  transfers between devices with their start and end apart: 2 -> 12, of which waited for: 2 -> 9; matrix products, arithmetic and copies ran while one was open for 0% -> 1% of each run, Pallas kernels for 0% -> 3%
where the time goes in v2:
time: 364 us; the launch traced here: 362 us
  blocking collectives  180 us (49%)
  waiting for transfers between devices  68.8 us (19%)
  starting transfers between devices  57.5 us (16%)
  Pallas kernels  29 us (8%)
  between operations  13.8 us (4%)
  local copies, waits for them, and re-layouts  9.3 us (3%)
    all_to_all x10, blocking collectives, exchanged(): return lax.all_to_all(blocks, axis, split_axis=0, concat_axis=0, tiled=True)  180 us
    all_to_all x7, waiting for transfers between devices, exchanged(): return lax.all_to_all(blocks, axis, split_axis=0, concat_axis=0, tiled=True)  50.5 us
    all_to_all x7, starting transfers between devices, exchanged(): return lax.all_to_all(blocks, axis, split_axis=0, concat_axis=0, tiled=True)  43.1 us
    ppermute x3, waiting for transfers between devices, swapped(): return lax.ppermute(block, axis, [(0, 1), (1, 0)])  18.4 us
    pallas_call x8, Pallas kernels, forward_layer(): return call(got, x, matrices)  15.9 us
    pallas_call x7, Pallas kernels, backward_layer(): return local_call(kernel, outs, members * columns, columns, specs)(*given)  13 us
    ppermute x3, starting transfers between devices, swapped(): return lax.ppermute(block, axis, [(0, 1), (1, 0)])  12.2 us
  transfers between devices with their start and end apart: 12, of which 9 were waited for; matrix products, arithmetic and copies ran while one was open for 1% of the time, Pallas kernels for 3%

profile of v2, /device:TPU:8, one launch (start us, length us, event | category | flops | bytes accessed | tf_op | source)
XLA Modules:
  0.0 362.2 jit_solution(10708654859388238104)
XLA Ops:
  6.5 0.7 constant_dynamic-update-slice_fusion.7
  7.2 0.7 broadcast_in_dim.8
  7.9 14.0 %all-to-all-start = ((bf16[32,16,128]{2,1,0:T(8,128)(2,1)}), bf16[32,16,128]{2,1,0:T(8,128)(2,1)S(1)}, u32[]{:S(2)}, u32[]{:S(2)}) async-start(bf16[32,16,128]{2,1,0:T(8,128)(2,1)} %broadcast_in_dim.8), calls=%async_computation | async-start | bytes 262144 | tf_op jit(solution)/shard_map/all_to_all | solution.py:25
  21.9 0.9 slice.78
  22.8 5.0 %collective-permute-start = (bf16[3,256,128]{2,1,0:T(8,128)(2,1)S(1)}, bf16[3,256,128]{2,1,0:T(8,128)(2,1)S(1)}, u32[]{:S(2)}, u32[]{:S(2)}) collective-permute-start(bf16[3,256,128]{2,1,0:T(8,128)(2,1)S(1)} %slice.78), channel_id=1, source_target_pairs={{0,64},{64,0},{1,65},{65,1},{2,66},{66,2},{3,67},{67,3},{4,68},{68... | collective-permute-start | bytes 589832 | tf_op jit(solution)/shard_map/ppermute | solution.py:29
  27.9 1.0 slice.79
  28.9 7.1 %collective-permute-done = bf16[3,256,128]{2,1,0:T(8,128)(2,1)S(1)} collective-permute-done((bf16[3,256,128]{2,1,0:T(8,128)(2,1)S(1)}, bf16[3,256,128]{2,1,0:T(8,128)(2,1)S(1)}, u32[]{:S(2)}, u32[]{:S(2)}) %collective-permute-start) | collective-permute-done | bytes 196640 | tf_op jit(solution)/shard_map/ppermute | solution.py:29
  35.9 1.0 select_bitcast_fusion.5
  37.0 1.4 broadcast_in_dim.10
  38.4 4.3 %all-to-all-start.1 = ((bf16[4,3,512,128]{3,2,1,0:T(8,128)(2,1)}), bf16[4,3,512,128]{3,2,1,0:T(8,128)(2,1)S(1)}, u32[]{:S(2)}, u32[]{:S(2)}) async-start(bf16[4,3,512,128]{3,2,1,0:T(8,128)(2,1)} %broadcast_in_dim.10), calls=%async_computation.1 | async-start | bytes 3145728 | tf_op jit(solution)/shard_map/all_to_all | solution.py:25
  42.7 5.2 %collective-permute-start.1 = (bf16[5,256,128]{2,1,0:T(8,128)(2,1)S(1)}, bf16[5,256,128]{2,1,0:T(8,128)(2,1)S(1)}, u32[]{:S(2)}, u32[]{:S(2)}) collective-permute-start(bf16[5,256,128]{2,1,0:T(8,128)(2,1)S(1)} %slice.79), channel_id=1, source_target_pairs={{0,64},{64,0},{1,65},{65,1},{2,66},{66,2},{3,67},{67,3},{4,68},{68... | collective-permute-start | bytes 983048 | tf_op jit(solution)/shard_map/ppermute | solution.py:29
  47.9 7.9 %collective-permute-done.1 = bf16[5,256,128]{2,1,0:T(8,128)(2,1)S(1)} collective-permute-done((bf16[5,256,128]{2,1,0:T(8,128)(2,1)S(1)}, bf16[5,256,128]{2,1,0:T(8,128)(2,1)S(1)}, u32[]{:S(2)}, u32[]{:S(2)}) %collective-permute-start.1) | collective-permute-done | bytes 327712 | tf_op jit(solution)/shard_map/ppermute | solution.py:29
  55.9 5.7 %all-to-all-done.1 = bf16[4,3,512,128]{3,2,1,0:T(8,128)(2,1)S(1)} async-done(((bf16[4,3,512,128]{3,2,1,0:T(8,128)(2,1)}), bf16[4,3,512,128]{3,2,1,0:T(8,128)(2,1)S(1)}, u32[]{:S(2)}, u32[]{:S(2)}) %all-to-all-start.1) | async-done | bytes 1572896 | tf_op jit(solution)/shard_map/all_to_all | solution.py:25
  61.6 0.9 copy.35
  62.6 1.9 collective-permute-start.2
  64.5 3.4 collective-permute-done.2
  68.1 0.3 maximum_bitcast_fusion
  68.4 2.0 copy.34
  70.4 2.2 shard_map.37
  72.6 23.6 %all_to_all.85.got.refs_4_ = bf16[32,16,128]{2,1,0:T(8,128)(2,1)S(1)} all-to-all(bf16[32,16,128]{2,1,0:T(8,128)(2,1)S(1)} %get-tuple-element.66), channel_id=1, replica_groups=mesh['x'=4,'far'=2,'core'=2,'tp'=32] {'tp'}, dimensions={0} | all-to-all | bytes 262144 | tf_op jit(solution)/shard_map/all_to_all | solution.py:25
  96.2 1.6 shard_map.38
  97.8 13.7 %all_to_all.86.got.refs_4_ = bf16[32,16,128]{2,1,0:T(8,128)(2,1)S(1)} all-to-all(bf16[32,16,128]{2,1,0:T(8,128)(2,1)S(1)} %get-tuple-element.68), channel_id=1, replica_groups=mesh['x'=4,'far'=2,'core'=2,'tp'=32] {'tp'}, dimensions={0} | all-to-all | bytes 262144 | tf_op jit(solution)/shard_map/all_to_all | solution.py:25
  111.6 1.6 shard_map.39
  113.2 13.6 %all_to_all.87.got.refs_5_ = bf16[32,16,128]{2,1,0:T(8,128)(2,1)S(1)} all-to-all(bf16[32,16,128]{2,1,0:T(8,128)(2,1)S(1)} %get-tuple-element.70), channel_id=1, replica_groups=mesh['x'=4,'far'=2,'core'=2,'tp'=32] {'tp'}, dimensions={0} | all-to-all | bytes 262144 | tf_op jit(solution)/shard_map/all_to_all | solution.py:25
  126.8 2.2 shard_map.40
  129.1 4.9 %all-to-all-start.5 = ((bf16[32,16,128]{2,1,0:T(8,128)(2,1)}), bf16[32,16,128]{2,1,0:T(8,128)(2,1)S(1)}, u32[]{:S(2)}, u32[]{:S(2)}) async-start(bf16[32,16,128]{2,1,0:T(8,128)(2,1)} %get-tuple-element.73), calls=%async_computation.5 | async-start | bytes 262144 | tf_op jit(solution)/shard_map/all_to_all | solution.py:25
  134.0 9.4 %all-to-all-done.5.got.refs_5_ = bf16[32,16,128]{2,1,0:T(8,128)(2,1)S(1)} async-done(((bf16[32,16,128]{2,1,0:T(8,128)(2,1)}), bf16[32,16,128]{2,1,0:T(8,128)(2,1)S(1)}, u32[]{:S(2)}, u32[]{:S(2)}) %all-to-all-start.5) | async-done | bytes 131104 | tf_op jit(solution)/shard_map/all_to_all | solution.py:25
  143.4 2.2 shard_map.41
  145.7 4.9 %all-to-all-start.6 = ((bf16[32,16,128]{2,1,0:T(8,128)(2,1)}), bf16[32,16,128]{2,1,0:T(8,128)(2,1)S(1)}, u32[]{:S(2)}, u32[]{:S(2)}) async-start(bf16[32,16,128]{2,1,0:T(8,128)(2,1)} %get-tuple-element.75), calls=%async_computation.6 | async-start | bytes 262144 | tf_op jit(solution)/shard_map/all_to_all | solution.py:25
  150.7 9.4 %all-to-all-done.6.got.refs_5_ = bf16[32,16,128]{2,1,0:T(8,128)(2,1)S(1)} async-done(((bf16[32,16,128]{2,1,0:T(8,128)(2,1)}), bf16[32,16,128]{2,1,0:T(8,128)(2,1)S(1)}, u32[]{:S(2)}, u32[]{:S(2)}) %all-to-all-start.6) | async-done | bytes 131104 | tf_op jit(solution)/shard_map/all_to_all | solution.py:25
  160.1 2.2 shard_map.42
  162.3 4.9 %all-to-all-start.7 = ((bf16[32,16,128]{2,1,0:T(8,128)(2,1)}), bf16[32,16,128]{2,1,0:T(8,128)(2,1)S(1)}, u32[]{:S(2)}, u32[]{:S(2)}) async-start(bf16[32,16,128]{2,1,0:T(8,128)(2,1)} %get-tuple-element.77), calls=%async_computation.7 | async-start | bytes 262144 | tf_op jit(solution)/shard_map/all_to_all | solution.py:25
  167.3 9.4 %all-to-all-done.7.got.refs_5_ = bf16[32,16,128]{2,1,0:T(8,128)(2,1)S(1)} async-done(((bf16[32,16,128]{2,1,0:T(8,128)(2,1)}), bf16[32,16,128]{2,1,0:T(8,128)(2,1)S(1)}, u32[]{:S(2)}, u32[]{:S(2)}) %all-to-all-start.7) | async-done | bytes 131104 | tf_op jit(solution)/shard_map/all_to_all | solution.py:25
  176.7 2.2 shard_map.43
  178.9 4.9 %all-to-all-start.8 = ((bf16[32,16,128]{2,1,0:T(8,128)(2,1)}), bf16[32,16,128]{2,1,0:T(8,128)(2,1)S(1)}, u32[]{:S(2)}, u32[]{:S(2)}) async-start(bf16[32,16,128]{2,1,0:T(8,128)(2,1)} %get-tuple-element.79), calls=%async_computation.8 | async-start | bytes 262144 | tf_op jit(solution)/shard_map/all_to_all | solution.py:25
  183.9 2.2 collective-permute-start.3
  186.1 7.2 %all-to-all-done.8.got.refs_4_ = bf16[32,16,128]{2,1,0:T(8,128)(2,1)S(1)} async-done(((bf16[32,16,128]{2,1,0:T(8,128)(2,1)}), bf16[32,16,128]{2,1,0:T(8,128)(2,1)S(1)}, u32[]{:S(2)}, u32[]{:S(2)}) %all-to-all-start.8) | async-done | bytes 131104 | tf_op jit(solution)/shard_map/all_to_all | solution.py:25
  193.3 1.6 shard_map.44
  194.9 0.7 subtract_multiply_fusion.refs_1_
  195.6 2.4 shard_map.45
  198.0 5.0 %all-to-all-start.9 = ((bf16[32,16,128]{2,1,0:T(8,128)(2,1)}), bf16[32,16,128]{2,1,0:T(8,128)(2,1)S(1)}, u32[]{:S(2)}, u32[]{:S(2)}) async-start(bf16[32,16,128]{2,1,0:T(8,128)(2,1)} %get-tuple-element.83), calls=%async_computation.9 | async-start | bytes 262144 | tf_op jit(solution)/shard_map/all_to_all | solution.py:25
  203.1 9.4 %all-to-all-done.9.refs_1_ = bf16[32,16,128]{2,1,0:T(8,128)(2,1)S(1)} async-done(((bf16[32,16,128]{2,1,0:T(8,128)(2,1)}), bf16[32,16,128]{2,1,0:T(8,128)(2,1)S(1)}, u32[]{:S(2)}, u32[]{:S(2)}) %all-to-all-start.9) | async-done | bytes 131104 | tf_op jit(solution)/shard_map/all_to_all | solution.py:25
  212.5 1.8 shard_map.46
  214.2 16.0 %all_to_all.88 = bf16[32,3,16,128]{3,2,1,0:T(8,128)(2,1)S(1)} all-to-all(bf16[32,3,16,128]{3,2,1,0:T(8,128)(2,1)S(1)} %get-tuple-element.87), channel_id=1, replica_groups=mesh['x'=4,'far'=2,'core'=2,'tp'=32] {'tp'}, dimensions={0} | all-to-all | bytes 786432 | tf_op jit(solution)/shard_map/all_to_all | solution.py:25
  230.3 1.8 shard_map.47
  232.1 19.1 %all_to_all.89 = bf16[32,3,16,128]{3,2,1,0:T(8,128)(2,1)S(1)} all-to-all(bf16[32,3,16,128]{3,2,1,0:T(8,128)(2,1)S(1)} %get-tuple-element.92), channel_id=1, replica_groups=mesh['x'=4,'far'=2,'core'=2,'tp'=32] {'tp'}, dimensions={0} | all-to-all | bytes 786432 | tf_op jit(solution)/shard_map/all_to_all | solution.py:25
  251.2 1.8 shard_map.48
  252.9 19.3 %all_to_all.90 = bf16[32,3,16,128]{3,2,1,0:T(8,128)(2,1)S(1)} all-to-all(bf16[32,3,16,128]{3,2,1,0:T(8,128)(2,1)S(1)} %get-tuple-element.96), channel_id=1, replica_groups=mesh['x'=4,'far'=2,'core'=2,'tp'=32] {'tp'}, dimensions={0} | all-to-all | bytes 786432 | tf_op jit(solution)/shard_map/all_to_all | solution.py:25
  272.2 1.8 shard_map.49
  274.0 19.3 %all_to_all.91 = bf16[32,3,16,128]{3,2,1,0:T(8,128)(2,1)S(1)} all-to-all(bf16[32,3,16,128]{3,2,1,0:T(8,128)(2,1)S(1)} %get-tuple-element.100), channel_id=1, replica_groups=mesh['x'=4,'far'=2,'core'=2,'tp'=32] {'tp'}, dimensions={0} | all-to-all | bytes 786432 | tf_op jit(solution)/shard_map/all_to_all | solution.py:25
  293.3 1.8 shard_map.50
  295.1 14.6 %all_to_all.92.refs_0_ = bf16[32,16,128]{2,1,0:T(8,128)(2,1)S(1)} all-to-all(bf16[32,16,128]{2,1,0:T(8,128)(2,1)S(1)} %get-tuple-element.104), channel_id=1, replica_groups=mesh['x'=4,'far'=2,'core'=2,'tp'=32] {'tp'}, dimensions={0} | all-to-all | bytes 262144 | tf_op jit(solution)/shard_map/all_to_all | solution.py:25
  309.7 1.8 shard_map.51
  311.5 13.6 %all_to_all.93 = bf16[32,16,128]{2,1,0:T(8,128)(2,1)S(1)} all-to-all(bf16[32,16,128]{2,1,0:T(8,128)(2,1)S(1)} %get-tuple-element.109), channel_id=1, replica_groups=mesh['x'=4,'far'=2,'core'=2,'tp'=32] {'tp'}, dimensions={0} | all-to-all | bytes 262144 | tf_op jit(solution)/shard_map/all_to_all | solution.py:25
  325.3 26.9 %all_to_all.94 = bf16[16,8,16,128]{3,2,1,0:T(8,128)(2,1)S(1)} all-to-all(bf16[16,8,16,128]{3,2,1,0:T(8,128)(2,1)S(1)} %broadcast_in_dim.22), channel_id=1, replica_groups=mesh['x'=4,'far'=2,'core'=2,'tp'=32] {'x','far','core'}, dimensions={0} | all-to-all | bytes 1048576 | tf_op jit(solution)/shard_map/all_to_all | solution.py:25
  352.4 0.2 fusion.1
  352.7 0.2 fusion.2
  352.9 0.2 fusion.3
  353.2 0.2 fusion.4
  353.4 0.2 fusion.5
  353.7 0.2 fusion.6
  354.0 0.2 fusion.7
  354.2 0.5 copy-done
  354.8 0.6 bitcast_dynamic-update-slice_fusion
  (40 shorter events, 1.1 us)
Async XLA Ops:
  7.9 28.0 %all-to-all-start = ((bf16[32,16,128]{2,1,0:T(8,128)(2,1)}), bf16[32,16,128]{2,1,0:T(8,128)(2,1)S(1)}, u32[]{:S(2)}, u32[]{:S(2)}) async-start(bf16[32,16,128]{2,1,0:T(8,128)(2,1)} %broadcast_in_dim.8), calls=%async_computation | async-start | bytes 262144 | tf_op jit(solution)/shard_map/all_to_all | solution.py:25
  22.8 13.1 %collective-permute-start = (bf16[3,256,128]{2,1,0:T(8,128)(2,1)S(1)}, bf16[3,256,128]{2,1,0:T(8,128)(2,1)S(1)}, u32[]{:S(2)}, u32[]{:S(2)}) collective-permute-start(bf16[3,256,128]{2,1,0:T(8,128)(2,1)S(1)} %slice.78), channel_id=1, source_target_pairs={{0,64},{64,0},{1,65},{65,1},{2,66},{66,2},{3,67},{67,3},{4,68},{68... | collective-permute-start | bytes 589832 | tf_op jit(solution)/shard_map/ppermute | solution.py:29
  38.4 23.1 %all-to-all-start.1 = ((bf16[4,3,512,128]{3,2,1,0:T(8,128)(2,1)}), bf16[4,3,512,128]{3,2,1,0:T(8,128)(2,1)S(1)}, u32[]{:S(2)}, u32[]{:S(2)}) async-start(bf16[4,3,512,128]{3,2,1,0:T(8,128)(2,1)} %broadcast_in_dim.10), calls=%async_computation.1 | async-start | bytes 3145728 | tf_op jit(solution)/shard_map/all_to_all | solution.py:25
  42.7 84.1 %all-gather.2.cloned.1.call-start = ((), (), s32[]{:S(2)}) async-start(), calls=%async_computation.17 | async-start | bytes 5898240 | tf_op jit(solution)/shard_map/all_gather | solution.py:48
  42.7 13.2 %collective-permute-start.1 = (bf16[5,256,128]{2,1,0:T(8,128)(2,1)S(1)}, bf16[5,256,128]{2,1,0:T(8,128)(2,1)S(1)}, u32[]{:S(2)}, u32[]{:S(2)}) collective-permute-start(bf16[5,256,128]{2,1,0:T(8,128)(2,1)S(1)} %slice.79), channel_id=1, source_target_pairs={{0,64},{64,0},{1,65},{65,1},{2,66},{66,2},{3,67},{67,3},{4,68},{68... | collective-permute-start | bytes 983048 | tf_op jit(solution)/shard_map/ppermute | solution.py:29
  62.6 5.3 %collective-permute-start.2 = (bf16[4,3,512,128]{3,2,1,0:T(8,128)(2,1)S(1)}, bf16[4,3,512,128]{3,2,1,0:T(8,128)(2,1)S(1)}, u32[]{:S(2)}, u32[]{:S(2)}) collective-permute-start(bf16[4,3,512,128]{3,2,1,0:T(8,128)(2,1)S(1)} %all-to-all-done.1), channel_id=1, source_target_pairs={{0,32},{32,0},{1,33},{33,1},{2,34},{34,2},{3,35},{35,3},{4,36},{36... | collective-permute-start | bytes 4718600 | tf_op jit(solution)/shard_map/ppermute | solution.py:29
  129.1 14.4 %all-to-all-start.5 = ((bf16[32,16,128]{2,1,0:T(8,128)(2,1)}), bf16[32,16,128]{2,1,0:T(8,128)(2,1)S(1)}, u32[]{:S(2)}, u32[]{:S(2)}) async-start(bf16[32,16,128]{2,1,0:T(8,128)(2,1)} %get-tuple-element.73), calls=%async_computation.5 | async-start | bytes 262144 | tf_op jit(solution)/shard_map/all_to_all | solution.py:25
  145.7 14.4 %all-to-all-start.6 = ((bf16[32,16,128]{2,1,0:T(8,128)(2,1)}), bf16[32,16,128]{2,1,0:T(8,128)(2,1)S(1)}, u32[]{:S(2)}, u32[]{:S(2)}) async-start(bf16[32,16,128]{2,1,0:T(8,128)(2,1)} %get-tuple-element.75), calls=%async_computation.6 | async-start | bytes 262144 | tf_op jit(solution)/shard_map/all_to_all | solution.py:25
  162.3 14.4 %all-to-all-start.7 = ((bf16[32,16,128]{2,1,0:T(8,128)(2,1)}), bf16[32,16,128]{2,1,0:T(8,128)(2,1)S(1)}, u32[]{:S(2)}, u32[]{:S(2)}) async-start(bf16[32,16,128]{2,1,0:T(8,128)(2,1)} %get-tuple-element.77), calls=%async_computation.7 | async-start | bytes 262144 | tf_op jit(solution)/shard_map/all_to_all | solution.py:25
  178.9 14.4 %all-to-all-start.8 = ((bf16[32,16,128]{2,1,0:T(8,128)(2,1)}), bf16[32,16,128]{2,1,0:T(8,128)(2,1)S(1)}, u32[]{:S(2)}, u32[]{:S(2)}) async-start(bf16[32,16,128]{2,1,0:T(8,128)(2,1)} %get-tuple-element.79), calls=%async_computation.8 | async-start | bytes 262144 | tf_op jit(solution)/shard_map/all_to_all | solution.py:25
  183.9 19.1 %collective-permute-start.3 = (bf16[8,16,128]{2,1,0:T(8,128)(2,1)S(1)}, bf16[8,16,128]{2,1,0:T(8,128)(2,1)S(1)}, u32[]{:S(2)}, u32[]{:S(2)}) collective-permute-start(bf16[8,16,128]{2,1,0:T(8,128)(2,1)S(1)} %constant_dynamic-update-slice_fusion), channel_id=1, source_target_pairs={{0,0},{1,1},{2,32},{3,33},{4,64},{5,65},{6,96},{7,97},{8,128},{9,1... | collective-permute-start | bytes 98312 | tf_op jit(solution)/shard_map/ppermute | solution.py:187
  198.0 14.5 %all-to-all-start.9 = ((bf16[32,16,128]{2,1,0:T(8,128)(2,1)}), bf16[32,16,128]{2,1,0:T(8,128)(2,1)S(1)}, u32[]{:S(2)}, u32[]{:S(2)}) async-start(bf16[32,16,128]{2,1,0:T(8,128)(2,1)} %get-tuple-element.83), calls=%async_computation.9 | async-start | bytes 262144 | tf_op jit(solution)/shard_map/all_to_all | solution.py:25
  354.0 0.8 copy-start
Sparse Core Ops, SparseCore 0:
  62.7 43.3 all-gather.1

commit v3 on v1

v3 whole, which is shorter than its diff:
```python
import functools

import jax
import jax.numpy as jnp
from jax import lax
from jax.experimental import pallas as pl
from jax.experimental.pallas import tpu as pltpu
from jax.sharding import Mesh, PartitionSpec as P

EPSILON = 1e-05
F32 = jnp.float32
BF16 = jnp.bfloat16
TP = "tp"
SECTION = ("x", "far", "core")
ACROSS, FAR, CORES = 4, 2, 2
EARLY = 3


def spread(block, copies):
    return lax.optimization_barrier(jnp.broadcast_to(block[None], (copies,) + block.shape))


def exchanged(blocks, axis):
    return lax.all_to_all(blocks, axis, split_axis=0, concat_axis=0, tiled=True)


def swapped(block, axis):
    return lax.ppermute(block, axis, [(0, 1), (1, 0)])


def fetched_matrices(weights, own_x, members):
    sections, row_count, columns = weights.shape
    first = weights[:EARLY]
    crossed = swapped(first, "far")
    blocks = exchanged(spread(own_x, members), TP)
    crossed, blocks, last = lax.optimization_barrier((crossed, blocks, weights[EARLY:]))
    crossed_last = swapped(last, "far")
    pair = jnp.stack([first, crossed], axis=1).reshape(-1, columns)
    mine = exchanged(spread(pair, ACROSS), "x")
    crossed_last, mine = lax.optimization_barrier((crossed_last, mine))
    pair = jnp.stack([last, crossed_last], axis=1).reshape(-1, 2 * row_count, columns)
    late = lax.all_gather(pair, ("x", "core"), axis=1, tiled=True)
    return blocks, (close(mine), close(swapped(mine, "core"))), (close(late),)


def block_order(early, per):
    far, core = lax.axis_index("far"), lax.axis_index("core")
    order = []
    for x in range(ACROSS):
        for k in range(CORES):
            owner = lax.rem(core + k, CORES) if early else k
            for q in range(FAR):
                section = (x * FAR + lax.rem(far + q, FAR)) * CORES + owner
                order += [per * section + b for b in range(per)]
    return order


def rows_of(layer, sources, n, rows):
    if len(sources) == 2:
        return sources[n % CORES][n // CORES, pl.ds(layer * rows, rows)]
    return sources[0][layer - EARLY, pl.ds(n * rows, rows)]


def forward_kernel(layer, per, count_in, got, x, *refs):
    sources, (*sent, x_new, slope, scaled) = refs[:count_in], refs[count_in:]
    members, tokens, columns = got.shape
    features = members * columns
    squares = jnp.zeros(x.shape, F32)
    for m in range(members):
        squares += jnp.square(got[m].astype(F32))
    mean = jnp.sum(squares, axis=1, keepdims=True) / features
    inverse_rms = lax.rsqrt(mean + EPSILON)
    order = block_order(layer < EARLY, per)
    count = ACROSS * CORES
    rows, blocks = features // count, members // count
    product = jnp.zeros(x.shape, F32)
    for n in range(count):
        segment = jnp.concatenate([got[m] for m in order[n * blocks : (n + 1) * blocks]], axis=1)
        product += jnp.dot(
            segment, rows_of(layer, sources, n, rows), preferred_element_type=F32
        )
    activation = inverse_rms * product
    sigmoid = jax.nn.sigmoid(activation)
    result = (x[...].astype(F32) + activation * sigmoid).astype(BF16)
    x_new[...] = result
    for target in sent:
        target[...] = jnp.broadcast_to(result[None], target.shape)
    slope[...] = inverse_rms * sigmoid * (1.0 + activation * (1.0 - sigmoid))
    scaled[...] = product * (inverse_rms * inverse_rms / features)


def backward_kernel(layer, per, count_in, received, cotangent, slope, scaled, got, *refs):
    sources, (parts, h_out, cot_out) = refs[:count_in], refs[count_in:]
    members, tokens, columns = got.shape
    cot = cotangent[...]
    if len(received.shape) == 3:
        total = cot
        for m in range(members):
            total += received[m].astype(F32)
        cot = total.astype(BF16).astype(F32)
    cot_out[...] = cot
    h = (slope[...] * cot).astype(BF16)
    h_out[...] = h
    share = jnp.sum(h.astype(F32) * scaled[...], axis=1, keepdims=True)
    order = block_order(layer < EARLY, per)
    count = ACROSS * CORES
    rows, blocks = members * columns // count, members // count
    for n in range(count):
        back = lax.dot_general(
            h,
            rows_of(layer, sources, n, rows),
            (((1,), (1,)), ((), ())),
            preferred_element_type=F32,
        )
        for k in range(blocks):
            m = order[n * blocks + k]
            mine = back[:, k * columns : (k + 1) * columns] - share * got[m].astype(F32)
            parts[m] = mine.astype(BF16)


def last_kernel(per, received, cotangent, slope, *refs):
    *others, packed = refs
    sections = (len(others) + 1) // 2
    gots, later = others[:sections], others[sections:]
    tokens = slope.shape[0]
    total = cotangent[...]
    for m in range(received.shape[0]):
        total += received[m].astype(F32)
    h = (slope[...] * total.astype(BF16).astype(F32)).astype(BF16)
    for s, block in enumerate([h] + [other[...] for other in later]):
        for g in range(packed.shape[0]):
            at = s * (per + 1) * tokens
            for b in range(per):
                packed[g, pl.ds(at + b * tokens, tokens)] = gots[s][per * g + b]
            packed[g, pl.ds(at + per * tokens, tokens)] = block


def grads_kernel(per, tokens, arrived, out):
    groups, _, columns = arrived.shape
    for s in range(out.shape[0]):
        at = s * (per + 1) * tokens
        gathered = [
            jnp.concatenate(
                [arrived[g, pl.ds(at + b * tokens, tokens)] for g in range(groups)], axis=0
            )
            for b in range(per + 1)
        ]
        for b in range(per):
            total = lax.dot_general(
                gathered[b], gathered[per], (((0,), (0,)), ((), ())), preferred_element_type=F32
            )
            out[s, pl.ds(b * columns, columns)] = total.astype(BF16)


def local_call(kernel, outs, *inputs):
    vmem = pl.BlockSpec(memory_space=pltpu.VMEM)
    call = pl.pallas_call(
        kernel,
        out_shape=[jax.ShapeDtypeStruct(shape, dtype) for shape, dtype in outs],
        in_specs=[vmem] * len(inputs),
        out_specs=[vmem] * len(outs),
        compiler_params=pltpu.CompilerParams(vmem_limit_bytes=32 * 2**20),
    )
    return call(*inputs)


def close(array):
    return pltpu.with_memory_space_constraint(array, pltpu.VMEM)


def on_device(inputs, weights, targets):
    groups = lax.axis_size(SECTION)
    members = lax.axis_size(TP)
    group = lax.axis_index(SECTION)
    sections, row_count, columns = weights.shape
    micro_tokens = inputs.shape[2]
    all_tokens = inputs.shape[0] * inputs.shape[1] * micro_tokens
    tokens = all_tokens // groups
    per = members // groups
    block = (tokens, columns)
    own_x = lax.dynamic_slice_in_dim(inputs.reshape(all_tokens, columns), group * tokens, tokens, 0)
    own_target = lax.dynamic_slice_in_dim(
        targets.reshape(all_tokens, columns), group * tokens, tokens, 0
    )
    blocks, early, late = fetched_matrices(weights, own_x, members)

    kept = []
    x = own_x
    for s in range(sections):
        sources = early if s < EARLY else late
        outs = [((members,) + block, BF16)] if s < sections - 1 else []
        outs += [(block, BF16), (block, F32), (block, F32)]
        kernel = functools.partial(forward_kernel, s, per, len(sources))
        *sent, x, slope, scaled = local_call(kernel, outs, blocks, x, *sources)
        kept.append((blocks, slope, scaled))
        if sent:
            blocks = exchanged(sent[0], TP)

    cotangent = (x.astype(F32) - own_target.astype(F32)) / micro_tokens
    grads_h = []
    received = x
    for s in range(sections - 1, 0, -1):
        sources = early if s < EARLY else late
        blocks, slope, scaled = kept[s]
        outs = [((members,) + block, BF16), (block, BF16), (block, F32)]
        kernel = functools.partial(backward_kernel, s, per, len(sources))
        parts, h, cotangent = local_call(
            kernel, outs, received, cotangent, slope, scaled, blocks, *sources
        )
        grads_h.insert(0, h)
        received = exchanged(parts, TP)
    (packed,) = local_call(
        functools.partial(last_kernel, per),
        [((groups, sections * (per + 1) * tokens, columns), BF16)],
        received,
        cotangent,
        kept[0][1],
        *[entry[0] for entry in kept],
        *grads_h,
    )
    (result,) = local_call(
        functools.partial(grads_kernel, per, tokens),
        [(weights.shape, BF16)],
        exchanged(packed, SECTION),
    )
    return result


def solution(mesh):
    devices = mesh.devices.reshape(ACROSS, FAR, CORES, mesh.shape[TP])
    finer = Mesh(devices, SECTION + (TP,))
    matrix = P(None, SECTION, TP)
    placed = (P(None, None, None, TP), matrix, P(None, None, None, TP))
    return jax.shard_map(
        on_device, mesh=finer, in_specs=placed, out_specs=matrix, check_vma=False
    )
```

time: 411 us -> 334 us (0.81)
  waiting for transfers between devices: 107 us -> 24.1 us
  starting transfers between devices: 4.94 us -> 30.4 us
  matrix products: 16.2 us -> 0 us
  Pallas kernels: 0 us -> 6.93 us
    all_gather x1, waiting for transfers between devices: 97.3 us -> 0.01 us  [fetched_matrices(): late = lax.all_gather(pair, ('x', 'core'), axis=1, tiled=True)]
    ppermute x0 -> x3, waiting for transfers between devices: none -> 18.4 us  [swapped(): return lax.ppermute(block, axis, [(0, 1), (1, 0)])]
    dot_general x23 -> x0, matrix products: 16.2 us -> none  [the longest x8 11.6 us: on_device(): product = jnp.dot(full, matrices[s], preferred_element_type=F32)]
    all_to_all x1 -> x2, starting transfers between devices: 4.94 us -> 18.3 us  [exchanged(): return lax.all_to_all(blocks, axis, split_axis=0, concat_axis=0, tiled=True)]
    ppermute x0 -> x3, starting transfers between devices: none -> 12.2 us  [swapped(): return lax.ppermute(block, axis, [(0, 1), (1, 0)])]
    pallas_call x0 -> x17, Pallas kernels: none -> 6.93 us  [local_call(): return call(*inputs)]
    concatenate x1 -> x0, local copies, waits for them, and re-layouts: 6.75 us -> none  [on_device(): arrived = exchanged(jnp.concatenate(outgoing, axis=1), 'section')]
    all_to_all x1 -> x2, waiting for transfers between devices: 8.53 us -> 5.65 us  [exchanged(): return lax.all_to_all(blocks, axis, split_axis=0, concat_axis=0, tiled=True)]
  transfers between devices with their start and end apart: 2 -> 6, of which waited for: 2 -> 4; matrix products, arithmetic and copies ran while one was open for 0% -> 1% of each run, Pallas kernels for 0% -> 0%
where the time goes in v3:
time: 334 us; the launch traced here: 333 us
  blocking collectives  249 us (75%)
  starting transfers between devices  30.4 us (9%)
  waiting for transfers between devices  24.1 us (7%)
  between operations  13.5 us (4%)
  local copies, waits for them, and re-layouts  8.67 us (3%)
  Pallas kernels  6.93 us (2%)
    all_to_all x15, blocking collectives, exchanged(): return lax.all_to_all(blocks, axis, split_axis=0, concat_axis=0, tiled=True)  249 us
    ppermute x3, waiting for transfers between devices, swapped(): return lax.ppermute(block, axis, [(0, 1), (1, 0)])  18.4 us
    all_to_all x2, starting transfers between devices, exchanged(): return lax.all_to_all(blocks, axis, split_axis=0, concat_axis=0, tiled=True)  18.3 us
    ppermute x3, starting transfers between devices, swapped(): return lax.ppermute(block, axis, [(0, 1), (1, 0)])  12.2 us
    pallas_call x17, Pallas kernels, local_call(): return call(*inputs)  6.93 us
  transfers between devices with their start and end apart: 6, of which 4 were waited for; matrix products, arithmetic and copies ran while one was open for 1% of the time, Pallas kernels for 0%

profile of v3, /device:TPU:8, one launch (start us, length us, event | category | flops | bytes accessed | tf_op | source)
XLA Modules:
  0.0 333.5 jit_solution(5585651506144716475)
XLA Ops:
  6.5 0.0 copy-start
  6.5 0.8 copy-done
  7.4 0.7 broadcast_in_dim.6
  8.1 14.0 %all-to-all-start = ((bf16[32,16,128]{2,1,0:T(8,128)(2,1)}), bf16[32,16,128]{2,1,0:T(8,128)(2,1)S(1)}, u32[]{:S(2)}, u32[]{:S(2)}) async-start(bf16[32,16,128]{2,1,0:T(8,128)(2,1)} %broadcast_in_dim.6), calls=%async_computation | async-start | bytes 262144 | tf_op jit(solution)/shard_map/all_to_all | solution.py:24
  22.0 1.0 slice_bitcast_fusion
  23.0 5.0 %collective-permute-start = (bf16[3,256,128]{2,1,0:T(8,128)(2,1)S(1)}, bf16[3,256,128]{2,1,0:T(8,128)(2,1)S(1)}, u32[]{:S(2)}, u32[]{:S(2)}) collective-permute-start(bf16[3,256,128]{2,1,0:T(8,128)(2,1)S(1)} %get-tuple-element.118), channel_id=1, source_target_pairs={{0,64},{64,0},{1,65},{65,1},{2,66},{66,2},{3,67},{67,3},{4,68},{68... | collective-permute-start | bytes 589832 | tf_op jit(solution)/shard_map/ppermute | solution.py:28
  28.1 1.0 slice.7
  29.1 7.1 %collective-permute-done = bf16[3,256,128]{2,1,0:T(8,128)(2,1)S(1)} collective-permute-done((bf16[3,256,128]{2,1,0:T(8,128)(2,1)S(1)}, bf16[3,256,128]{2,1,0:T(8,128)(2,1)S(1)}, u32[]{:S(2)}, u32[]{:S(2)}) %collective-permute-start) | collective-permute-done | bytes 196640 | tf_op jit(solution)/shard_map/ppermute | solution.py:28
  36.1 0.0 all-to-all-done.got.refs_0_
  36.1 0.0 copy-start.5
  36.2 1.4 broadcast_in_dim.15
  37.6 4.3 %all-to-all-start.1 = ((bf16[4,1536,128]{2,1,0:T(8,128)(2,1)}), bf16[4,1536,128]{2,1,0:T(8,128)(2,1)S(1)}, u32[]{:S(2)}, u32[]{:S(2)}) async-start(bf16[4,1536,128]{2,1,0:T(8,128)(2,1)} %broadcast_in_dim.15), calls=%async_computation.1 | async-start | bytes 3145728 | tf_op jit(solution)/shard_map/all_to_all | solution.py:24
  41.9 0.0 all-gather.2.cloned.1.call-start
  41.9 5.2 %collective-permute-start.1 = (bf16[5,256,128]{2,1,0:T(8,128)(2,1)S(1)}, bf16[5,256,128]{2,1,0:T(8,128)(2,1)S(1)}, u32[]{:S(2)}, u32[]{:S(2)}) collective-permute-start(bf16[5,256,128]{2,1,0:T(8,128)(2,1)S(1)} %slice.7), channel_id=1, source_target_pairs={{0,64},{64,0},{1,65},{65,1},{2,66},{66,2},{3,67},{67,3},{4,68},{68... | collective-permute-start | bytes 983048 | tf_op jit(solution)/shard_map/ppermute | solution.py:28
  47.1 7.9 %collective-permute-done.1 = bf16[5,256,128]{2,1,0:T(8,128)(2,1)S(1)} collective-permute-done((bf16[5,256,128]{2,1,0:T(8,128)(2,1)S(1)}, bf16[5,256,128]{2,1,0:T(8,128)(2,1)S(1)}, u32[]{:S(2)}, u32[]{:S(2)}) %collective-permute-start.1) | collective-permute-done | bytes 327712 | tf_op jit(solution)/shard_map/ppermute | solution.py:28
  55.0 5.7 %all-to-all-done.1.refs_0_ = bf16[4,1536,128]{2,1,0:T(8,128)(2,1)S(1)} async-done(((bf16[4,1536,128]{2,1,0:T(8,128)(2,1)}), bf16[4,1536,128]{2,1,0:T(8,128)(2,1)S(1)}, u32[]{:S(2)}, u32[]{:S(2)}) %all-to-all-start.1) | async-done | bytes 1572896 | tf_op jit(solution)/shard_map/all_to_all | solution.py:24
  60.7 0.1 pad_maximum_fusion
  60.7 0.9 copy.6
  61.6 0.0 all-gather.2.cloned.1.call-update
  61.7 1.9 collective-permute-start.2
  63.6 3.4 %collective-permute-done.2.refs_1_ = bf16[4,1536,128]{2,1,0:T(8,128)(2,1)S(1)} collective-permute-done((bf16[4,1536,128]{2,1,0:T(8,128)(2,1)S(1)}, bf16[4,1536,128]{2,1,0:T(8,128)(2,1)S(1)}, u32[]{:S(2)}, u32[]{:S(2)}) %collective-permute-start.2) | collective-permute-done | bytes 1572896 | tf_op jit(solution)/shard_map/ppermute | solution.py:28
  67.0 0.0 copy-done.5
  67.0 0.9 shard_map.37
  67.8 23.6 %all_to_all.85.got.refs_1_ = bf16[32,16,128]{2,1,0:T(8,128)(2,1)S(1)} all-to-all(bf16[32,16,128]{2,1,0:T(8,128)(2,1)S(1)} %get-tuple-element.65), channel_id=1, replica_groups=mesh['x'=4,'far'=2,'core'=2,'tp'=32] {'tp'}, dimensions={0} | all-to-all | bytes 262144 | tf_op jit(solution)/shard_map/all_to_all | solution.py:24
  91.4 0.3 shard_map.38
  91.7 13.8 %all_to_all.86.got.refs_2_ = bf16[32,16,128]{2,1,0:T(8,128)(2,1)S(1)} all-to-all(bf16[32,16,128]{2,1,0:T(8,128)(2,1)S(1)} %get-tuple-element.67), channel_id=1, replica_groups=mesh['x'=4,'far'=2,'core'=2,'tp'=32] {'tp'}, dimensions={0} | all-to-all | bytes 262144 | tf_op jit(solution)/shard_map/all_to_all | solution.py:24
  105.5 0.0 copy-start.3
  105.5 0.3 shard_map.39
  105.8 0.4 copy-done.3
  106.1 13.6 %all_to_all.87.got.refs_3_ = bf16[32,16,128]{2,1,0:T(8,128)(2,1)S(1)} all-to-all(bf16[32,16,128]{2,1,0:T(8,128)(2,1)S(1)} %get-tuple-element.69), channel_id=1, replica_groups=mesh['x'=4,'far'=2,'core'=2,'tp'=32] {'tp'}, dimensions={0} | all-to-all | bytes 262144 | tf_op jit(solution)/shard_map/all_to_all | solution.py:24
  119.8 0.0 all-gather.2.cloned.1.call-done.refs_0_
  119.8 0.0 copy-start.1
  119.8 2.5 copy-done.1
  122.3 0.0 copy-start.2
  122.3 0.3 shard_map.40
  122.5 13.9 %all_to_all.88.got.refs_4_ = bf16[32,16,128]{2,1,0:T(8,128)(2,1)S(1)} all-to-all(bf16[32,16,128]{2,1,0:T(8,128)(2,1)S(1)} %get-tuple-element.72), channel_id=1, replica_groups=mesh['x'=4,'far'=2,'core'=2,'tp'=32] {'tp'}, dimensions={0} | all-to-all | bytes 262144 | tf_op jit(solution)/shard_map/all_to_all | solution.py:24
  136.4 0.0 copy-done.2
  136.4 0.3 shard_map.41
  136.7 13.6 %all_to_all.89.got.refs_5_ = bf16[32,16,128]{2,1,0:T(8,128)(2,1)S(1)} all-to-all(bf16[32,16,128]{2,1,0:T(8,128)(2,1)S(1)} %get-tuple-element.74), channel_id=1, replica_groups=mesh['x'=4,'far'=2,'core'=2,'tp'=32] {'tp'}, dimensions={0} | all-to-all | bytes 262144 | tf_op jit(solution)/shard_map/all_to_all | solution.py:24
  150.3 0.3 shard_map.42
  150.6 13.6 %all_to_all.90.got.refs_6_ = bf16[32,16,128]{2,1,0:T(8,128)(2,1)S(1)} all-to-all(bf16[32,16,128]{2,1,0:T(8,128)(2,1)S(1)} %get-tuple-element.76), channel_id=1, replica_groups=mesh['x'=4,'far'=2,'core'=2,'tp'=32] {'tp'}, dimensions={0} | all-to-all | bytes 262144 | tf_op jit(solution)/shard_map/all_to_all | solution.py:24
  164.2 0.3 shard_map.43
  164.5 13.6 %all_to_all.91.got.refs_7_ = bf16[32,16,128]{2,1,0:T(8,128)(2,1)S(1)} all-to-all(bf16[32,16,128]{2,1,0:T(8,128)(2,1)S(1)} %get-tuple-element.78), channel_id=1, replica_groups=mesh['x'=4,'far'=2,'core'=2,'tp'=32] {'tp'}, dimensions={0} | all-to-all | bytes 262144 | tf_op jit(solution)/shard_map/all_to_all | solution.py:24
  178.1 0.3 shard_map.44
  178.3 0.7 subtract_multiply_fusion.cotangent
  179.0 0.4 shard_map.45
  179.4 13.6 %all_to_all.92.received = bf16[32,16,128]{2,1,0:T(8,128)(2,1)S(1)} all-to-all(bf16[32,16,128]{2,1,0:T(8,128)(2,1)S(1)} %get-tuple-element.83), channel_id=1, replica_groups=mesh['x'=4,'far'=2,'core'=2,'tp'=32] {'tp'}, dimensions={0} | all-to-all | bytes 262144 | tf_op jit(solution)/shard_map/all_to_all | solution.py:24
  193.0 0.4 shard_map.46
  193.4 13.6 %all_to_all.93.received = bf16[32,16,128]{2,1,0:T(8,128)(2,1)S(1)} all-to-all(bf16[32,16,128]{2,1,0:T(8,128)(2,1)S(1)} %get-tuple-element.87), channel_id=1, replica_groups=mesh['x'=4,'far'=2,'core'=2,'tp'=32] {'tp'}, dimensions={0} | all-to-all | bytes 262144 | tf_op jit(solution)/shard_map/all_to_all | solution.py:24
  207.0 0.4 shard_map.47
  207.4 13.6 %all_to_all.94.received = bf16[32,16,128]{2,1,0:T(8,128)(2,1)S(1)} all-to-all(bf16[32,16,128]{2,1,0:T(8,128)(2,1)S(1)} %get-tuple-element.91), channel_id=1, replica_groups=mesh['x'=4,'far'=2,'core'=2,'tp'=32] {'tp'}, dimensions={0} | all-to-all | bytes 262144 | tf_op jit(solution)/shard_map/all_to_all | solution.py:24
  221.0 0.4 shard_map.48
  221.4 13.6 %all_to_all.95.received = bf16[32,16,128]{2,1,0:T(8,128)(2,1)S(1)} all-to-all(bf16[32,16,128]{2,1,0:T(8,128)(2,1)S(1)} %get-tuple-element.95), channel_id=1, replica_groups=mesh['x'=4,'far'=2,'core'=2,'tp'=32] {'tp'}, dimensions={0} | all-to-all | bytes 262144 | tf_op jit(solution)/shard_map/all_to_all | solution.py:24
  235.0 0.4 shard_map.49
  235.4 13.6 %all_to_all.96.received = bf16[32,16,128]{2,1,0:T(8,128)(2,1)S(1)} all-to-all(bf16[32,16,128]{2,1,0:T(8,128)(2,1)S(1)} %get-tuple-element.99), channel_id=1, replica_groups=mesh['x'=4,'far'=2,'core'=2,'tp'=32] {'tp'}, dimensions={0} | all-to-all | bytes 262144 | tf_op jit(solution)/shard_map/all_to_all | solution.py:24
  249.0 0.0 copy-done.4
  249.0 0.4 shard_map.50
  249.4 13.6 %all_to_all.97.received = bf16[32,16,128]{2,1,0:T(8,128)(2,1)S(1)} all-to-all(bf16[32,16,128]{2,1,0:T(8,128)(2,1)S(1)} %get-tuple-element.103), channel_id=1, replica_groups=mesh['x'=4,'far'=2,'core'=2,'tp'=32] {'tp'}, dimensions={0} | all-to-all | bytes 262144 | tf_op jit(solution)/shard_map/all_to_all | solution.py:24
  263.0 0.4 shard_map.51
  263.4 13.6 %all_to_all.98.received = bf16[32,16,128]{2,1,0:T(8,128)(2,1)S(1)} all-to-all(bf16[32,16,128]{2,1,0:T(8,128)(2,1)S(1)} %get-tuple-element.107), channel_id=1, replica_groups=mesh['x'=4,'far'=2,'core'=2,'tp'=32] {'tp'}, dimensions={0} | all-to-all | bytes 262144 | tf_op jit(solution)/shard_map/all_to_all | solution.py:24
  277.0 0.0 copy-done.6
  277.1 0.2 shard_map.52
  277.2 48.1 %all_to_all.99.arrived = bf16[16,384,128]{2,1,0:T(8,128)(2,1)S(1)} all-to-all(bf16[16,384,128]{2,1,0:T(8,128)(2,1)S(1)} %shard_map.52), channel_id=1, replica_groups=mesh['x'=4,'far'=2,'core'=2,'tp'=32] {'x','far','core'}, dimensions={0} | all-to-all | bytes 3145728 | tf_op jit(solution)/shard_map/all_to_all | solution.py:24
  325.3 1.3 shard_map.53
  (4 shorter events, 0.0 us)
Async XLA Ops:
  6.5 0.8 copy-start
  8.1 28.1 %all-to-all-start = ((bf16[32,16,128]{2,1,0:T(8,128)(2,1)}), bf16[32,16,128]{2,1,0:T(8,128)(2,1)S(1)}, u32[]{:S(2)}, u32[]{:S(2)}) async-start(bf16[32,16,128]{2,1,0:T(8,128)(2,1)} %broadcast_in_dim.6), calls=%async_computation | async-start | bytes 262144 | tf_op jit(solution)/shard_map/all_to_all | solution.py:24
  23.0 13.1 %collective-permute-start = (bf16[3,256,128]{2,1,0:T(8,128)(2,1)S(1)}, bf16[3,256,128]{2,1,0:T(8,128)(2,1)S(1)}, u32[]{:S(2)}, u32[]{:S(2)}) collective-permute-start(bf16[3,256,128]{2,1,0:T(8,128)(2,1)S(1)} %get-tuple-element.118), channel_id=1, source_target_pairs={{0,64},{64,0},{1,65},{65,1},{2,66},{66,2},{3,67},{67,3},{4,68},{68... | collective-permute-start | bytes 589832 | tf_op jit(solution)/shard_map/ppermute | solution.py:28
  36.1 30.8 %copy-start.5 = (bf16[32,16,128]{2,1,0:T(8,128)(2,1)}, bf16[32,16,128]{2,1,0:T(8,128)(2,1)S(1)}, u32[]{:S(2)}) copy-start(bf16[32,16,128]{2,1,0:T(8,128)(2,1)S(1)} %all-to-all-done.got.refs_0_) | copy-start | bytes 393220
  37.6 23.1 %all-to-all-start.1 = ((bf16[4,1536,128]{2,1,0:T(8,128)(2,1)}), bf16[4,1536,128]{2,1,0:T(8,128)(2,1)S(1)}, u32[]{:S(2)}, u32[]{:S(2)}) async-start(bf16[4,1536,128]{2,1,0:T(8,128)(2,1)} %broadcast_in_dim.15), calls=%async_computation.1 | async-start | bytes 3145728 | tf_op jit(solution)/shard_map/all_to_all | solution.py:24
  41.9 77.9 %all-gather.2.cloned.1.call-start = ((), (), s32[]{:S(2)}) async-start(), calls=%async_computation.17 | async-start | bytes 5898240 | tf_op jit(solution)/shard_map/all_gather | solution.py:42
  41.9 13.2 %collective-permute-start.1 = (bf16[5,256,128]{2,1,0:T(8,128)(2,1)S(1)}, bf16[5,256,128]{2,1,0:T(8,128)(2,1)S(1)}, u32[]{:S(2)}, u32[]{:S(2)}) collective-permute-start(bf16[5,256,128]{2,1,0:T(8,128)(2,1)S(1)} %slice.7), channel_id=1, source_target_pairs={{0,64},{64,0},{1,65},{65,1},{2,66},{66,2},{3,67},{67,3},{4,68},{68... | collective-permute-start | bytes 983048 | tf_op jit(solution)/shard_map/ppermute | solution.py:28
  61.7 5.3 %collective-permute-start.2 = (bf16[4,1536,128]{2,1,0:T(8,128)(2,1)S(1)}, bf16[4,1536,128]{2,1,0:T(8,128)(2,1)S(1)}, u32[]{:S(2)}, u32[]{:S(2)}) collective-permute-start(bf16[4,1536,128]{2,1,0:T(8,128)(2,1)S(1)} %all-to-all-done.1.refs_0_), channel_id=1, source_target_pairs={{0,32},{32,0},{1,33},{33,1},{2,34},{34,2},{3,35},{35,3},{4,36},{36... | collective-permute-start | bytes 4718600 | tf_op jit(solution)/shard_map/ppermute | solution.py:28
  105.5 0.7 copy-start.3
  119.8 2.5 copy-start.1
  122.3 14.2 %copy-start.2 = (bf16[5,4096,128]{2,1,0:T(8,128)(2,1)S(1)}, bf16[5,4096,128]{2,1,0:T(8,128)(2,1)}, u32[]{:S(2)}) copy-start(bf16[5,4096,128]{2,1,0:T(8,128)(2,1)} %all-gather.2.cloned.1.call-done.refs_0_) | copy-start | bytes 15728644
  235.0 14.0 %copy-start.4 = (bf16[32,16,128]{2,1,0:T(8,128)(2,1)S(1)}, bf16[32,16,128]{2,1,0:T(8,128)(2,1)}, u32[]{:S(2)}) copy-start(bf16[32,16,128]{2,1,0:T(8,128)(2,1)} %copy-done.3) | copy-start | bytes 393220
  263.0 14.0 %copy-start.6 = (bf16[32,16,128]{2,1,0:T(8,128)(2,1)S(1)}, bf16[32,16,128]{2,1,0:T(8,128)(2,1)}, u32[]{:S(2)}) copy-start(bf16[32,16,128]{2,1,0:T(8,128)(2,1)} %copy-done.5) | copy-start | bytes 393220
Sparse Core Ops, SparseCore 0:
  61.8 43.3 all-gather.1

commit v4 on v3

--- a/solution.py
+++ b/solution.py
@@ -28,41 +28,38 @@
     return lax.ppermute(block, axis, [(0, 1), (1, 0)])
 
 
+def gathered(shard, crossed):
+    pair = jnp.concatenate([shard, crossed], axis=1)
+    return pair, functools.partial(lax.all_gather, axis_name=("x", "core"), axis=1, tiled=True)
+
+
 def fetched_matrices(weights, own_x, members):
-    sections, row_count, columns = weights.shape
     first = weights[:EARLY]
     crossed = swapped(first, "far")
+    pair, gather = gathered(first, crossed)
+    pair, own_x, last = lax.optimization_barrier((pair, own_x, weights[EARLY:]))
+    early = gather(pair)
+    crossed_last = swapped(last, "far")
     blocks = exchanged(spread(own_x, members), TP)
-    crossed, blocks, last = lax.optimization_barrier((crossed, blocks, weights[EARLY:]))
-    crossed_last = swapped(last, "far")
-    pair = jnp.stack([first, crossed], axis=1).reshape(-1, columns)
-    mine = exchanged(spread(pair, ACROSS), "x")
-    crossed_last, mine = lax.optimization_barrier((crossed_last, mine))
-    pair = jnp.stack([last, crossed_last], axis=1).reshape(-1, 2 * row_count, columns)
-    late = lax.all_gather(pair, ("x", "core"), axis=1, tiled=True)
-    return blocks, (close(mine), close(swapped(mine, "core"))), (close(late),)
-
-
-def block_order(early, per):
-    far, core = lax.axis_index("far"), lax.axis_index("core")
+    pair, gather = gathered(last, crossed_last)
+    pair, blocks = lax.optimization_barrier((pair, blocks))
+    late = gather(pair)
+    return blocks, close(early), close(late)
+
+
+def block_order(per):
+    far = lax.axis_index("far")
     order = []
     for x in range(ACROSS):
-        for k in range(CORES):
-            owner = lax.rem(core + k, CORES) if early else k
+        for core in range(CORES):
             for q in range(FAR):
-                section = (x * FAR + lax.rem(far + q, FAR)) * CORES + owner
+                section = (x * FAR + lax.rem(far + q, FAR)) * CORES + core
                 order += [per * section + b for b in range(per)]
     return order
 
 
-def rows_of(layer, sources, n, rows):
-    if len(sources) == 2:
-        return sources[n % CORES][n // CORES, pl.ds(layer * rows, rows)]
-    return sources[0][layer - EARLY, pl.ds(n * rows, rows)]
-
-
-def forward_kernel(layer, per, count_in, got, x, *refs):
-    sources, (*sent, x_new, slope, scaled) = refs[:count_in], refs[count_in:]
+def forward_kernel(layer, per, got, x, matrices, *outs):
+    *sent, x_new, slope, scaled = outs
     members, tokens, columns = got.shape
     features = members * columns
     squares = jnp.zeros(x.shape, F32)
@@ -70,14 +67,14 @@
         squares += jnp.square(got[m].astype(F32))
     mean = jnp.sum(squares, axis=1, keepdims=True) / features
     inverse_rms = lax.rsqrt(mean + EPSILON)
-    order = block_order(layer < EARLY, per)
+    order = block_order(per)
     count = ACROSS * CORES
     rows, blocks = features // count, members // count
     product = jnp.zeros(x.shape, F32)
     for n in range(count):
         segment = jnp.concatenate([got[m] for m in order[n * blocks : (n + 1) * blocks]], axis=1)
         product += jnp.dot(
-            segment, rows_of(layer, sources, n, rows), preferred_element_type=F32
+            segment, matrices[layer, pl.ds(n * rows, rows)], preferred_element_type=F32
         )
     activation = inverse_rms * product
     sigmoid = jax.nn.sigmoid(activation)
@@ -89,12 +86,13 @@
     scaled[...] = product * (inverse_rms * inverse_rms / features)
 
 
-def backward_kernel(layer, per, count_in, received, cotangent, slope, scaled, got, *refs):
-    sources, (parts, h_out, cot_out) = refs[:count_in], refs[count_in:]
+def backward_kernel(layer, per, micro_tokens, received, cotangent, slope, scaled, got, matrices, *outs):
+    parts, h_out, cot_out = outs
     members, tokens, columns = got.shape
-    cot = cotangent[...]
-    if len(received.shape) == 3:
-        total = cot
+    if len(received.shape) == 2:
+        cot = (received[...].astype(F32) - cotangent[...].astype(F32)) / micro_tokens
+    else:
+        total = cotangent[...]
         for m in range(members):
             total += received[m].astype(F32)
         cot = total.astype(BF16).astype(F32)
@@ -102,13 +100,13 @@
     h = (slope[...] * cot).astype(BF16)
     h_out[...] = h
     share = jnp.sum(h.astype(F32) * scaled[...], axis=1, keepdims=True)
-    order = block_order(layer < EARLY, per)
+    order = block_order(per)
     count = ACROSS * CORES
     rows, blocks = members * columns // count, members // count
     for n in range(count):
         back = lax.dot_general(
             h,
-            rows_of(layer, sources, n, rows),
+            matrices[layer, pl.ds(n * rows, rows)],
             (((1,), (1,)), ((), ())),
             preferred_element_type=F32,
         )
@@ -187,25 +185,24 @@
     kept = []
     x = own_x
     for s in range(sections):
-        sources = early if s < EARLY else late
+        matrices, at = (early, s) if s < EARLY else (late, s - EARLY)
         outs = [((members,) + block, BF16)] if s < sections - 1 else []
         outs += [(block, BF16), (block, F32), (block, F32)]
-        kernel = functools.partial(forward_kernel, s, per, len(sources))
-        *sent, x, slope, scaled = local_call(kernel, outs, blocks, x, *sources)
+        kernel = functools.partial(forward_kernel, at, per)
+        *sent, x, slope, scaled = local_call(kernel, outs, blocks, x, matrices)
         kept.append((blocks, slope, scaled))
         if sent:
             blocks = exchanged(sent[0], TP)
 
-    cotangent = (x.astype(F32) - own_target.astype(F32)) / micro_tokens
     grads_h = []
-    received = x
+    received, cotangent = x, own_target
     for s in range(sections - 1, 0, -1):
-        sources = early if s < EARLY else late
+        matrices, at = (early, s) if s < EARLY else (late, s - EARLY)
         blocks, slope, scaled = kept[s]
         outs = [((members,) + block, BF16), (block, BF16), (block, F32)]
-        kernel = functools.partial(backward_kernel, s, per, len(sources))
+        kernel = functools.partial(backward_kernel, at, per, micro_tokens)
         parts, h, cotangent = local_call(
-            kernel, outs, received, cotangent, slope, scaled, blocks, *sources
+            kernel, outs, received, cotangent, slope, scaled, blocks, matrices
         )
         grads_h.insert(0, h)
         received = exchanged(parts, TP)

time: 334 us -> 337 us (level)
  blocking collectives: 249 us -> 232 us
  waiting for transfers between devices: 24.1 us -> 33.2 us
  local copies, waits for them, and re-layouts: 8.67 us -> 13.6 us
    all_to_all x15 -> x14, blocking collectives: 249 us -> 232 us  [exchanged(): return lax.all_to_all(blocks, axis, split_axis=0, concat_axis=0, tiled=True)]
    all_to_all x2, waiting for transfers between devices: 5.65 us -> 19 us  [exchanged(): return lax.all_to_all(blocks, axis, split_axis=0, concat_axis=0, tiled=True)]
    ppermute x3 -> x2, waiting for transfers between devices: 18.4 us -> 7.56 us  [swapped(): return lax.ppermute(block, axis, [(0, 1), (1, 0)])]
    all_gather x1 -> x2, waiting for transfers between devices: 0.01 us -> 6.53 us  [the longest x1 6.53 us: fetched_matrices(): early = gather(pair)]
    unnamed x14 -> x54, local copies, waits for them, and re-layouts: 3.72 us -> 10.2 us
    ppermute x3 -> x2, starting transfers between devices: 12.2 us -> 13.8 us  [swapped(): return lax.ppermute(block, axis, [(0, 1), (1, 0)])]
  transfers between devices with their start and end apart: 6 -> 6, of which waited for: 4 -> 5; matrix products, arithmetic and copies ran while one was open for 1% -> 1% of each run, Pallas kernels for 0% -> 0%
where the time goes in v4:
time: 337 us; the launch traced here: 336 us
  blocking collectives  232 us (69%)
  waiting for transfers between devices  33.2 us (10%)
  starting transfers between devices  33 us (10%)
  local copies, waits for them, and re-layouts  13.6 us (4%)
  between operations  13.6 us (4%)
  Pallas kernels  9.7 us (3%)
    all_to_all x14, blocking collectives, exchanged(): return lax.all_to_all(blocks, axis, split_axis=0, concat_axis=0, tiled=True)  232 us
    all_to_all x2, starting transfers between devices, exchanged(): return lax.all_to_all(blocks, axis, split_axis=0, concat_axis=0, tiled=True)  19.1 us
    all_to_all x2, waiting for transfers between devices, exchanged(): return lax.all_to_all(blocks, axis, split_axis=0, concat_axis=0, tiled=True)  19 us
    ppermute x2, starting transfers between devices, swapped(): return lax.ppermute(block, axis, [(0, 1), (1, 0)])  13.8 us
    unnamed x54, local copies, waits for them, and re-layouts  10.2 us
    pallas_call x17, Pallas kernels, local_call(): return call(*inputs)  9.7 us
    ppermute x2, waiting for transfers between devices, swapped(): return lax.ppermute(block, axis, [(0, 1), (1, 0)])  7.56 us
  transfers between devices with their start and end apart: 6, of which 5 were waited for; matrix products, arithmetic and copies ran while one was open for 1% of the time, Pallas kernels for 0%

profile of v4, /device:TPU:8, one launch (start us, length us, event | category | flops | bytes accessed | tf_op | source)
XLA Modules:
  0.0 336.4 jit_solution(11527516157326063386)
XLA Ops:
  6.5 0.0 all-gather.3.cloned.1.call-start
  6.5 1.0 slice.6
  7.5 6.8 %collective-permute-start = (bf16[3,256,128]{2,1,0:T(8,128)(2,1)S(1)}, bf16[3,256,128]{2,1,0:T(8,128)(2,1)S(1)}, u32[]{:S(2)}, u32[]{:S(2)}) collective-permute-start(bf16[3,256,128]{2,1,0:T(8,128)(2,1)S(1)} %slice.6), channel_id=1, source_target_pairs={{0,64},{64,0},{1,65},{65,1},{2,66},{66,2},{3,67},{67,3},{4,68},{68... | collective-permute-start | bytes 589832 | tf_op jit(solution)/shard_map/ppermute | solution.py:28
  14.4 1.0 slice.7
  15.4 7.3 %collective-permute-done = bf16[3,256,128]{2,1,0:T(8,128)(2,1)S(1)} collective-permute-done((bf16[3,256,128]{2,1,0:T(8,128)(2,1)S(1)}, bf16[3,256,128]{2,1,0:T(8,128)(2,1)S(1)}, u32[]{:S(2)}, u32[]{:S(2)}) %collective-permute-start) | collective-permute-done | bytes 196640 | tf_op jit(solution)/shard_map/ppermute | solution.py:28
  22.7 0.8 pad_maximum_fusion.1
  23.4 0.0 all-gather.3.cloned.1.call-update
  23.5 7.0 %collective-permute-start.1 = (bf16[5,256,128]{2,1,0:T(8,128)(2,1)S(1)}, bf16[5,256,128]{2,1,0:T(8,128)(2,1)S(1)}, u32[]{:S(2)}, u32[]{:S(2)}) collective-permute-start(bf16[5,256,128]{2,1,0:T(8,128)(2,1)S(1)} %slice.7), channel_id=1, source_target_pairs={{0,64},{64,0},{1,65},{65,1},{2,66},{66,2},{3,67},{67,3},{4,68},{68... | collective-permute-start | bytes 983048 | tf_op jit(solution)/shard_map/ppermute | solution.py:28
  30.5 0.7 broadcast_in_dim.2
  31.2 13.5 %all-to-all-start = ((bf16[32,16,128]{2,1,0:T(8,128)(2,1)}), bf16[32,16,128]{2,1,0:T(8,128)(2,1)S(1)}, u32[]{:S(2)}, u32[]{:S(2)}) async-start(bf16[32,16,128]{2,1,0:T(8,128)(2,1)} %broadcast_in_dim.2), calls=%async_computation | async-start | bytes 262144 | tf_op jit(solution)/shard_map/all_to_all | solution.py:24
  44.7 0.0 all-gather.5.cloned.1.call-start
  44.8 0.3 collective-permute-done.1
  45.0 0.9 pad_maximum_fusion
  45.9 10.3 %all-to-all-done.got.refs_0_ = bf16[32,16,128]{2,1,0:T(8,128)(2,1)S(1)} async-done(((bf16[32,16,128]{2,1,0:T(8,128)(2,1)}), bf16[32,16,128]{2,1,0:T(8,128)(2,1)S(1)}, u32[]{:S(2)}, u32[]{:S(2)}) %all-to-all-start) | async-done | bytes 131104 | tf_op jit(solution)/shard_map/all_to_all | solution.py:24
  56.2 0.0 all-gather.5.cloned.1.call-update
  56.2 6.5 %all-gather.3.cloned.1.call-done.matrices = bf16[3,4096,128]{2,1,0:T(8,128)(2,1)} async-done(((bf16[3,512,128]{2,1,0:T(8,128)(2,1)}), bf16[3,4096,128]{2,1,0:T(8,128)(2,1)}) %all-gather.3.cloned.1.call-update) | async-done | bytes 3145744 | tf_op jit(solution)/shard_map/all_gather | solution.py:41
  62.7 1.9 copy-done.4
  64.6 0.9 shard_map.37
  65.5 0.0 copy-done.14
  65.5 20.2 %all_to_all.80.got.refs_1_ = bf16[32,16,128]{2,1,0:T(8,128)(2,1)S(1)} all-to-all(bf16[32,16,128]{2,1,0:T(8,128)(2,1)S(1)} %get-tuple-element.65), channel_id=1, replica_groups=mesh['x'=4,'far'=2,'core'=2,'tp'=32] {'tp'}, dimensions={0} | all-to-all | bytes 262144 | tf_op jit(solution)/shard_map/all_to_all | solution.py:24
  85.7 0.0 copy-done.5
  85.7 0.3 shard_map.38
  86.0 0.4 copy-done.10
  86.3 13.8 %all_to_all.81.got.refs_2_ = bf16[32,16,128]{2,1,0:T(8,128)(2,1)S(1)} all-to-all(bf16[32,16,128]{2,1,0:T(8,128)(2,1)S(1)} %get-tuple-element.67), channel_id=1, replica_groups=mesh['x'=4,'far'=2,'core'=2,'tp'=32] {'tp'}, dimensions={0} | all-to-all | bytes 262144 | tf_op jit(solution)/shard_map/all_to_all | solution.py:24
  100.2 0.3 shard_map.39
  100.5 0.4 copy-done.12
  100.8 13.6 %all_to_all.82.got.refs_3_ = bf16[32,16,128]{2,1,0:T(8,128)(2,1)S(1)} all-to-all(bf16[32,16,128]{2,1,0:T(8,128)(2,1)S(1)} %get-tuple-element.69), channel_id=1, replica_groups=mesh['x'=4,'far'=2,'core'=2,'tp'=32] {'tp'}, dimensions={0} | all-to-all | bytes 262144 | tf_op jit(solution)/shard_map/all_to_all | solution.py:24
  114.4 2.5 copy-done.1
  116.9 0.3 shard_map.40
  117.2 13.9 %all_to_all.83.got.refs_4_ = bf16[32,16,128]{2,1,0:T(8,128)(2,1)S(1)} all-to-all(bf16[32,16,128]{2,1,0:T(8,128)(2,1)S(1)} %get-tuple-element.72), channel_id=1, replica_groups=mesh['x'=4,'far'=2,'core'=2,'tp'=32] {'tp'}, dimensions={0} | all-to-all | bytes 262144 | tf_op jit(solution)/shard_map/all_to_all | solution.py:24
  131.1 0.3 shard_map.41
  131.4 13.6 %all_to_all.84.got.refs_5_ = bf16[32,16,128]{2,1,0:T(8,128)(2,1)S(1)} all-to-all(bf16[32,16,128]{2,1,0:T(8,128)(2,1)S(1)} %get-tuple-element.74), channel_id=1, replica_groups=mesh['x'=4,'far'=2,'core'=2,'tp'=32] {'tp'}, dimensions={0} | all-to-all | bytes 262144 | tf_op jit(solution)/shard_map/all_to_all | solution.py:24
  145.0 0.3 shard_map.42
  145.2 0.4 copy-done.6
  145.6 13.6 %all_to_all.85.got.refs_6_ = bf16[32,16,128]{2,1,0:T(8,128)(2,1)S(1)} all-to-all(bf16[32,16,128]{2,1,0:T(8,128)(2,1)S(1)} %get-tuple-element.76), channel_id=1, replica_groups=mesh['x'=4,'far'=2,'core'=2,'tp'=32] {'tp'}, dimensions={0} | all-to-all | bytes 262144 | tf_op jit(solution)/shard_map/all_to_all | solution.py:24
  159.2 0.3 shard_map.43
  159.5 0.4 copy-done.8
  159.9 0.7 copy-done.16
  160.5 0.6 copy-done.21
  161.1 0.6 copy-done.23
  161.7 5.6 %all-to-all-start.7 = ((bf16[32,16,128]{2,1,0:T(8,128)(2,1)}), bf16[32,16,128]{2,1,0:T(8,128)(2,1)}, u32[]{:S(2)}, u32[]{:S(2)}) async-start(bf16[32,16,128]{2,1,0:T(8,128)(2,1)} %copy-done.16), calls=%async_computation.7 | async-start | bytes 262144 | tf_op jit(solution)/shard_map/all_to_all | solution.py:24
  167.3 0.7 constant_dynamic-slice_fusion.cotangent
  168.0 8.8 %all-to-all-done.7.got.refs_7_ = bf16[32,16,128]{2,1,0:T(8,128)(2,1)} async-done(((bf16[32,16,128]{2,1,0:T(8,128)(2,1)}), bf16[32,16,128]{2,1,0:T(8,128)(2,1)}, u32[]{:S(2)}, u32[]{:S(2)}) %all-to-all-start.7) | async-done | bytes 131104 | tf_op jit(solution)/shard_map/all_to_all | solution.py:24
  176.8 2.5 copy-done.3
  179.2 1.2 shard_map.44
  180.4 1.3 shard_map.45
  181.8 13.5 %all_to_all.86.received = bf16[32,16,128]{2,1,0:T(8,128)(2,1)S(1)} all-to-all(bf16[32,16,128]{2,1,0:T(8,128)(2,1)S(1)} %get-tuple-element.83), channel_id=1, replica_groups=mesh['x'=4,'far'=2,'core'=2,'tp'=32] {'tp'}, dimensions={0} | all-to-all | bytes 262144 | tf_op jit(solution)/shard_map/all_to_all | solution.py:24
  195.4 0.0 slice-start
  195.4 0.4 shard_map.46
  195.8 13.8 %all_to_all.87.received = bf16[32,16,128]{2,1,0:T(8,128)(2,1)S(1)} all-to-all(bf16[32,16,128]{2,1,0:T(8,128)(2,1)S(1)} %get-tuple-element.87), channel_id=1, replica_groups=mesh['x'=4,'far'=2,'core'=2,'tp'=32] {'tp'}, dimensions={0} | all-to-all | bytes 262144 | tf_op jit(solution)/shard_map/all_to_all | solution.py:24
  209.6 0.0 slice-start.1
  209.6 0.4 shard_map.47
  210.0 13.5 %all_to_all.88.received = bf16[32,16,128]{2,1,0:T(8,128)(2,1)S(1)} all-to-all(bf16[32,16,128]{2,1,0:T(8,128)(2,1)S(1)} %get-tuple-element.91), channel_id=1, replica_groups=mesh['x'=4,'far'=2,'core'=2,'tp'=32] {'tp'}, dimensions={0} | all-to-all | bytes 262144 | tf_op jit(solution)/shard_map/all_to_all | solution.py:24
  223.5 0.4 shard_map.48
  223.9 13.5 %all_to_all.89.received = bf16[32,16,128]{2,1,0:T(8,128)(2,1)S(1)} all-to-all(bf16[32,16,128]{2,1,0:T(8,128)(2,1)S(1)} %get-tuple-element.95), channel_id=1, replica_groups=mesh['x'=4,'far'=2,'core'=2,'tp'=32] {'tp'}, dimensions={0} | all-to-all | bytes 262144 | tf_op jit(solution)/shard_map/all_to_all | solution.py:24
  237.4 0.4 shard_map.49
  237.8 13.5 %all_to_all.90.received = bf16[32,16,128]{2,1,0:T(8,128)(2,1)S(1)} all-to-all(bf16[32,16,128]{2,1,0:T(8,128)(2,1)S(1)} %get-tuple-element.99), channel_id=1, replica_groups=mesh['x'=4,'far'=2,'core'=2,'tp'=32] {'tp'}, dimensions={0} | all-to-all | bytes 262144 | tf_op jit(solution)/shard_map/all_to_all | solution.py:24
  251.3 0.4 shard_map.50
  251.7 13.5 %all_to_all.91.received = bf16[32,16,128]{2,1,0:T(8,128)(2,1)S(1)} all-to-all(bf16[32,16,128]{2,1,0:T(8,128)(2,1)S(1)} %get-tuple-element.103), channel_id=1, replica_groups=mesh['x'=4,'far'=2,'core'=2,'tp'=32] {'tp'}, dimensions={0} | all-to-all | bytes 262144 | tf_op jit(solution)/shard_map/all_to_all | solution.py:24
  265.2 0.4 shard_map.51
  265.6 13.6 %all_to_all.92.received = bf16[32,16,128]{2,1,0:T(8,128)(2,1)S(1)} all-to-all(bf16[32,16,128]{2,1,0:T(8,128)(2,1)S(1)} %get-tuple-element.107), channel_id=1, replica_groups=mesh['x'=4,'far'=2,'core'=2,'tp'=32] {'tp'}, dimensions={0} | all-to-all | bytes 262144 | tf_op jit(solution)/shard_map/all_to_all | solution.py:24
  279.2 1.1 shard_map.52
  280.2 48.0 %all_to_all.93.arrived = bf16[16,384,128]{2,1,0:T(8,128)(2,1)S(1)} all-to-all(bf16[16,384,128]{2,1,0:T(8,128)(2,1)S(1)} %shard_map.52), channel_id=1, replica_groups=mesh['x'=4,'far'=2,'core'=2,'tp'=32] {'x','far','core'}, dimensions={0} | all-to-all | bytes 3145728 | tf_op jit(solution)/shard_map/all_to_all | solution.py:24
  328.2 1.3 shard_map.53
  (43 shorter events, 0.1 us)
Async XLA Ops:
  6.5 8.8 %copy-start = (bf16[2,2,64,128]{3,2,1,0:T(8,128)(2,1)S(1)}, bf16[2,2,64,128]{3,2,1,0:T(8,128)(2,1)}, u32[]{:S(2)}) copy-start(bf16[2,2,64,128]{3,2,1,0:T(8,128)(2,1)} %param.3) | copy-start | bytes 196612
  6.5 56.2 %all-gather.3.cloned.1.call-start = ((), (), s32[]{:S(2)}) async-start(), calls=%async_computation.16 | async-start | bytes 3538944 | tf_op jit(solution)/shard_map/all_gather | solution.py:41
  7.5 15.2 %collective-permute-start = (bf16[3,256,128]{2,1,0:T(8,128)(2,1)S(1)}, bf16[3,256,128]{2,1,0:T(8,128)(2,1)S(1)}, u32[]{:S(2)}, u32[]{:S(2)}) collective-permute-start(bf16[3,256,128]{2,1,0:T(8,128)(2,1)S(1)} %slice.6), channel_id=1, source_target_pairs={{0,64},{64,0},{1,65},{65,1},{2,66},{66,2},{3,67},{67,3},{4,68},{68... | collective-permute-start | bytes 589832 | tf_op jit(solution)/shard_map/ppermute | solution.py:28
  23.5 21.6 %collective-permute-start.1 = (bf16[5,256,128]{2,1,0:T(8,128)(2,1)S(1)}, bf16[5,256,128]{2,1,0:T(8,128)(2,1)S(1)}, u32[]{:S(2)}, u32[]{:S(2)}) collective-permute-start(bf16[5,256,128]{2,1,0:T(8,128)(2,1)S(1)} %slice.7), channel_id=1, source_target_pairs={{0,64},{64,0},{1,65},{65,1},{2,66},{66,2},{3,67},{67,3},{4,68},{68... | collective-permute-start | bytes 983048 | tf_op jit(solution)/shard_map/ppermute | solution.py:28
  31.2 25.0 %all-to-all-start = ((bf16[32,16,128]{2,1,0:T(8,128)(2,1)}), bf16[32,16,128]{2,1,0:T(8,128)(2,1)S(1)}, u32[]{:S(2)}, u32[]{:S(2)}) async-start(bf16[32,16,128]{2,1,0:T(8,128)(2,1)} %broadcast_in_dim.2), calls=%async_computation | async-start | bytes 262144 | tf_op jit(solution)/shard_map/all_to_all | solution.py:24
  44.7 69.7 %all-gather.5.cloned.1.call-start = ((), (), s32[]{:S(2)}) async-start(), calls=%async_computation.17 | async-start | bytes 5898240 | tf_op jit(solution)/shard_map/all_gather | solution.py:46
  56.2 9.3 %copy-start.14 = (bf16[32,16,128]{2,1,0:T(8,128)(2,1)}, bf16[32,16,128]{2,1,0:T(8,128)(2,1)S(1)}, u32[]{:S(2)}) copy-start(bf16[32,16,128]{2,1,0:T(8,128)(2,1)S(1)} %all-to-all-done.got.refs_0_) | copy-start | bytes 393220
  62.7 1.9 copy-start.4
  64.6 21.0 %copy-start.5 = (bf16[3,4096,128]{2,1,0:T(8,128)(2,1)S(1)}, bf16[3,4096,128]{2,1,0:T(8,128)(2,1)}, u32[]{:S(2)}) copy-start(bf16[3,4096,128]{2,1,0:T(8,128)(2,1)} %all-gather.3.cloned.1.call-done.matrices) | copy-start | bytes 9437188
  85.7 0.7 copy-start.10
  100.2 0.7 copy-start.12
  114.4 2.5 copy-start.1
  116.9 14.2 %copy-start.2 = (bf16[5,4096,128]{2,1,0:T(8,128)(2,1)S(1)}, bf16[5,4096,128]{2,1,0:T(8,128)(2,1)}, u32[]{:S(2)}) copy-start(bf16[5,4096,128]{2,1,0:T(8,128)(2,1)} %all-gather.5.cloned.1.call-done.matrices) | copy-start | bytes 15728644
  145.0 0.7 copy-start.6
  145.6 13.6 %copy-start.17 = (f32[16,128]{1,0:T(8,128)}, f32[16,128]{1,0:T(8,128)S(1)}, u32[]{:S(2)}) copy-start(f32[16,128]{1,0:T(8,128)S(1)} %get-tuple-element.89.slope) | copy-start | bytes 24580
  145.6 13.6 %copy-start.19 = (f32[16,128]{1,0:T(8,128)}, f32[16,128]{1,0:T(8,128)S(1)}, u32[]{:S(2)}) copy-start(f32[16,128]{1,0:T(8,128)S(1)} %get-tuple-element.90.scaled) | copy-start | bytes 24580
  159.2 0.7 copy-start.8
  159.9 0.7 copy-start.16
  160.5 0.6 copy-start.21
  161.1 0.6 copy-start.23
  161.7 15.1 %all-to-all-start.7 = ((bf16[32,16,128]{2,1,0:T(8,128)(2,1)}), bf16[32,16,128]{2,1,0:T(8,128)(2,1)}, u32[]{:S(2)}, u32[]{:S(2)}) async-start(bf16[32,16,128]{2,1,0:T(8,128)(2,1)} %copy-done.16), calls=%async_computation.7 | async-start | bytes 262144 | tf_op jit(solution)/shard_map/all_to_all | solution.py:24
  176.8 2.5 copy-start.3
  180.4 14.9 %copy-start.9 = (bf16[32,16,128]{2,1,0:T(8,128)(2,1)S(1)}, bf16[32,16,128]{2,1,0:T(8,128)(2,1)}, u32[]{:S(2)}) copy-start(bf16[32,16,128]{2,1,0:T(8,128)(2,1)} %copy-done.8) | copy-start | bytes 393220
  180.4 14.9 %copy-start.22 = (f32[16,128]{1,0:T(8,128)S(1)}, f32[16,128]{1,0:T(8,128)}, u32[]{:S(2)}) copy-start(f32[16,128]{1,0:T(8,128)} %copy-done.21) | copy-start | bytes 24580
  180.4 14.9 %copy-start.24 = (f32[16,128]{1,0:T(8,128)S(1)}, f32[16,128]{1,0:T(8,128)}, u32[]{:S(2)}) copy-start(f32[16,128]{1,0:T(8,128)} %copy-done.23) | copy-start | bytes 24580
  195.3 14.2 %copy-start.7 = (bf16[32,16,128]{2,1,0:T(8,128)(2,1)S(1)}, bf16[32,16,128]{2,1,0:T(8,128)(2,1)}, u32[]{:S(2)}) copy-start(bf16[32,16,128]{2,1,0:T(8,128)(2,1)} %copy-done.6) | copy-start | bytes 393220
  195.4 14.2 %copy-start.18 = (f32[16,128]{1,0:T(8,128)S(1)}, f32[16,128]{1,0:T(8,128)}, u32[]{:S(2)}) copy-start(f32[16,128]{1,0:T(8,128)} %copy-done.17) | copy-start | bytes 24580
  195.4 14.2 %copy-start.20 = (f32[16,128]{1,0:T(8,128)S(1)}, f32[16,128]{1,0:T(8,128)}, u32[]{:S(2)}) copy-start(f32[16,128]{1,0:T(8,128)} %copy-done.19) | copy-start | bytes 24580
  195.4 42.0 %slice-start = ((s8[5242880]{0:T(1024)(128)(4,1)}), s8[4194304]{0:T(1024)(128)(4,1)S(1)}, s32[]{:S(2)}) async-start(s8[5242880]{0:T(1024)(128)(4,1)} %bitcast.3), calls=%async_computation.18 | async-start | bytes 8388608
  209.6 27.8 %slice-start.1 = ((s8[5242880]{0:T(1024)(128)(4,1)}), s8[1048576]{0:T(1024)(128)(4,1)S(1)}, s32[]{:S(2)}) async-start(s8[5242880]{0:T(1024)(128)(4,1)} %bitcast.3), calls=%async_computation.19 | async-start | bytes 2097152
  237.4 13.9 %copy-start.13 = (bf16[32,16,128]{2,1,0:T(8,128)(2,1)S(1)}, bf16[32,16,128]{2,1,0:T(8,128)(2,1)}, u32[]{:S(2)}) copy-start(bf16[32,16,128]{2,1,0:T(8,128)(2,1)} %copy-done.12) | copy-start | bytes 393220
  251.3 13.9 %copy-start.11 = (bf16[32,16,128]{2,1,0:T(8,128)(2,1)S(1)}, bf16[32,16,128]{2,1,0:T(8,128)(2,1)}, u32[]{:S(2)}) copy-start(bf16[32,16,128]{2,1,0:T(8,128)(2,1)} %copy-done.10) | copy-start | bytes 393220
  265.2 14.0 %copy-start.15 = (bf16[32,16,128]{2,1,0:T(8,128)(2,1)S(1)}, bf16[32,16,128]{2,1,0:T(8,128)(2,1)}, u32[]{:S(2)}) copy-start(bf16[32,16,128]{2,1,0:T(8,128)(2,1)} %copy-done.14) | copy-start | bytes 393220
Sparse Core Ops, SparseCore 0:
  23.6 39.1 all-gather.2
  64.9 41.9 all-gather.4

commit v5 on v4

--- a/solution.py
+++ b/solution.py
@@ -14,6 +14,7 @@
 SECTION = ("x", "far", "core")
 ACROSS, FAR, CORES = 4, 2, 2
 EARLY = 3
+FETCHING = (0, EARLY)
 
 
 def spread(block, copies):
@@ -44,7 +45,7 @@
     pair, gather = gathered(last, crossed_last)
     pair, blocks = lax.optimization_barrier((pair, blocks))
     late = gather(pair)
-    return blocks, close(early), close(late)
+    return blocks, early, late
 
 
 def block_order(per):
@@ -58,24 +59,35 @@
     return order
 
 
-def forward_kernel(layer, per, got, x, matrices, *outs):
-    *sent, x_new, slope, scaled = outs
+def forward_kernel(layer, per, fetching, got, x, matrices, *refs):
+    if fetching:
+        *refs, held, arrived = refs
+    *sent, x_new, slope, scaled = refs
     members, tokens, columns = got.shape
     features = members * columns
+    order = block_order(per)
+    count = ACROSS * CORES
+    rows, blocks = features // count, members // count
+    copies = []
+    for n in range(count if fetching else 0):
+        part = pl.ds(n * rows, rows)
+        copies.append(
+            pltpu.make_async_copy(matrices.at[layer, part], held.at[part], arrived.at[n])
+        )
+        copies[n].start()
     squares = jnp.zeros(x.shape, F32)
     for m in range(members):
         squares += jnp.square(got[m].astype(F32))
     mean = jnp.sum(squares, axis=1, keepdims=True) / features
     inverse_rms = lax.rsqrt(mean + EPSILON)
-    order = block_order(per)
-    count = ACROSS * CORES
-    rows, blocks = features // count, members // count
     product = jnp.zeros(x.shape, F32)
     for n in range(count):
         segment = jnp.concatenate([got[m] for m in order[n * blocks : (n + 1) * blocks]], axis=1)
-        product += jnp.dot(
-            segment, matrices[layer, pl.ds(n * rows, rows)], preferred_element_type=F32
-        )
+        part = pl.ds(n * rows, rows)
+        if fetching:
+            copies[n].wait()
+        matrix = held[part] if fetching else matrices[layer, part]
+        product += jnp.dot(segment, matrix, preferred_element_type=F32)
     activation = inverse_rms * product
     sigmoid = jax.nn.sigmoid(activation)
     result = (x[...].astype(F32) + activation * sigmoid).astype(BF16)
@@ -150,13 +162,15 @@
             out[s, pl.ds(b * columns, columns)] = total.astype(BF16)
 
 
-def local_call(kernel, outs, *inputs):
+def local_call(kernel, outs, *inputs, fetching=False, scratch=()):
     vmem = pl.BlockSpec(memory_space=pltpu.VMEM)
+    there = pl.BlockSpec(memory_space=pl.ANY)
     call = pl.pallas_call(
         kernel,
         out_shape=[jax.ShapeDtypeStruct(shape, dtype) for shape, dtype in outs],
-        in_specs=[vmem] * len(inputs),
+        in_specs=[vmem] * (len(inputs) - fetching) + [there] * fetching,
         out_specs=[vmem] * len(outs),
+        scratch_shapes=list(scratch),
         compiler_params=pltpu.CompilerParams(vmem_limit_bytes=32 * 2**20),
     )
     return call(*inputs)
@@ -180,16 +194,32 @@
     own_target = lax.dynamic_slice_in_dim(
         targets.reshape(all_tokens, columns), group * tokens, tokens, 0
     )
+    own_x, own_target = lax.optimization_barrier((own_x, own_target))
     blocks, early, late = fetched_matrices(weights, own_x, members)
 
+    scratch = [
+        pltpu.VMEM((members * columns, columns), BF16),
+        pltpu.SemaphoreType.DMA((ACROSS * CORES,)),
+    ]
+    early_there, late_there = [
+        pltpu.with_memory_space_constraint(array, pltpu.HBM) for array in (early, late)
+    ]
+    early, late = close(early), close(late)
     kept = []
     x = own_x
     for s in range(sections):
-        matrices, at = (early, s) if s < EARLY else (late, s - EARLY)
+        fetching = s in FETCHING
+        if s < EARLY:
+            matrices, at = early_there if fetching else early, s
+        else:
+            matrices, at = late_there if fetching else late, s - EARLY
         outs = [((members,) + block, BF16)] if s < sections - 1 else []
         outs += [(block, BF16), (block, F32), (block, F32)]
-        kernel = functools.partial(forward_kernel, at, per)
-        *sent, x, slope, scaled = local_call(kernel, outs, blocks, x, matrices)
+        kernel = functools.partial(forward_kernel, at, per, fetching)
+        given = (kernel, outs, blocks, x, matrices)
+        *sent, x, slope, scaled = local_call(
+            *given, fetching=fetching, scratch=scratch if fetching else ()
+        )
         kept.append((blocks, slope, scaled))
         if sent:
             blocks = exchanged(sent[0], TP)

time: 337 us -> 328 us (0.973)
  blocking collectives: 232 us -> 245 us
  waiting for transfers between devices: 33.2 us -> 23.6 us
  local copies, waits for them, and re-layouts: 13.6 us -> 5.12 us
  starting transfers between devices: 33 us -> 27.4 us
    all_to_all x14 -> x15, blocking collectives: 232 us -> 245 us  [exchanged(): return lax.all_to_all(blocks, axis, split_axis=0, concat_axis=0, tiled=True)]
    all_to_all x2 -> x1, waiting for transfers between devices: 19 us -> 10.2 us  [exchanged(): return lax.all_to_all(blocks, axis, split_axis=0, concat_axis=0, tiled=True)]
    unnamed x54 -> x24, local copies, waits for them, and re-layouts: 10.2 us -> 1.81 us
    all_to_all x2 -> x1, starting transfers between devices: 19.1 us -> 13.5 us  [exchanged(): return lax.all_to_all(blocks, axis, split_axis=0, concat_axis=0, tiled=True)]
  transfers between devices with their start and end apart: 6 -> 5, of which waited for: 5 -> 4; matrix products, arithmetic and copies ran while one was open for 1% -> 1% of each run, Pallas kernels for 0% -> 1%
where the time goes in v5:
time: 328 us; the launch traced here: 327 us
  blocking collectives  245 us (75%)
  starting transfers between devices  27.4 us (8%)
  waiting for transfers between devices  23.6 us (7%)
  between operations  13.6 us (4%)
  Pallas kernels  10.8 us (3%)
  local copies, waits for them, and re-layouts  5.12 us (2%)
    all_to_all x15, blocking collectives, exchanged(): return lax.all_to_all(blocks, axis, split_axis=0, concat_axis=0, tiled=True)  245 us
    ppermute x2, starting transfers between devices, swapped(): return lax.ppermute(block, axis, [(0, 1), (1, 0)])  13.8 us
    all_to_all x1, starting transfers between devices, exchanged(): return lax.all_to_all(blocks, axis, split_axis=0, concat_axis=0, tiled=True)  13.5 us
    pallas_call x17, Pallas kernels, local_call(): return call(*inputs)  10.8 us
    all_to_all x1, waiting for transfers between devices, exchanged(): return lax.all_to_all(blocks, axis, split_axis=0, concat_axis=0, tiled=True)  10.2 us
    ppermute x2, waiting for transfers between devices, swapped(): return lax.ppermute(block, axis, [(0, 1), (1, 0)])  6.88 us
  transfers between devices with their start and end apart: 5, of which 4 were waited for; matrix products, arithmetic and copies ran while one was open for 1% of the time, Pallas kernels for 1%

profile of v5, /device:TPU:8, one launch (start us, length us, event | category | flops | bytes accessed | tf_op | source)
XLA Modules:
  0.0 327.4 jit_solution(13101137933664709313)
XLA Ops:
  6.5 0.0 all-gather.3.cloned.1.call-start
  6.5 0.9 slice.6
  7.5 6.8 %collective-permute-start = (bf16[3,256,128]{2,1,0:T(8,128)(2,1)S(1)}, bf16[3,256,128]{2,1,0:T(8,128)(2,1)S(1)}, u32[]{:S(2)}, u32[]{:S(2)}) collective-permute-start(bf16[3,256,128]{2,1,0:T(8,128)(2,1)S(1)} %slice.6), channel_id=1, source_target_pairs={{0,64},{64,0},{1,65},{65,1},{2,66},{66,2},{3,67},{67,3},{4,68},{68... | collective-permute-start | bytes 589832 | tf_op jit(solution)/shard_map/ppermute | solution.py:29
  14.3 1.0 slice.7
  15.3 0.7 constant_dynamic-slice_fusion
  16.0 6.6 %collective-permute-done = bf16[3,256,128]{2,1,0:T(8,128)(2,1)S(1)} collective-permute-done((bf16[3,256,128]{2,1,0:T(8,128)(2,1)S(1)}, bf16[3,256,128]{2,1,0:T(8,128)(2,1)S(1)}, u32[]{:S(2)}, u32[]{:S(2)}) %collective-permute-start) | collective-permute-done | bytes 196640 | tf_op jit(solution)/shard_map/ppermute | solution.py:29
  22.6 0.8 pad_maximum_fusion.1
  23.4 0.0 all-gather.3.cloned.1.call-update
  23.4 7.0 %collective-permute-start.1 = (bf16[5,256,128]{2,1,0:T(8,128)(2,1)S(1)}, bf16[5,256,128]{2,1,0:T(8,128)(2,1)S(1)}, u32[]{:S(2)}, u32[]{:S(2)}) collective-permute-start(bf16[5,256,128]{2,1,0:T(8,128)(2,1)S(1)} %slice.7), channel_id=1, source_target_pairs={{0,64},{64,0},{1,65},{65,1},{2,66},{66,2},{3,67},{67,3},{4,68},{68... | collective-permute-start | bytes 983048 | tf_op jit(solution)/shard_map/ppermute | solution.py:29
  30.4 0.7 broadcast_in_dim.2
  31.1 13.5 %all-to-all-start = ((bf16[32,16,128]{2,1,0:T(8,128)(2,1)}), bf16[32,16,128]{2,1,0:T(8,128)(2,1)S(1)}, u32[]{:S(2)}, u32[]{:S(2)}) async-start(bf16[32,16,128]{2,1,0:T(8,128)(2,1)} %broadcast_in_dim.2), calls=%async_computation | async-start | bytes 262144 | tf_op jit(solution)/shard_map/all_to_all | solution.py:25
  44.7 0.0 all-gather.5.cloned.1.call-start
  44.7 0.3 collective-permute-done.1
  45.0 0.9 pad_maximum_fusion
  46.0 10.2 %all-to-all-done.got.refs_0_ = bf16[32,16,128]{2,1,0:T(8,128)(2,1)S(1)} async-done(((bf16[32,16,128]{2,1,0:T(8,128)(2,1)}), bf16[32,16,128]{2,1,0:T(8,128)(2,1)S(1)}, u32[]{:S(2)}, u32[]{:S(2)}) %all-to-all-start) | async-done | bytes 131104 | tf_op jit(solution)/shard_map/all_to_all | solution.py:25
  56.1 0.0 copy-start.2
  56.2 0.0 all-gather.5.cloned.1.call-update
  56.2 6.5 %all-gather.3.cloned.1.call-done.matrices = bf16[3,4096,128]{2,1,0:T(8,128)(2,1)} async-done(((bf16[3,512,128]{2,1,0:T(8,128)(2,1)}), bf16[3,4096,128]{2,1,0:T(8,128)(2,1)}) %all-gather.3.cloned.1.call-update) | async-done | bytes 3145744 | tf_op jit(solution)/shard_map/all_gather | solution.py:42
  62.7 2.8 shard_map.37
  65.5 0.0 copy-done.2
  65.5 20.1 %all_to_all.80.got.refs_1_ = bf16[32,16,128]{2,1,0:T(8,128)(2,1)S(1)} all-to-all(bf16[32,16,128]{2,1,0:T(8,128)(2,1)S(1)} %get-tuple-element.68), channel_id=1, replica_groups=mesh['x'=4,'far'=2,'core'=2,'tp'=32] {'tp'}, dimensions={0} | all-to-all | bytes 262144 | tf_op jit(solution)/shard_map/all_to_all | solution.py:25
  85.6 0.0 copy-done.1
  85.6 0.3 shard_map.38
  85.9 0.0 copy-start.6
  85.9 0.6 copy-done.6
  86.4 13.8 %all_to_all.81.got.refs_2_ = bf16[32,16,128]{2,1,0:T(8,128)(2,1)S(1)} all-to-all(bf16[32,16,128]{2,1,0:T(8,128)(2,1)S(1)} %get-tuple-element.70), channel_id=1, replica_groups=mesh['x'=4,'far'=2,'core'=2,'tp'=32] {'tp'}, dimensions={0} | all-to-all | bytes 262144 | tf_op jit(solution)/shard_map/all_to_all | solution.py:25
  100.3 0.0 copy-done.4
  100.3 0.3 shard_map.39
  100.6 0.0 copy-start.8
  100.6 0.6 copy-done.8
  101.2 0.6 copy-done.10
  101.8 13.6 %all_to_all.82.got.refs_3_ = bf16[32,16,128]{2,1,0:T(8,128)(2,1)S(1)} all-to-all(bf16[32,16,128]{2,1,0:T(8,128)(2,1)S(1)} %get-tuple-element.72), channel_id=1, replica_groups=mesh['x'=4,'far'=2,'core'=2,'tp'=32] {'tp'}, dimensions={0} | all-to-all | bytes 262144 | tf_op jit(solution)/shard_map/all_to_all | solution.py:25
  115.4 2.2 shard_map.40
  117.6 13.6 %all_to_all.83.got.refs_4_ = bf16[32,16,128]{2,1,0:T(8,128)(2,1)S(1)} all-to-all(bf16[32,16,128]{2,1,0:T(8,128)(2,1)S(1)} %get-tuple-element.75), channel_id=1, replica_groups=mesh['x'=4,'far'=2,'core'=2,'tp'=32] {'tp'}, dimensions={0} | all-to-all | bytes 262144 | tf_op jit(solution)/shard_map/all_to_all | solution.py:25
  131.2 0.0 copy-done
  131.2 0.3 shard_map.41
  131.5 13.6 %all_to_all.84.got.refs_5_ = bf16[32,16,128]{2,1,0:T(8,128)(2,1)S(1)} all-to-all(bf16[32,16,128]{2,1,0:T(8,128)(2,1)S(1)} %get-tuple-element.77), channel_id=1, replica_groups=mesh['x'=4,'far'=2,'core'=2,'tp'=32] {'tp'}, dimensions={0} | all-to-all | bytes 262144 | tf_op jit(solution)/shard_map/all_to_all | solution.py:25
  145.1 0.3 shard_map.42
  145.4 13.6 %all_to_all.85.got.refs_6_ = bf16[32,16,128]{2,1,0:T(8,128)(2,1)S(1)} all-to-all(bf16[32,16,128]{2,1,0:T(8,128)(2,1)S(1)} %get-tuple-element.79), channel_id=1, replica_groups=mesh['x'=4,'far'=2,'core'=2,'tp'=32] {'tp'}, dimensions={0} | all-to-all | bytes 262144 | tf_op jit(solution)/shard_map/all_to_all | solution.py:25
  159.0 0.3 shard_map.43
  159.2 13.6 %all_to_all.86.got.refs_7_ = bf16[32,16,128]{2,1,0:T(8,128)(2,1)S(1)} all-to-all(bf16[32,16,128]{2,1,0:T(8,128)(2,1)S(1)} %get-tuple-element.81), channel_id=1, replica_groups=mesh['x'=4,'far'=2,'core'=2,'tp'=32] {'tp'}, dimensions={0} | all-to-all | bytes 262144 | tf_op jit(solution)/shard_map/all_to_all | solution.py:25
  172.8 0.3 shard_map.44
  173.1 0.4 shard_map.45
  173.5 13.6 %all_to_all.87.received = bf16[32,16,128]{2,1,0:T(8,128)(2,1)S(1)} all-to-all(bf16[32,16,128]{2,1,0:T(8,128)(2,1)S(1)} %get-tuple-element.87), channel_id=1, replica_groups=mesh['x'=4,'far'=2,'core'=2,'tp'=32] {'tp'}, dimensions={0} | all-to-all | bytes 262144 | tf_op jit(solution)/shard_map/all_to_all | solution.py:25
  187.1 0.4 shard_map.46
  187.5 13.6 %all_to_all.88.received = bf16[32,16,128]{2,1,0:T(8,128)(2,1)S(1)} all-to-all(bf16[32,16,128]{2,1,0:T(8,128)(2,1)S(1)} %get-tuple-element.91), channel_id=1, replica_groups=mesh['x'=4,'far'=2,'core'=2,'tp'=32] {'tp'}, dimensions={0} | all-to-all | bytes 262144 | tf_op jit(solution)/shard_map/all_to_all | solution.py:25
  201.1 0.4 shard_map.47
  201.5 13.6 %all_to_all.89.received = bf16[32,16,128]{2,1,0:T(8,128)(2,1)S(1)} all-to-all(bf16[32,16,128]{2,1,0:T(8,128)(2,1)S(1)} %get-tuple-element.95), channel_id=1, replica_groups=mesh['x'=4,'far'=2,'core'=2,'tp'=32] {'tp'}, dimensions={0} | all-to-all | bytes 262144 | tf_op jit(solution)/shard_map/all_to_all | solution.py:25
  215.1 0.4 shard_map.48
  215.5 13.6 %all_to_all.90.received = bf16[32,16,128]{2,1,0:T(8,128)(2,1)S(1)} all-to-all(bf16[32,16,128]{2,1,0:T(8,128)(2,1)S(1)} %get-tuple-element.99), channel_id=1, replica_groups=mesh['x'=4,'far'=2,'core'=2,'tp'=32] {'tp'}, dimensions={0} | all-to-all | bytes 262144 | tf_op jit(solution)/shard_map/all_to_all | solution.py:25
  229.1 0.4 shard_map.49
  229.5 13.6 %all_to_all.91.received = bf16[32,16,128]{2,1,0:T(8,128)(2,1)S(1)} all-to-all(bf16[32,16,128]{2,1,0:T(8,128)(2,1)S(1)} %get-tuple-element.103), channel_id=1, replica_groups=mesh['x'=4,'far'=2,'core'=2,'tp'=32] {'tp'}, dimensions={0} | all-to-all | bytes 262144 | tf_op jit(solution)/shard_map/all_to_all | solution.py:25
  243.1 0.0 copy-done.9
  243.1 0.0 copy-done.11
  243.1 0.4 shard_map.50
  243.5 13.6 %all_to_all.92.received = bf16[32,16,128]{2,1,0:T(8,128)(2,1)S(1)} all-to-all(bf16[32,16,128]{2,1,0:T(8,128)(2,1)S(1)} %get-tuple-element.107), channel_id=1, replica_groups=mesh['x'=4,'far'=2,'core'=2,'tp'=32] {'tp'}, dimensions={0} | all-to-all | bytes 262144 | tf_op jit(solution)/shard_map/all_to_all | solution.py:25
  257.1 0.0 copy-done.5
  257.1 0.0 copy-done.7
  257.1 0.4 shard_map.51
  257.5 13.6 %all_to_all.93.received = bf16[32,16,128]{2,1,0:T(8,128)(2,1)S(1)} all-to-all(bf16[32,16,128]{2,1,0:T(8,128)(2,1)S(1)} %get-tuple-element.111), channel_id=1, replica_groups=mesh['x'=4,'far'=2,'core'=2,'tp'=32] {'tp'}, dimensions={0} | all-to-all | bytes 262144 | tf_op jit(solution)/shard_map/all_to_all | solution.py:25
  271.1 0.0 copy-done.3
  271.1 0.2 shard_map.52
  271.3 48.0 %all_to_all.94.arrived = bf16[16,384,128]{2,1,0:T(8,128)(2,1)S(1)} all-to-all(bf16[16,384,128]{2,1,0:T(8,128)(2,1)S(1)} %shard_map.52), channel_id=1, replica_groups=mesh['x'=4,'far'=2,'core'=2,'tp'=32] {'x','far','core'}, dimensions={0} | all-to-all | bytes 3145728 | tf_op jit(solution)/shard_map/all_to_all | solution.py:25
  319.3 1.3 shard_map.53
  (10 shorter events, 0.0 us)
Async XLA Ops:
  6.5 56.2 %all-gather.3.cloned.1.call-start = ((), (), s32[]{:S(2)}) async-start(), calls=%async_computation.16 | async-start | bytes 3538944 | tf_op jit(solution)/shard_map/all_gather | solution.py:42
  7.5 15.2 %collective-permute-start = (bf16[3,256,128]{2,1,0:T(8,128)(2,1)S(1)}, bf16[3,256,128]{2,1,0:T(8,128)(2,1)S(1)}, u32[]{:S(2)}, u32[]{:S(2)}) collective-permute-start(bf16[3,256,128]{2,1,0:T(8,128)(2,1)S(1)} %slice.6), channel_id=1, source_target_pairs={{0,64},{64,0},{1,65},{65,1},{2,66},{66,2},{3,67},{67,3},{4,68},{68... | collective-permute-start | bytes 589832 | tf_op jit(solution)/shard_map/ppermute | solution.py:29
  23.4 21.6 %collective-permute-start.1 = (bf16[5,256,128]{2,1,0:T(8,128)(2,1)S(1)}, bf16[5,256,128]{2,1,0:T(8,128)(2,1)S(1)}, u32[]{:S(2)}, u32[]{:S(2)}) collective-permute-start(bf16[5,256,128]{2,1,0:T(8,128)(2,1)S(1)} %slice.7), channel_id=1, source_target_pairs={{0,64},{64,0},{1,65},{65,1},{2,66},{66,2},{3,67},{67,3},{4,68},{68... | collective-permute-start | bytes 983048 | tf_op jit(solution)/shard_map/ppermute | solution.py:29
  31.1 25.0 %all-to-all-start = ((bf16[32,16,128]{2,1,0:T(8,128)(2,1)}), bf16[32,16,128]{2,1,0:T(8,128)(2,1)S(1)}, u32[]{:S(2)}, u32[]{:S(2)}) async-start(bf16[32,16,128]{2,1,0:T(8,128)(2,1)} %broadcast_in_dim.2), calls=%async_computation | async-start | bytes 262144 | tf_op jit(solution)/shard_map/all_to_all | solution.py:25
  44.7 70.7 %all-gather.5.cloned.1.call-start = ((), (), s32[]{:S(2)}) async-start(), calls=%async_computation.17 | async-start | bytes 5898240 | tf_op jit(solution)/shard_map/all_gather | solution.py:47
  56.1 9.3 %copy-start.2 = (bf16[32,16,128]{2,1,0:T(8,128)(2,1)}, bf16[32,16,128]{2,1,0:T(8,128)(2,1)S(1)}, u32[]{:S(2)}) copy-start(bf16[32,16,128]{2,1,0:T(8,128)(2,1)S(1)} %all-to-all-done.got.refs_0_) | copy-start | bytes 393220
  62.7 22.9 %copy-start.1 = (bf16[3,4096,128]{2,1,0:T(8,128)(2,1)S(1)}, bf16[3,4096,128]{2,1,0:T(8,128)(2,1)}, u32[]{:S(2)}) copy-start(bf16[3,4096,128]{2,1,0:T(8,128)(2,1)} %all-gather.3.cloned.1.call-done.matrices) | copy-start | bytes 9437188
  85.9 0.6 copy-start.6
  86.4 13.8 %copy-start.4 = (f32[16,128]{1,0:T(8,128)}, f32[16,128]{1,0:T(8,128)S(1)}, u32[]{:S(2)}) copy-start(f32[16,128]{1,0:T(8,128)S(1)} %get-tuple-element.109.slope) | copy-start | bytes 24580
  100.6 0.6 copy-start.8
  101.2 0.6 copy-start.10
  115.4 15.8 %copy-start = (bf16[5,4096,128]{2,1,0:T(8,128)(2,1)S(1)}, bf16[5,4096,128]{2,1,0:T(8,128)(2,1)}, u32[]{:S(2)}) copy-start(bf16[5,4096,128]{2,1,0:T(8,128)(2,1)} %all-gather.5.cloned.1.call-done.matrices) | copy-start | bytes 15728644
  229.1 14.0 %copy-start.9 = (f32[16,128]{1,0:T(8,128)S(1)}, f32[16,128]{1,0:T(8,128)}, u32[]{:S(2)}) copy-start(f32[16,128]{1,0:T(8,128)} %copy-done.8) | copy-start | bytes 24580
  229.1 14.0 %copy-start.11 = (f32[16,128]{1,0:T(8,128)S(1)}, f32[16,128]{1,0:T(8,128)}, u32[]{:S(2)}) copy-start(f32[16,128]{1,0:T(8,128)} %copy-done.10) | copy-start | bytes 24580
  243.1 14.0 %copy-start.5 = (f32[16,128]{1,0:T(8,128)S(1)}, f32[16,128]{1,0:T(8,128)}, u32[]{:S(2)}) copy-start(f32[16,128]{1,0:T(8,128)} %copy-done.4) | copy-start | bytes 24580
  243.1 14.0 %copy-start.7 = (f32[16,128]{1,0:T(8,128)S(1)}, f32[16,128]{1,0:T(8,128)}, u32[]{:S(2)}) copy-start(f32[16,128]{1,0:T(8,128)} %copy-done.6) | copy-start | bytes 24580
  257.1 14.0 %copy-start.3 = (bf16[32,16,128]{2,1,0:T(8,128)(2,1)S(1)}, bf16[32,16,128]{2,1,0:T(8,128)(2,1)}, u32[]{:S(2)}) copy-start(bf16[32,16,128]{2,1,0:T(8,128)(2,1)} %copy-done.2) | copy-start | bytes 393220
Sparse Core Ops, SparseCore 0:
  23.6 39.1 all-gather.2
  64.8 41.9 all-gather.4

commit v6 on v5

--- a/solution.py
+++ b/solution.py
@@ -14,7 +14,7 @@
 SECTION = ("x", "far", "core")
 ACROSS, FAR, CORES = 4, 2, 2
 EARLY = 3
-FETCHING = (0, EARLY)
+FETCHING = (0, 2, EARLY)
 
 
 def spread(block, copies):
@@ -62,7 +62,7 @@
 def forward_kernel(layer, per, fetching, got, x, matrices, *refs):
     if fetching:
         *refs, held, arrived = refs
-    *sent, x_new, slope, scaled = refs
+    *sent, x_new, factors = refs
     members, tokens, columns = got.shape
     features = members * columns
     order = block_order(per)
@@ -94,11 +94,11 @@
     x_new[...] = result
     for target in sent:
         target[...] = jnp.broadcast_to(result[None], target.shape)
-    slope[...] = inverse_rms * sigmoid * (1.0 + activation * (1.0 - sigmoid))
-    scaled[...] = product * (inverse_rms * inverse_rms / features)
-
-
-def backward_kernel(layer, per, micro_tokens, received, cotangent, slope, scaled, got, matrices, *outs):
+    factors[0] = inverse_rms * sigmoid * (1.0 + activation * (1.0 - sigmoid))
+    factors[1] = product * (inverse_rms * inverse_rms / features)
+
+
+def backward_kernel(layer, per, micro_tokens, received, cotangent, factors, got, matrices, *outs):
     parts, h_out, cot_out = outs
     members, tokens, columns = got.shape
     if len(received.shape) == 2:
@@ -109,9 +109,9 @@
             total += received[m].astype(F32)
         cot = total.astype(BF16).astype(F32)
     cot_out[...] = cot
-    h = (slope[...] * cot).astype(BF16)
+    h = (factors[0] * cot).astype(BF16)
     h_out[...] = h
-    share = jnp.sum(h.astype(F32) * scaled[...], axis=1, keepdims=True)
+    share = jnp.sum(h.astype(F32) * factors[1], axis=1, keepdims=True)
     order = block_order(per)
     count = ACROSS * CORES
     rows, blocks = members * columns // count, members // count
@@ -128,15 +128,15 @@
             parts[m] = mine.astype(BF16)
 
 
-def last_kernel(per, received, cotangent, slope, *refs):
+def last_kernel(per, received, cotangent, factors, *refs):
     *others, packed = refs
     sections = (len(others) + 1) // 2
     gots, later = others[:sections], others[sections:]
-    tokens = slope.shape[0]
+    tokens = cotangent.shape[0]
     total = cotangent[...]
     for m in range(received.shape[0]):
         total += received[m].astype(F32)
-    h = (slope[...] * total.astype(BF16).astype(F32)).astype(BF16)
+    h = (factors[0] * total.astype(BF16).astype(F32)).astype(BF16)
     for s, block in enumerate([h] + [other[...] for other in later]):
         for g in range(packed.shape[0]):
             at = s * (per + 1) * tokens
@@ -214,13 +214,13 @@
         else:
             matrices, at = late_there if fetching else late, s - EARLY
         outs = [((members,) + block, BF16)] if s < sections - 1 else []
-        outs += [(block, BF16), (block, F32), (block, F32)]
+        outs += [(block, BF16), ((2,) + block, F32)]
         kernel = functools.partial(forward_kernel, at, per, fetching)
         given = (kernel, outs, blocks, x, matrices)
-        *sent, x, slope, scaled = local_call(
+        *sent, x, factors = local_call(
             *given, fetching=fetching, scratch=scratch if fetching else ()
         )
-        kept.append((blocks, slope, scaled))
+        kept.append((blocks, factors))
         if sent:
             blocks = exchanged(sent[0], TP)
 
@@ -228,11 +228,11 @@
     received, cotangent = x, own_target
     for s in range(sections - 1, 0, -1):
         matrices, at = (early, s) if s < EARLY else (late, s - EARLY)
-        blocks, slope, scaled = kept[s]
+        blocks, factors = kept[s]
         outs = [((members,) + block, BF16), (block, BF16), (block, F32)]
         kernel = functools.partial(backward_kernel, at, per, micro_tokens)
         parts, h, cotangent = local_call(
-            kernel, outs, received, cotangent, slope, scaled, blocks, matrices
+            kernel, outs, received, cotangent, factors, blocks, matrices
         )
         grads_h.insert(0, h)
         received = exchanged(parts, TP)

time: 328 us -> 328 us (level)
  no operation moved by 1% of the time
where the time goes in v6:
time: 328 us; the launch traced here: 327 us
  blocking collectives  245 us (75%)
  starting transfers between devices  27.4 us (8%)
  waiting for transfers between devices  23.6 us (7%)
  between operations  13.5 us (4%)
  Pallas kernels  12 us (4%)
  local copies, waits for them, and re-layouts  3.34 us (1%)
    all_to_all x15, blocking collectives, exchanged(): return lax.all_to_all(blocks, axis, split_axis=0, concat_axis=0, tiled=True)  245 us
    ppermute x2, starting transfers between devices, swapped(): return lax.ppermute(block, axis, [(0, 1), (1, 0)])  13.8 us
    all_to_all x1, starting transfers between devices, exchanged(): return lax.all_to_all(blocks, axis, split_axis=0, concat_axis=0, tiled=True)  13.5 us
    pallas_call x17, Pallas kernels, local_call(): return call(*inputs)  12 us
    all_to_all x1, waiting for transfers between devices, exchanged(): return lax.all_to_all(blocks, axis, split_axis=0, concat_axis=0, tiled=True)  10.2 us
    ppermute x2, waiting for transfers between devices, swapped(): return lax.ppermute(block, axis, [(0, 1), (1, 0)])  6.86 us
  transfers between devices with their start and end apart: 5, of which 4 were waited for; matrix products, arithmetic and copies ran while one was open for 1% of the time, Pallas kernels for 1%

profile of v6, /device:TPU:8, one launch (start us, length us, event | category | flops | bytes accessed | tf_op | source)
XLA Modules:
  0.0 327.0 jit_solution(14581871153513984827)
XLA Ops:
  6.5 0.0 all-gather.3.cloned.1.call-start
  6.5 0.9 slice.6
  7.5 6.8 %collective-permute-start = (bf16[3,256,128]{2,1,0:T(8,128)(2,1)S(1)}, bf16[3,256,128]{2,1,0:T(8,128)(2,1)S(1)}, u32[]{:S(2)}, u32[]{:S(2)}) collective-permute-start(bf16[3,256,128]{2,1,0:T(8,128)(2,1)S(1)} %slice.6), channel_id=1, source_target_pairs={{0,64},{64,0},{1,65},{65,1},{2,66},{66,2},{3,67},{67,3},{4,68},{68... | collective-permute-start | bytes 589832 | tf_op jit(solution)/shard_map/ppermute | solution.py:29
  14.3 1.0 slice.7
  15.3 0.7 constant_dynamic-slice_fusion
  16.0 6.6 %collective-permute-done = bf16[3,256,128]{2,1,0:T(8,128)(2,1)S(1)} collective-permute-done((bf16[3,256,128]{2,1,0:T(8,128)(2,1)S(1)}, bf16[3,256,128]{2,1,0:T(8,128)(2,1)S(1)}, u32[]{:S(2)}, u32[]{:S(2)}) %collective-permute-start) | collective-permute-done | bytes 196640 | tf_op jit(solution)/shard_map/ppermute | solution.py:29
  22.6 0.8 pad_maximum_fusion.1
  23.4 0.0 all-gather.3.cloned.1.call-update
  23.4 7.0 %collective-permute-start.1 = (bf16[5,256,128]{2,1,0:T(8,128)(2,1)S(1)}, bf16[5,256,128]{2,1,0:T(8,128)(2,1)S(1)}, u32[]{:S(2)}, u32[]{:S(2)}) collective-permute-start(bf16[5,256,128]{2,1,0:T(8,128)(2,1)S(1)} %slice.7), channel_id=1, source_target_pairs={{0,64},{64,0},{1,65},{65,1},{2,66},{66,2},{3,67},{67,3},{4,68},{68... | collective-permute-start | bytes 983048 | tf_op jit(solution)/shard_map/ppermute | solution.py:29
  30.4 0.7 broadcast_in_dim.2
  31.1 13.5 %all-to-all-start = ((bf16[32,16,128]{2,1,0:T(8,128)(2,1)}), bf16[32,16,128]{2,1,0:T(8,128)(2,1)S(1)}, u32[]{:S(2)}, u32[]{:S(2)}) async-start(bf16[32,16,128]{2,1,0:T(8,128)(2,1)} %broadcast_in_dim.2), calls=%async_computation | async-start | bytes 262144 | tf_op jit(solution)/shard_map/all_to_all | solution.py:25
  44.7 0.0 all-gather.5.cloned.1.call-start
  44.7 0.3 collective-permute-done.1
  45.0 1.0 pad_maximum_fusion
  46.0 10.2 %all-to-all-done.got.refs_0_ = bf16[32,16,128]{2,1,0:T(8,128)(2,1)S(1)} async-done(((bf16[32,16,128]{2,1,0:T(8,128)(2,1)}), bf16[32,16,128]{2,1,0:T(8,128)(2,1)S(1)}, u32[]{:S(2)}, u32[]{:S(2)}) %all-to-all-start) | async-done | bytes 131104 | tf_op jit(solution)/shard_map/all_to_all | solution.py:25
  56.1 0.0 all-gather.5.cloned.1.call-update
  56.2 6.5 %all-gather.3.cloned.1.call-done.matrices = bf16[3,4096,128]{2,1,0:T(8,128)(2,1)} async-done(((bf16[3,512,128]{2,1,0:T(8,128)(2,1)}), bf16[3,4096,128]{2,1,0:T(8,128)(2,1)}) %all-gather.3.cloned.1.call-update) | async-done | bytes 3145744 | tf_op jit(solution)/shard_map/all_gather | solution.py:42
  62.7 0.0 copy-start.1
  62.7 2.2 shard_map.37
  64.9 20.1 %all_to_all.80.got.refs_1_ = bf16[32,16,128]{2,1,0:T(8,128)(2,1)S(1)} all-to-all(bf16[32,16,128]{2,1,0:T(8,128)(2,1)S(1)} %get-tuple-element.61), channel_id=1, replica_groups=mesh['x'=4,'far'=2,'core'=2,'tp'=32] {'tp'}, dimensions={0} | all-to-all | bytes 262144 | tf_op jit(solution)/shard_map/all_to_all | solution.py:25
  85.0 0.0 copy-done.1
  85.0 0.3 shard_map.38
  85.3 13.9 %all_to_all.81.got.refs_2_ = bf16[32,16,128]{2,1,0:T(8,128)(2,1)S(1)} all-to-all(bf16[32,16,128]{2,1,0:T(8,128)(2,1)S(1)} %get-tuple-element.63), channel_id=1, replica_groups=mesh['x'=4,'far'=2,'core'=2,'tp'=32] {'tp'}, dimensions={0} | all-to-all | bytes 262144 | tf_op jit(solution)/shard_map/all_to_all | solution.py:25
  99.1 2.0 shard_map.39
  101.2 13.6 %all_to_all.82.got.refs_3_ = bf16[32,16,128]{2,1,0:T(8,128)(2,1)S(1)} all-to-all(bf16[32,16,128]{2,1,0:T(8,128)(2,1)S(1)} %get-tuple-element.65), channel_id=1, replica_groups=mesh['x'=4,'far'=2,'core'=2,'tp'=32] {'tp'}, dimensions={0} | all-to-all | bytes 262144 | tf_op jit(solution)/shard_map/all_to_all | solution.py:25
  114.8 0.0 all-gather.5.cloned.1.call-done.matrices
  114.8 0.0 copy-start
  114.8 2.2 shard_map.40
  117.0 13.6 %all_to_all.83.got.refs_4_ = bf16[32,16,128]{2,1,0:T(8,128)(2,1)S(1)} all-to-all(bf16[32,16,128]{2,1,0:T(8,128)(2,1)S(1)} %get-tuple-element.68), channel_id=1, replica_groups=mesh['x'=4,'far'=2,'core'=2,'tp'=32] {'tp'}, dimensions={0} | all-to-all | bytes 262144 | tf_op jit(solution)/shard_map/all_to_all | solution.py:25
  130.6 0.0 copy-done
  130.6 0.3 shard_map.41
  130.9 13.6 %all_to_all.84.got.refs_5_ = bf16[32,16,128]{2,1,0:T(8,128)(2,1)S(1)} all-to-all(bf16[32,16,128]{2,1,0:T(8,128)(2,1)S(1)} %get-tuple-element.70), channel_id=1, replica_groups=mesh['x'=4,'far'=2,'core'=2,'tp'=32] {'tp'}, dimensions={0} | all-to-all | bytes 262144 | tf_op jit(solution)/shard_map/all_to_all | solution.py:25
  144.5 0.3 shard_map.42
  144.8 13.6 %all_to_all.85.got.refs_6_ = bf16[32,16,128]{2,1,0:T(8,128)(2,1)S(1)} all-to-all(bf16[32,16,128]{2,1,0:T(8,128)(2,1)S(1)} %get-tuple-element.72), channel_id=1, replica_groups=mesh['x'=4,'far'=2,'core'=2,'tp'=32] {'tp'}, dimensions={0} | all-to-all | bytes 262144 | tf_op jit(solution)/shard_map/all_to_all | solution.py:25
  158.4 0.3 shard_map.43
  158.6 13.6 %all_to_all.86.got.refs_7_ = bf16[32,16,128]{2,1,0:T(8,128)(2,1)S(1)} all-to-all(bf16[32,16,128]{2,1,0:T(8,128)(2,1)S(1)} %get-tuple-element.74), channel_id=1, replica_groups=mesh['x'=4,'far'=2,'core'=2,'tp'=32] {'tp'}, dimensions={0} | all-to-all | bytes 262144 | tf_op jit(solution)/shard_map/all_to_all | solution.py:25
  172.2 0.3 shard_map.44
  172.5 0.4 shard_map.45
  172.9 13.6 %all_to_all.87.received = bf16[32,16,128]{2,1,0:T(8,128)(2,1)S(1)} all-to-all(bf16[32,16,128]{2,1,0:T(8,128)(2,1)S(1)} %get-tuple-element.79), channel_id=1, replica_groups=mesh['x'=4,'far'=2,'core'=2,'tp'=32] {'tp'}, dimensions={0} | all-to-all | bytes 262144 | tf_op jit(solution)/shard_map/all_to_all | solution.py:25
  186.5 0.4 shard_map.46
  186.9 13.6 %all_to_all.88.received = bf16[32,16,128]{2,1,0:T(8,128)(2,1)S(1)} all-to-all(bf16[32,16,128]{2,1,0:T(8,128)(2,1)S(1)} %get-tuple-element.82), channel_id=1, replica_groups=mesh['x'=4,'far'=2,'core'=2,'tp'=32] {'tp'}, dimensions={0} | all-to-all | bytes 262144 | tf_op jit(solution)/shard_map/all_to_all | solution.py:25
  200.5 0.4 shard_map.47
  200.9 13.6 %all_to_all.89.received = bf16[32,16,128]{2,1,0:T(8,128)(2,1)S(1)} all-to-all(bf16[32,16,128]{2,1,0:T(8,128)(2,1)S(1)} %get-tuple-element.85), channel_id=1, replica_groups=mesh['x'=4,'far'=2,'core'=2,'tp'=32] {'tp'}, dimensions={0} | all-to-all | bytes 262144 | tf_op jit(solution)/shard_map/all_to_all | solution.py:25
  214.5 0.4 shard_map.48
  214.9 13.6 %all_to_all.90.received = bf16[32,16,128]{2,1,0:T(8,128)(2,1)S(1)} all-to-all(bf16[32,16,128]{2,1,0:T(8,128)(2,1)S(1)} %get-tuple-element.88), channel_id=1, replica_groups=mesh['x'=4,'far'=2,'core'=2,'tp'=32] {'tp'}, dimensions={0} | all-to-all | bytes 262144 | tf_op jit(solution)/shard_map/all_to_all | solution.py:25
  228.5 0.0 copy-start.2
  228.5 0.4 shard_map.49
  228.9 13.7 %all_to_all.91.received = bf16[32,16,128]{2,1,0:T(8,128)(2,1)S(1)} all-to-all(bf16[32,16,128]{2,1,0:T(8,128)(2,1)S(1)} %get-tuple-element.91), channel_id=1, replica_groups=mesh['x'=4,'far'=2,'core'=2,'tp'=32] {'tp'}, dimensions={0} | all-to-all | bytes 262144 | tf_op jit(solution)/shard_map/all_to_all | solution.py:25
  242.7 0.0 copy-done.2
  242.7 0.4 shard_map.50
  243.0 13.6 %all_to_all.92.received = bf16[32,16,128]{2,1,0:T(8,128)(2,1)S(1)} all-to-all(bf16[32,16,128]{2,1,0:T(8,128)(2,1)S(1)} %get-tuple-element.94), channel_id=1, replica_groups=mesh['x'=4,'far'=2,'core'=2,'tp'=32] {'tp'}, dimensions={0} | all-to-all | bytes 262144 | tf_op jit(solution)/shard_map/all_to_all | solution.py:25
  256.7 0.4 shard_map.51
  257.0 13.6 %all_to_all.93.received = bf16[32,16,128]{2,1,0:T(8,128)(2,1)S(1)} all-to-all(bf16[32,16,128]{2,1,0:T(8,128)(2,1)S(1)} %get-tuple-element.97), channel_id=1, replica_groups=mesh['x'=4,'far'=2,'core'=2,'tp'=32] {'tp'}, dimensions={0} | all-to-all | bytes 262144 | tf_op jit(solution)/shard_map/all_to_all | solution.py:25
  270.7 0.2 shard_map.52
  270.8 48.0 %all_to_all.94.arrived = bf16[16,384,128]{2,1,0:T(8,128)(2,1)S(1)} all-to-all(bf16[16,384,128]{2,1,0:T(8,128)(2,1)S(1)} %shard_map.52), channel_id=1, replica_groups=mesh['x'=4,'far'=2,'core'=2,'tp'=32] {'x','far','core'}, dimensions={0} | all-to-all | bytes 3145728 | tf_op jit(solution)/shard_map/all_to_all | solution.py:25
  318.8 1.3 shard_map.53
Async XLA Ops:
  6.5 56.2 %all-gather.3.cloned.1.call-start = ((), (), s32[]{:S(2)}) async-start(), calls=%async_computation.16 | async-start | bytes 3538944 | tf_op jit(solution)/shard_map/all_gather | solution.py:42
  7.5 15.2 %collective-permute-start = (bf16[3,256,128]{2,1,0:T(8,128)(2,1)S(1)}, bf16[3,256,128]{2,1,0:T(8,128)(2,1)S(1)}, u32[]{:S(2)}, u32[]{:S(2)}) collective-permute-start(bf16[3,256,128]{2,1,0:T(8,128)(2,1)S(1)} %slice.6), channel_id=1, source_target_pairs={{0,64},{64,0},{1,65},{65,1},{2,66},{66,2},{3,67},{67,3},{4,68},{68... | collective-permute-start | bytes 589832 | tf_op jit(solution)/shard_map/ppermute | solution.py:29
  23.4 21.6 %collective-permute-start.1 = (bf16[5,256,128]{2,1,0:T(8,128)(2,1)S(1)}, bf16[5,256,128]{2,1,0:T(8,128)(2,1)S(1)}, u32[]{:S(2)}, u32[]{:S(2)}) collective-permute-start(bf16[5,256,128]{2,1,0:T(8,128)(2,1)S(1)} %slice.7), channel_id=1, source_target_pairs={{0,64},{64,0},{1,65},{65,1},{2,66},{66,2},{3,67},{67,3},{4,68},{68... | collective-permute-start | bytes 983048 | tf_op jit(solution)/shard_map/ppermute | solution.py:29
  31.1 25.0 %all-to-all-start = ((bf16[32,16,128]{2,1,0:T(8,128)(2,1)}), bf16[32,16,128]{2,1,0:T(8,128)(2,1)S(1)}, u32[]{:S(2)}, u32[]{:S(2)}) async-start(bf16[32,16,128]{2,1,0:T(8,128)(2,1)} %broadcast_in_dim.2), calls=%async_computation | async-start | bytes 262144 | tf_op jit(solution)/shard_map/all_to_all | solution.py:25
  44.7 70.1 %all-gather.5.cloned.1.call-start = ((), (), s32[]{:S(2)}) async-start(), calls=%async_computation.17 | async-start | bytes 5898240 | tf_op jit(solution)/shard_map/all_gather | solution.py:47
  62.7 22.3 %copy-start.1 = (bf16[3,4096,128]{2,1,0:T(8,128)(2,1)S(1)}, bf16[3,4096,128]{2,1,0:T(8,128)(2,1)}, u32[]{:S(2)}) copy-start(bf16[3,4096,128]{2,1,0:T(8,128)(2,1)} %all-gather.3.cloned.1.call-done.matrices) | copy-start | bytes 9437188
  114.8 15.8 %copy-start = (bf16[5,4096,128]{2,1,0:T(8,128)(2,1)S(1)}, bf16[5,4096,128]{2,1,0:T(8,128)(2,1)}, u32[]{:S(2)}) copy-start(bf16[5,4096,128]{2,1,0:T(8,128)(2,1)} %all-gather.5.cloned.1.call-done.matrices) | copy-start | bytes 15728644
  228.5 14.1 %copy-start.2 = (bf16[3,4096,128]{2,1,0:T(8,128)(2,1)S(1)}, bf16[3,4096,128]{2,1,0:T(8,128)(2,1)}, u32[]{:S(2)}) copy-start(bf16[3,4096,128]{2,1,0:T(8,128)(2,1)} %all-gather.3.cloned.1.call-done.matrices) | copy-start | bytes 9437188
Sparse Core Ops, SparseCore 0:
  23.6 39.1 all-gather.2
  64.8 41.9 all-gather.4

commit v7 on v6

--- a/solution.py
+++ b/solution.py
@@ -69,8 +69,8 @@
     count = ACROSS * CORES
     rows, blocks = features // count, members // count
     copies = []
-    for n in range(count if fetching else 0):
-        part = pl.ds(n * rows, rows)
+    for n in range(ACROSS if fetching else 0):
+        part = pl.ds(n * CORES * rows, CORES * rows)
         copies.append(
             pltpu.make_async_copy(matrices.at[layer, part], held.at[part], arrived.at[n])
         )
@@ -84,8 +84,8 @@
     for n in range(count):
         segment = jnp.concatenate([got[m] for m in order[n * blocks : (n + 1) * blocks]], axis=1)
         part = pl.ds(n * rows, rows)
-        if fetching:
-            copies[n].wait()
+        if fetching and n % CORES == 0:
+            copies[n // CORES].wait()
         matrix = held[part] if fetching else matrices[layer, part]
         product += jnp.dot(segment, matrix, preferred_element_type=F32)
     activation = inverse_rms * product
@@ -199,7 +199,7 @@
 
     scratch = [
         pltpu.VMEM((members * columns, columns), BF16),
-        pltpu.SemaphoreType.DMA((ACROSS * CORES,)),
+        pltpu.SemaphoreType.DMA((ACROSS,)),
     ]
     early_there, late_there = [
         pltpu.with_memory_space_constraint(array, pltpu.HBM) for array in (early, late)

time: 328 us -> 327 us (level)
  no operation moved by 1% of the time
where the time goes in v7:
time: 327 us; the launch traced here: 326 us
  blocking collectives  245 us (75%)
  starting transfers between devices  27.4 us (8%)
  waiting for transfers between devices  23.6 us (7%)
  between operations  13.5 us (4%)
  Pallas kernels  10.8 us (3%)
  local copies, waits for them, and re-layouts  3.34 us (1%)
    all_to_all x15, blocking collectives, exchanged(): return lax.all_to_all(blocks, axis, split_axis=0, concat_axis=0, tiled=True)  245 us
    ppermute x2, starting transfers between devices, swapped(): return lax.ppermute(block, axis, [(0, 1), (1, 0)])  13.8 us
    all_to_all x1, starting transfers between devices, exchanged(): return lax.all_to_all(blocks, axis, split_axis=0, concat_axis=0, tiled=True)  13.5 us
    pallas_call x17, Pallas kernels, local_call(): return call(*inputs)  10.8 us
    all_to_all x1, waiting for transfers between devices, exchanged(): return lax.all_to_all(blocks, axis, split_axis=0, concat_axis=0, tiled=True)  10.2 us
    ppermute x2, waiting for transfers between devices, swapped(): return lax.ppermute(block, axis, [(0, 1), (1, 0)])  6.86 us
  transfers between devices with their start and end apart: 5, of which 4 were waited for; matrix products, arithmetic and copies ran while one was open for 1% of the time, Pallas kernels for 1%

profile of v7, /device:TPU:8, one launch (start us, length us, event | category | flops | bytes accessed | tf_op | source)
XLA Modules:
  0.0 325.9 jit_solution(634408481552280258)
XLA Ops:
  6.5 0.0 all-gather.3.cloned.1.call-start
  6.5 0.9 slice.6
  7.5 6.8 %collective-permute-start = (bf16[3,256,128]{2,1,0:T(8,128)(2,1)S(1)}, bf16[3,256,128]{2,1,0:T(8,128)(2,1)S(1)}, u32[]{:S(2)}, u32[]{:S(2)}) collective-permute-start(bf16[3,256,128]{2,1,0:T(8,128)(2,1)S(1)} %slice.6), channel_id=1, source_target_pairs={{0,64},{64,0},{1,65},{65,1},{2,66},{66,2},{3,67},{67,3},{4,68},{68... | collective-permute-start | bytes 589832 | tf_op jit(solution)/shard_map/ppermute | solution.py:29
  14.3 1.0 slice.7
  15.3 0.7 constant_dynamic-slice_fusion
  16.0 6.6 %collective-permute-done = bf16[3,256,128]{2,1,0:T(8,128)(2,1)S(1)} collective-permute-done((bf16[3,256,128]{2,1,0:T(8,128)(2,1)S(1)}, bf16[3,256,128]{2,1,0:T(8,128)(2,1)S(1)}, u32[]{:S(2)}, u32[]{:S(2)}) %collective-permute-start) | collective-permute-done | bytes 196640 | tf_op jit(solution)/shard_map/ppermute | solution.py:29
  22.6 0.8 pad_maximum_fusion.1
  23.4 0.0 all-gather.3.cloned.1.call-update
  23.4 7.0 %collective-permute-start.1 = (bf16[5,256,128]{2,1,0:T(8,128)(2,1)S(1)}, bf16[5,256,128]{2,1,0:T(8,128)(2,1)S(1)}, u32[]{:S(2)}, u32[]{:S(2)}) collective-permute-start(bf16[5,256,128]{2,1,0:T(8,128)(2,1)S(1)} %slice.7), channel_id=1, source_target_pairs={{0,64},{64,0},{1,65},{65,1},{2,66},{66,2},{3,67},{67,3},{4,68},{68... | collective-permute-start | bytes 983048 | tf_op jit(solution)/shard_map/ppermute | solution.py:29
  30.4 0.7 broadcast_in_dim.2
  31.1 13.5 %all-to-all-start = ((bf16[32,16,128]{2,1,0:T(8,128)(2,1)}), bf16[32,16,128]{2,1,0:T(8,128)(2,1)S(1)}, u32[]{:S(2)}, u32[]{:S(2)}) async-start(bf16[32,16,128]{2,1,0:T(8,128)(2,1)} %broadcast_in_dim.2), calls=%async_computation | async-start | bytes 262144 | tf_op jit(solution)/shard_map/all_to_all | solution.py:25
  44.7 0.0 all-gather.5.cloned.1.call-start
  44.7 0.3 collective-permute-done.1
  45.0 1.0 pad_maximum_fusion
  46.0 10.2 %all-to-all-done.got.refs_0_ = bf16[32,16,128]{2,1,0:T(8,128)(2,1)S(1)} async-done(((bf16[32,16,128]{2,1,0:T(8,128)(2,1)}), bf16[32,16,128]{2,1,0:T(8,128)(2,1)S(1)}, u32[]{:S(2)}, u32[]{:S(2)}) %all-to-all-start) | async-done | bytes 131104 | tf_op jit(solution)/shard_map/all_to_all | solution.py:25
  56.1 0.0 all-gather.5.cloned.1.call-update
  56.2 6.5 %all-gather.3.cloned.1.call-done.matrices = bf16[3,4096,128]{2,1,0:T(8,128)(2,1)} async-done(((bf16[3,512,128]{2,1,0:T(8,128)(2,1)}), bf16[3,4096,128]{2,1,0:T(8,128)(2,1)}) %all-gather.3.cloned.1.call-update) | async-done | bytes 3145744 | tf_op jit(solution)/shard_map/all_gather | solution.py:42
  62.7 0.0 copy-start.1
  62.7 1.8 shard_map.37
  64.5 20.1 %all_to_all.80.got.refs_1_ = bf16[32,16,128]{2,1,0:T(8,128)(2,1)S(1)} all-to-all(bf16[32,16,128]{2,1,0:T(8,128)(2,1)S(1)} %get-tuple-element.61), channel_id=1, replica_groups=mesh['x'=4,'far'=2,'core'=2,'tp'=32] {'tp'}, dimensions={0} | all-to-all | bytes 262144 | tf_op jit(solution)/shard_map/all_to_all | solution.py:25
  84.6 0.0 copy-done.1
  84.6 0.3 shard_map.38
  84.8 13.9 %all_to_all.81.got.refs_2_ = bf16[32,16,128]{2,1,0:T(8,128)(2,1)S(1)} all-to-all(bf16[32,16,128]{2,1,0:T(8,128)(2,1)S(1)} %get-tuple-element.63), channel_id=1, replica_groups=mesh['x'=4,'far'=2,'core'=2,'tp'=32] {'tp'}, dimensions={0} | all-to-all | bytes 262144 | tf_op jit(solution)/shard_map/all_to_all | solution.py:25
  98.7 1.7 shard_map.39
  100.4 13.5 %all_to_all.82.got.refs_3_ = bf16[32,16,128]{2,1,0:T(8,128)(2,1)S(1)} all-to-all(bf16[32,16,128]{2,1,0:T(8,128)(2,1)S(1)} %get-tuple-element.65), channel_id=1, replica_groups=mesh['x'=4,'far'=2,'core'=2,'tp'=32] {'tp'}, dimensions={0} | all-to-all | bytes 262144 | tf_op jit(solution)/shard_map/all_to_all | solution.py:25
  113.9 0.0 all-gather.5.cloned.1.call-done.matrices
  113.9 0.0 copy-start
  113.9 1.8 shard_map.40
  115.7 13.8 %all_to_all.83.got.refs_4_ = bf16[32,16,128]{2,1,0:T(8,128)(2,1)S(1)} all-to-all(bf16[32,16,128]{2,1,0:T(8,128)(2,1)S(1)} %get-tuple-element.68), channel_id=1, replica_groups=mesh['x'=4,'far'=2,'core'=2,'tp'=32] {'tp'}, dimensions={0} | all-to-all | bytes 262144 | tf_op jit(solution)/shard_map/all_to_all | solution.py:25
  129.5 0.0 copy-done
  129.5 0.3 shard_map.41
  129.8 13.6 %all_to_all.84.got.refs_5_ = bf16[32,16,128]{2,1,0:T(8,128)(2,1)S(1)} all-to-all(bf16[32,16,128]{2,1,0:T(8,128)(2,1)S(1)} %get-tuple-element.70), channel_id=1, replica_groups=mesh['x'=4,'far'=2,'core'=2,'tp'=32] {'tp'}, dimensions={0} | all-to-all | bytes 262144 | tf_op jit(solution)/shard_map/all_to_all | solution.py:25
  143.4 0.3 shard_map.42
  143.7 13.6 %all_to_all.85.got.refs_6_ = bf16[32,16,128]{2,1,0:T(8,128)(2,1)S(1)} all-to-all(bf16[32,16,128]{2,1,0:T(8,128)(2,1)S(1)} %get-tuple-element.72), channel_id=1, replica_groups=mesh['x'=4,'far'=2,'core'=2,'tp'=32] {'tp'}, dimensions={0} | all-to-all | bytes 262144 | tf_op jit(solution)/shard_map/all_to_all | solution.py:25
  157.3 0.3 shard_map.43
  157.5 13.6 %all_to_all.86.got.refs_7_ = bf16[32,16,128]{2,1,0:T(8,128)(2,1)S(1)} all-to-all(bf16[32,16,128]{2,1,0:T(8,128)(2,1)S(1)} %get-tuple-element.74), channel_id=1, replica_groups=mesh['x'=4,'far'=2,'core'=2,'tp'=32] {'tp'}, dimensions={0} | all-to-all | bytes 262144 | tf_op jit(solution)/shard_map/all_to_all | solution.py:25
  171.1 0.3 shard_map.44
  171.4 0.4 shard_map.45
  171.8 13.6 %all_to_all.87.received = bf16[32,16,128]{2,1,0:T(8,128)(2,1)S(1)} all-to-all(bf16[32,16,128]{2,1,0:T(8,128)(2,1)S(1)} %get-tuple-element.79), channel_id=1, replica_groups=mesh['x'=4,'far'=2,'core'=2,'tp'=32] {'tp'}, dimensions={0} | all-to-all | bytes 262144 | tf_op jit(solution)/shard_map/all_to_all | solution.py:25
  185.4 0.4 shard_map.46
  185.8 13.6 %all_to_all.88.received = bf16[32,16,128]{2,1,0:T(8,128)(2,1)S(1)} all-to-all(bf16[32,16,128]{2,1,0:T(8,128)(2,1)S(1)} %get-tuple-element.82), channel_id=1, replica_groups=mesh['x'=4,'far'=2,'core'=2,'tp'=32] {'tp'}, dimensions={0} | all-to-all | bytes 262144 | tf_op jit(solution)/shard_map/all_to_all | solution.py:25
  199.4 0.4 shard_map.47
  199.8 13.6 %all_to_all.89.received = bf16[32,16,128]{2,1,0:T(8,128)(2,1)S(1)} all-to-all(bf16[32,16,128]{2,1,0:T(8,128)(2,1)S(1)} %get-tuple-element.85), channel_id=1, replica_groups=mesh['x'=4,'far'=2,'core'=2,'tp'=32] {'tp'}, dimensions={0} | all-to-all | bytes 262144 | tf_op jit(solution)/shard_map/all_to_all | solution.py:25
  213.4 0.4 shard_map.48
  213.8 13.6 %all_to_all.90.received = bf16[32,16,128]{2,1,0:T(8,128)(2,1)S(1)} all-to-all(bf16[32,16,128]{2,1,0:T(8,128)(2,1)S(1)} %get-tuple-element.88), channel_id=1, replica_groups=mesh['x'=4,'far'=2,'core'=2,'tp'=32] {'tp'}, dimensions={0} | all-to-all | bytes 262144 | tf_op jit(solution)/shard_map/all_to_all | solution.py:25
  227.4 0.0 copy-start.2
  227.4 0.4 shard_map.49
  227.8 13.7 %all_to_all.91.received = bf16[32,16,128]{2,1,0:T(8,128)(2,1)S(1)} all-to-all(bf16[32,16,128]{2,1,0:T(8,128)(2,1)S(1)} %get-tuple-element.91), channel_id=1, replica_groups=mesh['x'=4,'far'=2,'core'=2,'tp'=32] {'tp'}, dimensions={0} | all-to-all | bytes 262144 | tf_op jit(solution)/shard_map/all_to_all | solution.py:25
  241.6 0.0 copy-done.2
  241.6 0.4 shard_map.50
  241.9 13.6 %all_to_all.92.received = bf16[32,16,128]{2,1,0:T(8,128)(2,1)S(1)} all-to-all(bf16[32,16,128]{2,1,0:T(8,128)(2,1)S(1)} %get-tuple-element.94), channel_id=1, replica_groups=mesh['x'=4,'far'=2,'core'=2,'tp'=32] {'tp'}, dimensions={0} | all-to-all | bytes 262144 | tf_op jit(solution)/shard_map/all_to_all | solution.py:25
  255.6 0.4 shard_map.51
  255.9 13.6 %all_to_all.93.received = bf16[32,16,128]{2,1,0:T(8,128)(2,1)S(1)} all-to-all(bf16[32,16,128]{2,1,0:T(8,128)(2,1)S(1)} %get-tuple-element.97), channel_id=1, replica_groups=mesh['x'=4,'far'=2,'core'=2,'tp'=32] {'tp'}, dimensions={0} | all-to-all | bytes 262144 | tf_op jit(solution)/shard_map/all_to_all | solution.py:25
  269.6 0.2 shard_map.52
  269.7 48.0 %all_to_all.94.arrived = bf16[16,384,128]{2,1,0:T(8,128)(2,1)S(1)} all-to-all(bf16[16,384,128]{2,1,0:T(8,128)(2,1)S(1)} %shard_map.52), channel_id=1, replica_groups=mesh['x'=4,'far'=2,'core'=2,'tp'=32] {'x','far','core'}, dimensions={0} | all-to-all | bytes 3145728 | tf_op jit(solution)/shard_map/all_to_all | solution.py:25
  317.7 1.3 shard_map.53
Async XLA Ops:
  6.5 56.2 %all-gather.3.cloned.1.call-start = ((), (), s32[]{:S(2)}) async-start(), calls=%async_computation.16 | async-start | bytes 3538944 | tf_op jit(solution)/shard_map/all_gather | solution.py:42
  7.5 15.2 %collective-permute-start = (bf16[3,256,128]{2,1,0:T(8,128)(2,1)S(1)}, bf16[3,256,128]{2,1,0:T(8,128)(2,1)S(1)}, u32[]{:S(2)}, u32[]{:S(2)}) collective-permute-start(bf16[3,256,128]{2,1,0:T(8,128)(2,1)S(1)} %slice.6), channel_id=1, source_target_pairs={{0,64},{64,0},{1,65},{65,1},{2,66},{66,2},{3,67},{67,3},{4,68},{68... | collective-permute-start | bytes 589832 | tf_op jit(solution)/shard_map/ppermute | solution.py:29
  23.4 21.6 %collective-permute-start.1 = (bf16[5,256,128]{2,1,0:T(8,128)(2,1)S(1)}, bf16[5,256,128]{2,1,0:T(8,128)(2,1)S(1)}, u32[]{:S(2)}, u32[]{:S(2)}) collective-permute-start(bf16[5,256,128]{2,1,0:T(8,128)(2,1)S(1)} %slice.7), channel_id=1, source_target_pairs={{0,64},{64,0},{1,65},{65,1},{2,66},{66,2},{3,67},{67,3},{4,68},{68... | collective-permute-start | bytes 983048 | tf_op jit(solution)/shard_map/ppermute | solution.py:29
  31.1 25.0 %all-to-all-start = ((bf16[32,16,128]{2,1,0:T(8,128)(2,1)}), bf16[32,16,128]{2,1,0:T(8,128)(2,1)S(1)}, u32[]{:S(2)}, u32[]{:S(2)}) async-start(bf16[32,16,128]{2,1,0:T(8,128)(2,1)} %broadcast_in_dim.2), calls=%async_computation | async-start | bytes 262144 | tf_op jit(solution)/shard_map/all_to_all | solution.py:25
  44.7 69.3 %all-gather.5.cloned.1.call-start = ((), (), s32[]{:S(2)}) async-start(), calls=%async_computation.17 | async-start | bytes 5898240 | tf_op jit(solution)/shard_map/all_gather | solution.py:47
  62.7 21.8 %copy-start.1 = (bf16[3,4096,128]{2,1,0:T(8,128)(2,1)S(1)}, bf16[3,4096,128]{2,1,0:T(8,128)(2,1)}, u32[]{:S(2)}) copy-start(bf16[3,4096,128]{2,1,0:T(8,128)(2,1)} %all-gather.3.cloned.1.call-done.matrices) | copy-start | bytes 9437188
  113.9 15.5 %copy-start = (bf16[5,4096,128]{2,1,0:T(8,128)(2,1)S(1)}, bf16[5,4096,128]{2,1,0:T(8,128)(2,1)}, u32[]{:S(2)}) copy-start(bf16[5,4096,128]{2,1,0:T(8,128)(2,1)} %all-gather.5.cloned.1.call-done.matrices) | copy-start | bytes 15728644
  227.4 14.1 %copy-start.2 = (bf16[3,4096,128]{2,1,0:T(8,128)(2,1)S(1)}, bf16[3,4096,128]{2,1,0:T(8,128)(2,1)}, u32[]{:S(2)}) copy-start(bf16[3,4096,128]{2,1,0:T(8,128)(2,1)} %all-gather.3.cloned.1.call-done.matrices) | copy-start | bytes 9437188
Sparse Core Ops, SparseCore 0:
  23.6 39.1 all-gather.2
  64.8 41.9 all-gather.4
